TPU v7x, 128 devices: a whole 4x4x4 slice. The times are simulated.
128 devices in a mesh: tm: 16 (over z, y), seq: 8 (over x, core).
Axes of the slice: x: 4, y: 4, z: 4, core: 2. Of those that a mesh axis runs over, the one named last changes fastest.
Arguments:
- latents: float32 [16, 1536, 3072], P('tm', 'seq'), may hold values from -6 to 6
- timesteps: int32 [17], replicated, may hold values from 1 to 999, as said below
- mod_weight: bfloat16 [256, 9216], replicated, may hold values from -0.375 to 0.375
- qkv_weight: bfloat16 [3, 3072, 3072], P(None, None, 'seq'), may hold values from -0.109375 to 0.109375
- qk_gain: float32 [2, 128], replicated, may hold values from 1 to 3
- out_weight: bfloat16 [3072, 3072], P('seq'), may hold values from -0.109375 to 0.109375
- block_list: int32 [24, 4, 3], P('seq'), may hold values from 0 to 3, as said below
Outputs:
- updated: float32 [16, 1536, 3072], P('tm', 'seq')
Inputs may be any that keep to these rules, and one draw needn't show every extreme that they name: `timesteps`: strictly falling, first entry 999, last entry 1. `block_list`: each row names 3 different key tiles, the first being the query tile itself.
All inputs are finite; a program needn't handle non-finite values.
Results may differ from a plain program's by a relative error of at most 0.008.
Values may be sent and summed in bfloat16 or wider, within the bound.
No kernel may reach another device: no remote copies, remote signals or barrier semaphores. Data moves between devices by JAX's collectives and lax.ppermute only.
A program may use at most 128 MiB of HBM per device.

v0:
```python
import math

import jax
import jax.numpy as jnp
from jax import lax
from jax.sharding import PartitionSpec as P

BLOCK = 384


eps_norm = 1e-06


def entering(array, axis, combine, identity):
    size, place = (lax.axis_size(axis), lax.axis_index(axis))
    everything = lax.all_gather(array, axis)
    start = jnp.broadcast_to(jnp.asarray(identity, array.dtype), array.shape)

    def hop(k, before):
        reached = k < place
        new = combine(before, everything[k])
        return jnp.where(reached, new, before)

    return lax.fori_loop(0, size, hop, start)


def embed(stamp, freq_dim):
    half = freq_dim // 2
    freqs = jnp.exp(-jnp.log(10000.0) * jnp.arange(half, dtype=jnp.float32) / half)
    angles = stamp.astype(jnp.float32) * freqs
    return jnp.concatenate([jnp.cos(angles), jnp.sin(angles)]).astype(jnp.bfloat16)


def modulate(current, stamp, mod_weight):
    emb = embed(stamp, mod_weight.shape[0])
    mod = jnp.dot(emb[None, :], mod_weight, preferred_element_type=jnp.float32)[0]
    width = current.shape[-1]
    shift = mod[:width]
    scale = mod[width : 2 * width]
    gate = mod[2 * width :]
    mean = jnp.mean(current, axis=-1, keepdims=True)
    centred = current - mean
    var = jnp.mean(centred * centred, axis=-1, keepdims=True)
    normed = centred * lax.rsqrt(var + eps_norm)
    return ((normed * (1.0 + scale) + shift).astype(jnp.bfloat16), gate)


def head_norm(proj, gain, head_dim):
    count = proj.shape[0]
    split = proj.reshape(count, -1, head_dim)
    inverse = lax.rsqrt(jnp.mean(split * split, axis=-1, keepdims=True) + eps_norm)
    return (split * inverse * gain).reshape(count, -1).astype(jnp.bfloat16)


def attend(query, keyset, valset, block_list, head_dim, block):
    tokens = query.shape[0]
    heads = query.shape[1] // head_dim
    nblk = tokens // block

    def arrange(x):
        return x.reshape(nblk, block, heads, head_dim).transpose(2, 0, 1, 3)

    q_heads = arrange(query)
    k_heads = arrange(keyset)
    v_heads = arrange(valset)
    picker = jax.vmap(lambda tiles, idx: tiles[idx])
    k_sel = picker(k_heads, block_list).reshape(heads, nblk, -1, head_dim)
    v_sel = picker(v_heads, block_list).reshape(heads, nblk, -1, head_dim)
    scores = jnp.einsum(
        "hqbd,hqkd->hqbk", q_heads, k_sel, preferred_element_type=jnp.float32
    ) / math.sqrt(head_dim)
    weights = jax.nn.softmax(scores, axis=-1)
    probs = weights.astype(jnp.bfloat16)
    result = jnp.einsum("hqbk,hqkd->hqbd", probs, v_sel, preferred_element_type=jnp.float32).astype(
        jnp.bfloat16
    )
    return result.transpose(1, 2, 0, 3).reshape(tokens, heads * head_dim)


def add_terms(earlier, later):
    return earlier + later


def per_device(latents, timesteps, mod_weight, qkv_weight, qk_gain, out_weight, block_list):
    step = lax.axis_index("tm")
    current = latents[0]
    head_dim = qk_gain.shape[1]
    stamp = lax.dynamic_index_in_dim(timesteps, step, 0, keepdims=False)
    later = lax.dynamic_index_in_dim(timesteps, step + 1, 0, keepdims=False)
    modulated, gate = modulate(current, stamp, mod_weight)
    piece = lax.all_gather(modulated, "seq", axis=0, tiled=True)
    query = jnp.dot(piece, qkv_weight[0], preferred_element_type=jnp.float32)
    keyset = jnp.dot(piece, qkv_weight[1], preferred_element_type=jnp.float32)
    valset = jnp.dot(piece, qkv_weight[2], preferred_element_type=jnp.float32)
    stacked = jnp.stack(
        [
            head_norm(query, qk_gain[0], head_dim),
            head_norm(keyset, qk_gain[1], head_dim),
            valset.astype(jnp.bfloat16),
        ],
        axis=1,
    )
    attended = attend(stacked[:, 0], stacked[:, 1], stacked[:, 2], block_list, head_dim, BLOCK)
    projected = lax.psum_scatter(
        jnp.dot(attended, out_weight, preferred_element_type=jnp.float32).astype(jnp.bfloat16),
        "seq",
        scatter_dimension=0,
        tiled=True,
    ).astype(jnp.float32)
    delta = (later - stamp).astype(jnp.float32) / 1000.0
    term = delta * (gate * projected) + jnp.where(step == 0, current, jnp.float32(0.0))
    earlier = entering(term, "tm", add_terms, jnp.zeros_like(term))
    updated = (earlier + term)[None]
    return updated


def solution(mesh):
    return jax.shard_map(
        per_device,
        mesh=mesh,
        in_specs=(
            P("tm", "seq", None),
            P(),
            P(),
            P(None, None, "seq"),
            P(),
            P("seq", None),
            P("seq", None, None),
        ),
        out_specs=P("tm", "seq", None),
        check_vma=False,
    )
```

profile of v0, /device:TPU:1, one launch (start us, length us, event | category | flops | bytes accessed | tf_op | source)
XLA Modules:
  0.0 504.6 jit_solution(7607073733041581429)
XLA Ops:
  6.5 0.0 copy-start
  6.5 0.0 all-gather.4.cloned.1.call-start
  6.5 1.5 fusion.22
  8.6 0.1 sine_convert_fusion
  8.7 3.1 fusion.23
  11.8 1.9 reduce_sum.45
  13.7 2.2 multiply_reduce_fusion.2
  15.9 0.2 copy-done.1
  16.0 1.5 add_convert_fusion
  17.6 0.0 all-gather.4.cloned.1.call-update
  17.6 0.0 reduce-scatter.2.cloned.1.call-start
  17.6 5.0 slice_bitcast_fusion
  22.7 4.3 copy.12
  27.0 0.0 copy-done.5
  27.0 0.1 reshape.70
  27.1 0.0 copy-start.7
  27.1 4.3 copy.11
  31.4 0.0 copy-done.7
  31.4 0.6 slice_bitcast_fusion.2
  31.9 43.5 %all-gather.4.cloned.1.call-done = bf16[1536,3072]{1,0:T(8,128)(2,1)} async-done(((bf16[192,3072]{1,0:T(8,128)(2,1)}), bf16[1536,3072]{1,0:T(8,128)(2,1)}) %all-gather.4.cloned.1.call-update) | async-done | bytes 9437200 | tf_op jit(solution)/shard_map/all_gather | solution.py:91
  75.5 9.9 %multiply_reduce_fusion = (f32[1536,3]{0,1:T(4,128)S(1)}, f32[1536,3,128]{2,0,1:T(8,128)}) fusion(bf16[3,128,3072]{2,1,0:T(8,128)(2,1)} %bitcast.88, bf16[1536,3072]{1,0:T(8,128)(2,1)} %all-gather.4.cloned.1.call-done), kind=kOutput, calls=%fused_computation.22 | convolution fusion | flops 3625053696 | bytes 14174208 | tf_op jit(solution)/shard_map/dot_general | solution.py:93
  85.4 0.6 add_rsqrt_fusion
  86.0 0.0 copy-done.2
  86.0 0.0 copy-done.8
  86.0 6.7 %multiply_reduce_fusion.1 = (f32[1536,3]{0,1:T(4,128)S(1)}, f32[1536,3,128]{2,0,1:T(8,128)}) fusion(bf16[3,128,3072]{2,1,0:T(8,128)(2,1)S(1)} %bitcast.89, bf16[1536,3072]{1,0:T(8,128)(2,1)S(1)} %copy-done.8), kind=kOutput, calls=%fused_computation.25 | convolution fusion | flops 3625053696 | bytes 14174208 | tf_op jit(solution)/shard_map/dot_general | solution.py:92
  92.7 0.6 add_rsqrt_fusion.1
  93.3 6.8 %convolution_convert_fusion.1 = bf16[1536,384]{1,0:T(8,128)(2,1)S(1)} fusion(bf16[1536,3072]{1,0:T(8,128)(2,1)S(1)} %copy-done.8, bf16[3,3072,384]{2,1,0:T(8,128)(2,1)} %param.12), kind=kOutput, calls=%fused_computation.14 | convolution fusion | flops 3624468480 | bytes 12976128 | tf_op jit(solution)/shard_map/dot_general | solution.py:94
  100.1 1.8 reshape.93
  102.0 1.8 copy.20
  103.8 0.3 copy-done.3
  104.1 0.0 copy-done.4
  104.1 1.6 multiply_convert_fusion
  105.7 4.4 gather_fusion
  110.1 3.2 gather_fusion.1
  113.3 2.1 multiply_convert_fusion.1
  115.3 8.5 %exponential_reduce_fusion = f32[3,4,384]{2,1,0:T(4,128)} fusion(bf16[3,4,384,128]{3,2,1,0:T(8,128)(2,1)S(1)} %bitcast.91, bf16[3,4,1152,128]{3,2,1,0:T(8,128)(2,1)} %bitcast.85), kind=kOutput, calls=%fused_computation.7 | convolution fusion | flops 1374880896 | bytes 4737024 | tf_op jit(solution)/shard_map/sub | solution.py:72
  123.9 12.6 %fusion.11 = bf16[4,384,3,128]{3,1,0,2:T(8,128)(2,1)} fusion(bf16[3,4,1152,128]{3,2,1,0:T(8,128)(2,1)} %bitcast.87, f32[3,4,384]{2,1,0:T(4,128)} %exponential_reduce_fusion, bf16[3,4,384,128]{3,2,1,0:T(8,128)(2,1)S(1)} %bitcast.92, bf16[3,4,1152,128]{3,2,1,0:T(8,128)(2,1)} %bitcast.86), kind=kOutput, calls=%fused_computation.30 | convolution fusion | flops 2739738112 | bytes 9455616 | tf_op jit(solution)/shard_map/hqbk,hqkd->hqbd/dot_general | solution.py:74
  136.4 2.5 copy.15
  139.0 0.2 copy.18
  139.2 7.9 %convolution_convert_fusion = bf16[1536,3072]{1,0:T(8,128)(2,1)} fusion(bf16[1536,384]{0,1:T(8,128)(2,1)S(1)} %bitcast.90, bf16[384,3072]{1,0:T(8,128)(2,1)S(1)} %copy-done), kind=kOutput, calls=%fused_computation.8 | convolution fusion | flops 3628597248 | bytes 12976128 | tf_op jit(solution)/shard_map/dot_general | solution.py:105
  147.1 0.0 reduce-scatter.2.cloned.1.call-update
  147.1 0.0 all-gather.6.cloned.1.call-start
  148.4 55.5 %reduce-scatter.2.cloned.1.call-done = bf16[192,3072]{1,0:T(8,128)(2,1)} async-done(((bf16[1536,3072]{1,0:T(8,128)(2,1)}), bf16[192,3072]{1,0:T(8,128)(2,1)}) %reduce-scatter.2.cloned.1.call-update) | async-done | bytes 1179664 | tf_op jit(solution)/shard_map/reduce_scatter | solution.py:104
  203.9 3.8 fusion.8
  207.7 0.0 all-gather.6.cloned.1.call-update
  207.7 218.9 %all-gather.6.cloned.1.call-done = f32[3072,3072]{1,0:T(8,128)} async-done(((f32[192,3072]{1,0:T(8,128)}), f32[3072,3072]{1,0:T(8,128)}) %all-gather.6.cloned.1.call-update) | async-done | bytes 37748752 | tf_op jit(solution)/shard_map/all_gather | solution.py:16
  426.7 67.3 %while.14 = (s32[]{:T(128)}, f32[192,3072]{1,0:T(8,128)}, s32[]{:T(128)}, f32[16,192,3072]{2,1,0:T(8,128)}, s32[]{:T(128)}, /*index=5*/s32[]{:T(128)}) while((s32[]{:T(128)}, f32[192,3072]{1,0:T(8,128)}, s32[]{:T(128)}, f32[16,192,3072]{2,1,0:T(8,128)}, s32[]{:T(128)}, /*index=5*/s32[]{:T(128)}) %tuple.49), condition=%wide.region_8.9_spmd.clone, body=%wide.region_7.8_spmd.clone.sunk | while | flops 1769476 | bytes 7077981 | solution.py:24
  426.7 3.5 add_select_fusion.2
  430.2 4.2 add_select_fusion.2
  434.5 4.2 add_select_fusion.2
  438.7 4.2 add_select_fusion.2
  443.0 4.2 add_select_fusion.2
  447.2 4.2 add_select_fusion.2
  451.5 4.2 add_select_fusion.2
  455.7 4.2 add_select_fusion.2
  460.0 4.2 add_select_fusion.2
  464.2 4.2 add_select_fusion.2
  468.5 4.2 add_select_fusion.2
  472.7 4.2 add_select_fusion.2
  477.0 4.2 add_select_fusion.2
  481.2 4.2 add_select_fusion.2
  485.5 4.2 add_select_fusion.2
  489.7 4.2 add_select_fusion.2
  494.0 4.1 add_bitcast_fusion
  (16 shorter events, 0.1 us)
Async XLA Ops:
  6.5 132.6 %copy-start = (bf16[384,3072]{1,0:T(8,128)(2,1)S(1)}, bf16[384,3072]{1,0:T(8,128)(2,1)}, u32[]{:S(2)}) copy-start(bf16[384,3072]{1,0:T(8,128)(2,1)} %param.14) | copy-start | bytes 7077892
  6.5 68.9 %all-gather.4.cloned.1.call-start = ((), (), s32[]{:S(2)}) async-start(), calls=%async_computation.1 | async-start | bytes 10616832 | tf_op jit(solution)/shard_map/all_gather | solution.py:91
  13.7 2.4 copy-start.1
  17.6 186.3 %reduce-scatter.2.cloned.1.call-start = ((), (), s32[]{:S(2)}) async-start(), calls=%async_computation.2 | async-start | bytes 10616832 | tf_op jit(solution)/shard_map/reduce_scatter | solution.py:104
  22.7 4.3 copy-start.5
  27.1 4.3 copy-start.7
  75.5 10.6 %copy-start.2 = (bf16[384,3072]{1,0:T(8,128)(2,1)S(1)}, bf16[384,3072]{1,0:T(8,128)(2,1)}, u32[]{:S(2)}) copy-start(bf16[384,3072]{1,0:T(8,128)(2,1)} %copy.11) | copy-start | bytes 7077892
  75.5 10.6 %copy-start.8 = (bf16[1536,3072]{1,0:T(8,128)(2,1)S(1)}, bf16[1536,3072]{1,0:T(8,128)(2,1)}, u32[]{:S(2)}) copy-start(bf16[1536,3072]{1,0:T(8,128)(2,1)} %all-gather.4.cloned.1.call-done) | copy-start | bytes 28311556
  102.0 2.1 copy-start.3
  102.0 2.1 copy-start.4
  102.0 2.1 copy-start.6
  147.1 279.6 %all-gather.6.cloned.1.call-start = ((), (), s32[]{:S(2)}) async-start(), calls=%async_computation.3 | async-start | bytes 40108032 | tf_op jit(solution)/shard_map/all_gather | solution.py:16
Sparse Core Ops, SparseCore 0:
  17.7 57.7 all-gather.3
  147.2 56.6 reduce-scatter.1
  207.9 218.7 all-gather.5
where the time goes:
time: 505 us
  waiting for transfers between devices  318 us (63%)
  other arithmetic  85.8 us (17%)
  matrix products  55.4 us (11%)
  local copies, waits for them, and re-layouts  30.1 us (6%)
  between operations  15.1 us (3%)
    all_gather x1, waiting for transfers between devices, entering(): everything = lax.all_gather(array, axis)  219 us
    select_n x16, other arithmetic, hop(): return jnp.where(reached, new, before)  67.3 us
    reduce_scatter x1, waiting for transfers between devices, per_device(): lax.psum_scatter(jnp.dot(attended, out_weight, preferred_element_type=jnp...  55.5 us
    all_gather x1, waiting for transfers between devices, per_device(): piece = lax.all_gather(modulated, 'seq', axis=0, tiled=True)  43.5 us
    dot_general x1, matrix products, attend(): jnp.einsum('hqbk,hqkd->hqbd', probs, v_sel, preferred_element_type=jnp.fl...  12.6 us
  transfers between devices with their start and end apart: 3, of which 3 were waited for; matrix products, arithmetic and copies ran while one was open for 3% of the time, Pallas kernels for 0%

commit v1 on v0

v1 whole, which is shorter than its diff:
```python
import functools
import math

import jax
import jax.numpy as jnp
from jax import lax
from jax.experimental import pallas as pl
from jax.experimental.pallas import tpu as pltpu
from jax.sharding import PartitionSpec as P

D = 3072
BLOCK = 384
HEAD = 128
LOCAL_HEADS = 3
WIDTH = LOCAL_HEADS * HEAD
NX = 4
NY = 4
NZ = 4
ROWS = 192
SUB = 48
COLS = D // NY
DEEP = WIDTH // NZ
eps_norm = 1e-06

BF = jnp.bfloat16
F32 = jnp.float32


def embed(stamp, freq_dim):
    half = freq_dim // 2
    freqs = jnp.exp(-jnp.log(10000.0) * jnp.arange(half, dtype=F32) / half)
    angles = stamp.astype(F32) * freqs
    return jnp.concatenate([jnp.cos(angles), jnp.sin(angles)]).astype(BF)


def modulate(current, stamp, mod_weight):
    emb = embed(stamp, mod_weight.shape[0])
    mod = jnp.dot(emb[None, :], mod_weight[:, : 2 * D], preferred_element_type=F32)[0]
    shift = mod[:D]
    scale = mod[D:]
    mean = jnp.mean(current, axis=-1, keepdims=True)
    centred = current - mean
    var = jnp.mean(centred * centred, axis=-1, keepdims=True)
    normed = centred * lax.rsqrt(var + eps_norm)
    return (normed * (1.0 + scale) + shift).astype(BF)


def shift_x(array, by):
    return lax.ppermute(array, "seq", [(i, (i + 2 * by) % 8) for i in range(8)])


def swap_core(array):
    return lax.ppermute(array, "seq", [(i, i ^ 1) for i in range(8)])


def shift_y(array, by):
    pairs = [(z * NY + y, z * NY + (y + by) % NY) for z in range(NZ) for y in range(NY)]
    return lax.ppermute(array, "tm", pairs)


def up_z(array, by):
    pairs = [(z * NY + y, (z + by) * NY + y) for z in range(NZ - by) for y in range(NY)]
    return lax.ppermute(array, "tm", pairs)


def qkv_kernel(parts, *refs):
    ins = refs[:parts]
    gain_ref, w_ref, _, out_ref, rows, sems = refs[parts:]
    kind = pl.program_id(0)

    @pl.when(kind == 0)
    def _():
        copies = []
        at = 0
        for n, part in enumerate(ins):
            size = part.shape[0]
            copies.append(pltpu.make_async_copy(part, rows.at[pl.ds(at, size)], sems.at[n]))
            at += size
        for copy in copies:
            copy.start()
        for copy in copies:
            copy.wait()

    proj = jnp.dot(rows[...], w_ref[0], preferred_element_type=F32)

    @pl.when(kind < 2)
    def _():
        gain = gain_ref[pl.ds(kind, 1), :]
        for h in range(LOCAL_HEADS):
            cols = slice(h * HEAD, (h + 1) * HEAD)
            part = proj[:, cols]
            inverse = lax.rsqrt(jnp.mean(part * part, axis=-1, keepdims=True) + eps_norm)
            out_ref[0, 0, :, cols] = (part * inverse * gain).astype(BF)

    @pl.when(kind == 2)
    def _():
        out_ref[0, 0] = proj.astype(BF)


def qkv_tile(parts, place, gain, weight, held):
    n = len(parts)
    return pl.pallas_call(
        functools.partial(qkv_kernel, n),
        grid=(3,),
        in_specs=[pl.BlockSpec(memory_space=pl.ANY)] * n
        + [
            pl.BlockSpec((2, HEAD), lambda i: (0, 0)),
            pl.BlockSpec((1, D, WIDTH), lambda i: (i, 0, 0)),
            pl.BlockSpec(memory_space=pl.ANY),
        ],
        out_specs=pl.BlockSpec((1, 1, BLOCK, WIDTH), lambda i: (i, place, 0, 0)),
        out_shape=jax.ShapeDtypeStruct((3, NX, BLOCK, WIDTH), BF),
        scratch_shapes=[pltpu.VMEM((BLOCK, D), BF), pltpu.SemaphoreType.DMA((n,))],
        input_output_aliases={n + 2: 0},
        compiler_params=pltpu.CompilerParams(vmem_limit_bytes=32 << 20),
        cost_estimate=pl.CostEstimate(
            flops=2 * BLOCK * D * 3 * WIDTH, bytes_accessed=10_000_000, transcendentals=0
        ),
        name="qkv_tile",
    )(*parts, gain, weight, held)


def attend_kernel(list_ref, q_ref, k_ref, v_ref, out_ref):
    head = pl.program_id(0)
    factor = math.log2(math.e) / math.sqrt(HEAD)
    query = q_ref[0, 0]
    tiles = [list_ref[head * 3 + n] for n in range(3)]
    scores = [
        lax.dot_general(query, k_ref[0, t], (((1,), (1,)), ((), ())), preferred_element_type=F32)
        for t in tiles
    ]
    top = functools.reduce(jnp.maximum, [jnp.max(s, axis=-1, keepdims=True) for s in scores])
    total = jnp.zeros((BLOCK, 2 * HEAD), F32)
    ones = jnp.ones((BLOCK, HEAD), BF)
    for s, t in zip(scores, tiles):
        probs = jnp.exp2((s - top) * factor).astype(BF)
        total += jnp.dot(probs, jnp.concatenate([v_ref[0, t], ones], axis=1), preferred_element_type=F32)
    out_ref[...] = (total[:, :HEAD] / total[:, HEAD:]).astype(BF)


def attend_tile(key_tiles, place, held):
    def tile(kind):
        return pl.BlockSpec((1, NX, BLOCK, HEAD), lambda h, t, kind=kind: (kind, 0, 0, h))

    return pl.pallas_call(
        attend_kernel,
        grid_spec=pltpu.PrefetchScalarGridSpec(
            num_scalar_prefetch=1,
            grid=(LOCAL_HEADS,),
            in_specs=[
                pl.BlockSpec((1, 1, BLOCK, HEAD), lambda h, t: (0, place, 0, h)),
                tile(1),
                tile(2),
            ],
            out_specs=pl.BlockSpec((BLOCK, HEAD), lambda h, t: (0, h)),
        ),
        out_shape=jax.ShapeDtypeStruct((BLOCK, WIDTH), BF),
        compiler_params=pltpu.CompilerParams(vmem_limit_bytes=32 << 20),
        cost_estimate=pl.CostEstimate(
            flops=4 * 3 * BLOCK * 3 * BLOCK * HEAD * 2,
            bytes_accessed=3_000_000,
            transcendentals=3 * BLOCK * 3 * BLOCK,
        ),
        name="attend_tile",
    )(key_tiles, held, held, held)


def out_kernel(a0, a1, a2, a3, own_ref, w_ref, out_ref):
    acc = jnp.zeros((ROWS, COLS), F32)
    for d in range(NX):
        rows = jnp.concatenate([a[d, 0] for a in (a0, a1, a2, a3)], axis=0)
        weight = own_ref[...] if d == 0 else w_ref[:, 0, d - 1].reshape(WIDTH, COLS)
        acc += jnp.dot(rows, weight, preferred_element_type=F32)
    out_ref[...] = acc.astype(out_ref.dtype)


def out_half(pieces, half, own, gathered, dtype):
    piece = pl.BlockSpec((NX, 1, SUB, WIDTH), lambda n: (0, half, 0, 0))
    return pl.pallas_call(
        out_kernel,
        grid=(NY,),
        in_specs=[piece] * 4
        + [
            pl.BlockSpec((WIDTH, COLS), lambda n: (0, n)),
            pl.BlockSpec((NZ, 1, NX - 1, DEEP, COLS), lambda n: (0, n, 0, 0, 0)),
        ],
        out_specs=pl.BlockSpec((ROWS, COLS), lambda n: (0, n)),
        out_shape=jax.ShapeDtypeStruct((ROWS, D), dtype),
        compiler_params=pltpu.CompilerParams(vmem_limit_bytes=32 << 20),
        cost_estimate=pl.CostEstimate(
            flops=2 * ROWS * NX * WIDTH * D, bytes_accessed=12_000_000, transcendentals=0
        ),
        name="out_half",
    )(*pieces, own, gathered)


def row_kernel(order_ref, own_ref, other_ref, gate_ref, part_ref, total_ref, held):
    for d in range(NY):
        term = own_ref[d] + other_ref[d].astype(F32)
        held[order_ref[d]] = gate_ref[pl.ds(d, 1), :] * term
    held[1] = held[0] + held[1]
    held[2] = held[1] + held[2]
    held[3] = held[2] + held[3]
    total_ref[...] = held[3].astype(BF)
    for d in range(NY):
        part_ref[d] = held[order_ref[d]]


def row_prefix(order, own, other, gates):
    cols = D // 4
    return pl.pallas_call(
        row_kernel,
        grid_spec=pltpu.PrefetchScalarGridSpec(
            num_scalar_prefetch=1,
            grid=(4,),
            in_specs=[
                pl.BlockSpec((NY, SUB, cols), lambda n, o: (0, 0, n)),
                pl.BlockSpec((NY, SUB, cols), lambda n, o: (0, 0, n)),
                pl.BlockSpec((NY, cols), lambda n, o: (0, n)),
            ],
            out_specs=[
                pl.BlockSpec((NY, SUB, cols), lambda n, o: (0, 0, n)),
                pl.BlockSpec((SUB, cols), lambda n, o: (0, n)),
            ],
            scratch_shapes=[pltpu.VMEM((NY, SUB, cols), F32)],
        ),
        out_shape=[
            jax.ShapeDtypeStruct((NY, SUB, D), F32),
            jax.ShapeDtypeStruct((SUB, D), BF),
        ],
        compiler_params=pltpu.CompilerParams(vmem_limit_bytes=32 << 20),
        cost_estimate=pl.CostEstimate(flops=8 * ROWS * D, bytes_accessed=6_000_000, transcendentals=0),
        name="row_prefix",
    )(order, own.reshape(NY, SUB, D), other.reshape(NY, SUB, D), gates)


def final_kernel(place_ref, lat_ref, p0, p1, p2, p3, out_ref):
    n = pl.program_id(0)
    for d, piece in enumerate((p0, p1, p2, p3)):

        @pl.when(n == d)
        def _(piece=piece):
            out_ref[0] = lat_ref[0] + piece[...].astype(F32)


def final_sum(place, lat, pieces):
    piece = pl.BlockSpec((SUB, D), lambda n, o: (0, 0))
    block = pl.BlockSpec((1, SUB, D), lambda n, o: (o[n], 0, 0))
    return pl.pallas_call(
        final_kernel,
        grid_spec=pltpu.PrefetchScalarGridSpec(
            num_scalar_prefetch=1,
            grid=(NY,),
            in_specs=[block, piece, piece, piece, piece],
            out_specs=block,
        ),
        out_shape=jax.ShapeDtypeStruct((NY, SUB, D), F32),
        compiler_params=pltpu.CompilerParams(vmem_limit_bytes=32 << 20),
        cost_estimate=pl.CostEstimate(flops=ROWS * D, bytes_accessed=6_000_000, transcendentals=0),
        name="final_sum",
    )(place, lat.reshape(NY, SUB, D), *pieces)


def first_latents(current, step, y):
    half = current.astype(jnp.float16)
    mine = half[:SUB]
    for to in range(1, NY):
        got = lax.ppermute(half[to * SUB : (to + 1) * SUB], "tm", [(0, to)])
        mine = jnp.where(y == to, got, mine)
    part = mine[:, :COLS]
    for to in range(1, NZ):
        got = lax.ppermute(
            mine[:, to * COLS : (to + 1) * COLS], "tm", [(n, to * NY + n) for n in range(NY)]
        )
        part = jnp.where(step // NY == to, got, part)
    whole = lax.all_gather(part, "tm").reshape(NZ, NY, SUB, COLS)
    whole = whole.transpose(1, 2, 0, 3).reshape(ROWS, D).astype(F32)
    return jnp.where(step == 0, current, whole)


def per_device(latents, timesteps, mod_weight, qkv_weight, qk_gain, out_weight, block_list):
    step = lax.axis_index("tm")
    z, y = step // NY, step % NY
    x = lax.axis_index("seq") // 2
    current = latents[0]

    piece = lax.dynamic_slice(out_weight, (z * DEEP, y * COLS), (DEEP, COLS))
    piece = jnp.stack([shift_x(piece, d) for d in range(1, NX)])
    gathered = lax.all_gather(piece, "tm").reshape(NZ, NY, NX - 1, DEEP, COLS)

    stamp = lax.dynamic_index_in_dim(timesteps, step, 0, keepdims=False)
    modulated = modulate(current, stamp, mod_weight)

    twin = swap_core(modulated)
    before = shift_x(modulated, 1)
    after = shift_x(modulated, -1)
    far_top = shift_x(before[: ROWS // 2], 1)
    far_low = shift_x(after[ROWS // 2 :], -1)
    held = jnp.zeros((3, NX, BLOCK, WIDTH), BF)
    held = qkv_tile([modulated, twin], 0, qk_gain, qkv_weight, held)
    held = qkv_tile([after, swap_core(after)], 1, qk_gain, qkv_weight, held)
    held = qkv_tile([before, swap_core(before)], 3, qk_gain, qkv_weight, held)
    held = qkv_tile(
        [far_top, far_low, swap_core(far_top), swap_core(far_low)], 2, qk_gain, qkv_weight, held
    )

    tiles = (block_list - x) % NX
    arrived = [None] * NX
    for d in (2, 1, 3, 0):
        key_tiles = lax.dynamic_index_in_dim(tiles, (x + d) % NX, 1, keepdims=False).reshape(-1)
        attended = attend_tile(key_tiles, d, held)
        arrived[d] = shift_x(attended, d) if d else attended
    rows = jnp.stack(arrived).reshape(NX, 2, NY, SUB, WIDTH)

    pieces = []
    for d in range(NY):
        send = lax.dynamic_index_in_dim(rows, (y + d) % NY, 2, keepdims=False)
        pieces.append(shift_y(send, d) if d else send)

    other = swap_core(out_half(pieces, 1, out_weight, gathered, BF))
    own = out_half(pieces, 0, out_weight, gathered, F32)

    order = (y - jnp.arange(NY, dtype=jnp.int32)) % NY
    stamps = z * NY + order
    row_emb = jax.vmap(lambda s: embed(s, mod_weight.shape[0]))(timesteps[stamps])
    gates = jnp.dot(row_emb, mod_weight[:, 2 * D :], preferred_element_type=F32)
    delta = (timesteps[stamps + 1] - timesteps[stamps]).astype(F32) / 1000.0
    parts, total = row_prefix(order, own, other, gates * delta[:, None])
    base = sum(up_z(total, by).astype(F32) for by in range(1, NZ))

    back = []
    for d in range(NY):
        send = (parts[d] + base).astype(BF)
        back.append(shift_y(send, -d) if d else send)
    place = (y + jnp.arange(NY, dtype=jnp.int32)) % NY
    lat = first_latents(current, step, y)
    return final_sum(place, lat, back).reshape(1, ROWS, D)


def solution(mesh):
    return jax.shard_map(
        per_device,
        mesh=mesh,
        in_specs=(
            P("tm", "seq", None),
            P(),
            P(),
            P(None, None, "seq"),
            P(),
            P("seq", None),
            P("seq", None, None),
        ),
        out_specs=P("tm", "seq", None),
        check_vma=False,
    )
```

time: 505 us -> 240 us (0.48)
  waiting for transfers between devices: 318 us -> 53.8 us
  other arithmetic: 85.8 us -> 10.7 us
  Pallas kernels: 0 us -> 52.7 us
  matrix products: 55.4 us -> 2.86 us
  starting transfers between devices: 0.09 us -> 51.1 us
  blocking collectives: 0 us -> 27.1 us
  local copies, waits for them, and re-layouts: 30.1 us -> 23.8 us
    all_gather x2 -> x1, waiting for transfers between devices: 262 us -> 0.02 us  [per_device(): gathered = lax.all_gather(piece, 'tm').reshape(NZ, NY, NX - 1, DEEP, COLS)]
    select_n x16 -> x7, other arithmetic: 67.3 us -> 2.11 us  [the longest x1 1.15 us: first_latents(): mine = jnp.where(y == to, got, mine)]
    reduce_scatter x1 -> x0, waiting for transfers between devices: 55.5 us -> none  [per_device(): lax.psum_scatter(jnp.dot(attended, out_weight, preferred_element_type=jnp...]
    ppermute x0 -> x31, waiting for transfers between devices: none -> 53.8 us  [the longest x10 31.3 us: shift_x(): return lax.ppermute(array, 'seq', [(i, (i + 2 * by) % 8) for i in range(8)])]
    pallas_call x0 -> x12, Pallas kernels: none -> 52.7 us  [the longest x4 22.9 us: qkv_tile(): pl.pallas_call(functools.partial(qkv_kernel, n), grid=(3,), in_specs=[pl....]
    ppermute x0 -> x31, starting transfers between devices: none -> 51.1 us  [the longest x10 16.3 us: shift_x(): return lax.ppermute(array, 'seq', [(i, (i + 2 * by) % 8) for i in range(8)])]
    dot_general x6 -> x2, matrix products: 46.9 us -> 2.86 us  [the longest x1 2.34 us: per_device(): gates = jnp.dot(row_emb, mod_weight[:, 2 * D:], preferred_element_type=F32)]
    all_gather x0 -> x1, blocking collectives: none -> 27.1 us  [first_latents(): whole = lax.all_gather(part, 'tm').reshape(NZ, NY, SUB, COLS)]
  transfers between devices with their start and end apart: 3 -> 32, of which waited for: 3 -> 9; matrix products, arithmetic and copies ran while one was open for 3% -> 12% of each run, Pallas kernels for 0% -> 21%
where the time goes in v1:
time: 240 us; the launch traced here: 237 us
  waiting for transfers between devices  53.8 us (22%)
  Pallas kernels  52.7 us (22%)
  starting transfers between devices  51.1 us (21%)
  blocking collectives  27.1 us (11%)
  local copies, waits for them, and re-layouts  23.8 us (10%)
  between operations  14.7 us (6%)
  other arithmetic  10.7 us (4%)
  matrix products  2.86 us (1%)
    ppermute x10, waiting for transfers between devices, shift_x(): return lax.ppermute(array, 'seq', [(i, (i + 2 * by) % 8) for i in range(8)])  31.3 us
    all_gather x1, blocking collectives, first_latents(): whole = lax.all_gather(part, 'tm').reshape(NZ, NY, SUB, COLS)  27.1 us
    pallas_call x4, Pallas kernels, qkv_tile(): pl.pallas_call(functools.partial(qkv_kernel, n), grid=(3,), in_specs=[pl....  22.9 us
    ppermute x6, waiting for transfers between devices, shift_y(): return lax.ppermute(array, 'tm', pairs)  22.5 us
    pallas_call x4, Pallas kernels, attend_tile(): pl.pallas_call(attend_kernel, grid_spec=pltpu.PrefetchScalarGridSpec(num_...  17.7 us
    ppermute x10, starting transfers between devices, shift_x(): return lax.ppermute(array, 'seq', [(i, (i + 2 * by) % 8) for i in range(8)])  16.3 us
    ppermute x3, starting transfers between devices, first_latents(): got = lax.ppermute(half[to * SUB:(to + 1) * SUB], 'tm', [(0, to)])  13.2 us
    pallas_call x2, Pallas kernels, out_half(): pl.pallas_call(out_kernel, grid=(NY,), in_specs=[piece] * 4 + [pl.BlockSp...  7.9 us
  transfers between devices with their start and end apart: 32, of which 9 were waited for; matrix products, arithmetic and copies ran while one was open for 12% of the time, Pallas kernels for 21%

profile of v1, /device:TPU:1, one launch (start us, length us, event | category | flops | bytes accessed | tf_op | source)
XLA Modules:
  0.0 236.8 jit_solution(7981119293244415533)
XLA Ops:
  6.5 0.9 dynamic_slice.42
  7.5 2.1 collective-permute-start.21
  9.6 2.5 %collective-permute-start.22 = (bf16[96,768]{1,0:T(8,128)(2,1)S(1)}, bf16[96,768]{1,0:T(8,128)(2,1)S(1)}, u32[]{:S(2)}, u32[]{:S(2)}) collective-permute-start(bf16[96,768]{1,0:T(8,128)(2,1)S(1)} %dynamic_slice.42), channel_id=1, source_target_pairs={{0,4},{1,5},{2,6},{3,7},{4,0},{5,1},{6,2},{7,3},{8,12},{9,13},{10,... | collective-permute-start | bytes 442376 | tf_op jit(solution)/shard_map/ppermute | solution.py:49
  12.0 1.2 collective-permute-start.23
  13.2 0.8 collective-permute-done.21
  14.0 4.5 %collective-permute-done.22 = bf16[96,768]{1,0:T(8,128)(2,1)S(1)} collective-permute-done((bf16[96,768]{1,0:T(8,128)(2,1)S(1)}, bf16[96,768]{1,0:T(8,128)(2,1)S(1)}, u32[]{:S(2)}, u32[]{:S(2)}) %collective-permute-start.22) | collective-permute-done | bytes 147488 | tf_op jit(solution)/shard_map/ppermute | solution.py:49
  18.4 0.8 pad_maximum_fusion.1
  19.3 1.3 dynamic_slice.34
  21.3 3.0 %fusion.28 = (f32[192]{0:T(256)S(1)}, f16[192,3072]{1,0:T(8,128)(2,1)}) fusion(f32[1,192,3072]{2,1,0:T(8,128)} %param.7), kind=kLoop, calls=%fused_computation.80 | loop fusion | flops 1179456 | bytes 3539712 | tf_op jit(solution)/shard_map/reduce_sum | solution.py:41
  25.7 2.2 collective-permute-start.8
  27.9 1.6 collective-permute-start.14
  30.4 0.7 reshape.152.list_ref
  31.2 0.7 reshape.153.list_ref
  33.0 2.0 gather_fusion
  35.0 16.8 %collective-permute-done.8.refs_0_ = bf16[192,3072]{1,0:T(8,128)(2,1)S(1)} collective-permute-done((bf16[192,3072]{1,0:T(8,128)(2,1)S(1)}, bf16[192,3072]{1,0:T(8,128)(2,1)S(1)}, u32[]{:S(2)}, u32[]{:S(2)}) %collective-permute-start.8) | collective-permute-done | bytes 1179680 | tf_op jit(solution)/shard_map/ppermute | solution.py:49
  51.8 2.4 collective-permute-start.13
  54.2 1.2 pad_clamp_fusion
  55.4 2.0 gather_fusion.1
  57.4 1.2 convert_element_type.71
  58.7 1.2 collective-permute-start.7
  59.9 2.3 collective-permute-start.9
  62.5 1.0 fusion.29
  63.5 5.5 %collective-permute-start = (f16[48,3072]{1,0:T(8,128)(2,1)}, f16[48,3072]{1,0:T(8,128)(2,1)}, u32[]{:S(2)}, u32[]{:S(2)}) collective-permute-start(f16[48,3072]{1,0:T(8,128)(2,1)} %get-tuple-element.25), channel_id=1, source_target_pairs={{0,24},{1,25},{2,26},{3,27},{4,28},{5,29},{6,30},{7,31}} | collective-permute-start | bytes 884744 | tf_op jit(solution)/shard_map/ppermute | solution.py:268
  69.0 6.9 %collective-permute-done.7.refs_0_ = bf16[96,3072]{1,0:T(8,128)(2,1)S(1)} collective-permute-done((bf16[96,3072]{1,0:T(8,128)(2,1)S(1)}, bf16[96,3072]{1,0:T(8,128)(2,1)S(1)}, u32[]{:S(2)}, u32[]{:S(2)}) %collective-permute-start.7) | collective-permute-done | bytes 589856 | tf_op jit(solution)/shard_map/ppermute | solution.py:49
  76.8 3.1 %copy-done = bf16[3,3072,384]{2,1,0:T(8,128)(2,1)S(1)} copy-done((bf16[3,3072,384]{2,1,0:T(8,128)(2,1)S(1)}, bf16[3,3072,384]{2,1,0:T(8,128)(2,1)}, u32[]{:S(2)}) %copy-start) | copy-done | bytes 7077912
  80.0 6.2 %qkv_tile.4.refs_4_ = bf16[3,4,384,384]{3,2,1,0:T(8,128)(2,1)S(1)} custom-call(bf16[192,3072]{1,0:T(8,128)(2,1)S(1)} %add_convert_fusion.refs_0_, bf16[192,3072]{1,0:T(8,128)(2,1)} %collective-permute-done.14.refs_1_, f32[2,128]{1,0:T(2,128)S(1)} %copy-done.4, bf16[3,3072,384]{2,1,0:T(8,128)(2,1)S(1)} %copy-done, ...), custom_call_target="tpu_custom_call", output_to_operand_aliasing={{}: (4, {})} | custom-call | flops 2717908992 | bytes 10000000 | tf_op jit(solution)/shard_map/qkv_tile/pallas_call | solution.py:102
  86.2 5.7 %collective-permute-start.1 = (f16[48,3072]{1,0:T(8,128)(2,1)}, f16[48,3072]{1,0:T(8,128)(2,1)}, u32[]{:S(2)}, u32[]{:S(2)}) collective-permute-start(f16[48,3072]{1,0:T(8,128)(2,1)} %get-tuple-element.24), channel_id=1, source_target_pairs={{0,16},{1,17},{2,18},{3,19},{4,20},{5,21},{6,22},{7,23}} | collective-permute-start | bytes 884744 | tf_op jit(solution)/shard_map/ppermute | solution.py:268
  91.9 6.2 %qkv_tile.5.refs_4_ = bf16[3,4,384,384]{3,2,1,0:T(8,128)(2,1)S(1)} custom-call(bf16[192,3072]{1,0:T(8,128)(2,1)S(1)} %collective-permute-done.8.refs_0_, bf16[192,3072]{1,0:T(8,128)(2,1)} %collective-permute-done.13.refs_1_, f32[2,128]{1,0:T(2,128)S(1)} %copy-done.4, bf16[3,3072,384]{2,1,0:T(8,128)(2,1)S(1)} %copy-done, ...), custom_call_target="tpu_custom_call", output_to_operand_aliasing={{}: (4, {})} | custom-call | flops 2717908992 | bytes 10000000 | tf_op jit(solution)/shard_map/qkv_tile/pallas_call | solution.py:102
  98.2 5.2 %qkv_tile.6.refs_6_ = bf16[3,4,384,384]{3,2,1,0:T(8,128)(2,1)S(1)} custom-call(bf16[192,3072]{1,0:T(8,128)(2,1)S(1)} %collective-permute-done.6.refs_0_, bf16[192,3072]{1,0:T(8,128)(2,1)S(1)} %collective-permute-done.12.refs_1_, f32[2,128]{1,0:T(2,128)S(1)} %copy-done.4, bf16[3,3072,384]{2,1,0:T(8,128)(2,1)S(1)} %copy-done, ...), custom_call_target="tpu_custom_call", output_to_operand_aliasing={{}: (4, {})} | custom-call | flops 2717908992 | bytes 10000000 | tf_op jit(solution)/shard_map/qkv_tile/pallas_call | solution.py:102
  103.4 5.3 %qkv_tile.7.q_ref.k_ref.v_ref = bf16[3,4,384,384]{3,2,1,0:T(8,128)(2,1)S(1)} custom-call(bf16[96,3072]{1,0:T(8,128)(2,1)S(1)} %collective-permute-done.7.refs_0_, bf16[96,3072]{1,0:T(8,128)(2,1)S(1)} %collective-permute-done.9.refs_1_, bf16[96,3072]{1,0:T(8,128)(2,1)S(1)} %collective-permute-done.10.refs_2_, ...), custom_call_target="tpu_custom_call", output_to_operand_aliasing={{}: (6, {})} | custom-call | flops 2717908992 | bytes 10000000 | tf_op jit(solution)/shard_map/qkv_tile/pallas_call | solution.py:102
  108.7 4.4 %attend_tile.5 = bf16[384,384]{1,0:T(8,128)(2,1)S(1)} custom-call(s32[9]{0:T(128)S(1)} %reshape.151.list_ref, bf16[3,4,384,384]{3,2,1,0:T(8,128)(2,1)S(1)} %qkv_tile.7.q_ref.k_ref.v_ref, bf16[3,4,384,384]{3,2,1,0:T(8,128)(2,1)S(1)} %qkv_tile.7.q_ref.k_ref.v_ref, bf16[3,4,384,384]{3,2,1,0:T(8,128)(2,1)S(1)} %qkv_tile.7.q_ref.k_ref.v_ref), custom_call_target="tpu_custom_call" | custom-call | flops 1358954496 | bytes 3000000 | tf_op jit(solution)/shard_map/attend_tile/pallas_call | solution.py:145
  113.1 1.0 collective-permute-start.15
  114.1 4.4 %attend_tile.6 = bf16[384,384]{1,0:T(8,128)(2,1)S(1)} custom-call(s32[9]{0:T(128)S(1)} %reshape.152.list_ref, bf16[3,4,384,384]{3,2,1,0:T(8,128)(2,1)S(1)} %qkv_tile.7.q_ref.k_ref.v_ref, bf16[3,4,384,384]{3,2,1,0:T(8,128)(2,1)S(1)} %qkv_tile.7.q_ref.k_ref.v_ref, bf16[3,4,384,384]{3,2,1,0:T(8,128)(2,1)S(1)} %qkv_tile.7.q_ref.k_ref.v_ref), custom_call_target="tpu_custom_call" | custom-call | flops 1358954496 | bytes 3000000 | tf_op jit(solution)/shard_map/attend_tile/pallas_call | solution.py:145
  118.5 3.1 %collective-permute-start.16 = (bf16[384,384]{1,0:T(8,128)(2,1)S(1)}, bf16[384,384]{1,0:T(8,128)(2,1)S(1)}, u32[]{:S(2)}, u32[]{:S(2)}) collective-permute-start(bf16[384,384]{1,0:T(8,128)(2,1)S(1)} %attend_tile.6), channel_id=1, source_target_pairs={{0,4},{1,5},{2,6},{3,7},{4,0},{5,1},{6,2},{7,3},{8,12},{9,13},{10,... | collective-permute-start | bytes 884744 | tf_op jit(solution)/shard_map/ppermute | solution.py:49
  121.6 4.4 %attend_tile.7 = bf16[384,384]{1,0:T(8,128)(2,1)S(1)} custom-call(s32[9]{0:T(128)S(1)} %reshape.153.list_ref, bf16[3,4,384,384]{3,2,1,0:T(8,128)(2,1)S(1)} %qkv_tile.7.q_ref.k_ref.v_ref, bf16[3,4,384,384]{3,2,1,0:T(8,128)(2,1)S(1)} %qkv_tile.7.q_ref.k_ref.v_ref, bf16[3,4,384,384]{3,2,1,0:T(8,128)(2,1)S(1)} %qkv_tile.7.q_ref.k_ref.v_ref), custom_call_target="tpu_custom_call" | custom-call | flops 1358954496 | bytes 3000000 | tf_op jit(solution)/shard_map/attend_tile/pallas_call | solution.py:145
  126.1 0.9 collective-permute-start.17
  127.1 4.4 %attend_tile.4 = bf16[384,384]{1,0:T(8,128)(2,1)S(1)} custom-call(s32[9]{0:T(128)S(1)} %reshape.150.list_ref, bf16[3,4,384,384]{3,2,1,0:T(8,128)(2,1)S(1)} %qkv_tile.7.q_ref.k_ref.v_ref, bf16[3,4,384,384]{3,2,1,0:T(8,128)(2,1)S(1)} %qkv_tile.7.q_ref.k_ref.v_ref, bf16[3,4,384,384]{3,2,1,0:T(8,128)(2,1)S(1)} %qkv_tile.7.q_ref.k_ref.v_ref), custom_call_target="tpu_custom_call" | custom-call | flops 1358954496 | bytes 3000000 | tf_op jit(solution)/shard_map/attend_tile/pallas_call | solution.py:145
  131.5 2.3 collective-permute-done.17
  134.0 1.0 dynamic-slice_bitcast_fusion
  135.2 2.7 %collective-permute-start.20 = (bf16[4,2,48,384]{3,2,1,0:T(8,128)(2,1)}, bf16[4,2,48,384]{3,2,1,0:T(8,128)(2,1)S(1)}, u32[]{:S(2)}, u32[]{:S(2)}) collective-permute-start(bf16[4,2,48,384]{3,2,1,0:T(8,128)(2,1)} %get-tuple-element.19), channel_id=1, source_target_pairs={{0,24},{8,0},{16,8},{24,16},{32,56},{40,32},{48,40},{56,48},{64,88... | collective-permute-start | bytes 884744 | tf_op jit(solution)/shard_map/ppermute | solution.py:58
  137.9 2.3 convolution_multiply_fusion.gate_ref
  140.2 9.4 %collective-permute-done.18.a1 = bf16[4,2,48,384]{3,2,1,0:T(8,128)(2,1)S(1)} collective-permute-done((bf16[4,2,48,384]{3,2,1,0:T(8,128)(2,1)S(1)}, bf16[4,2,48,384]{3,2,1,0:T(8,128)(2,1)S(1)}, u32[]{:S(2)}, u32[]{:S(2)}) %collective-permute-start.18) | collective-permute-done | bytes 294944 | tf_op jit(solution)/shard_map/ppermute | solution.py:58
  149.6 2.0 collective-permute-start.2
  151.7 3.0 %copy-done.1 = bf16[48,96,768]{2,1,0:T(8,128)(2,1)S(1)} copy-done((bf16[48,96,768]{2,1,0:T(8,128)(2,1)S(1)}, bf16[48,96,768]{2,1,0:T(8,128)(2,1)}, u32[]{:S(2)}) %copy-start.1) | copy-done | bytes 7077912
  154.7 3.9 %out_half.3 = bf16[192,3072]{1,0:T(8,128)(2,1)S(1)} custom-call(bf16[4,2,48,384]{3,2,1,0:T(8,128)(2,1)S(1)} %get-tuple-element.22.a0, bf16[4,2,48,384]{3,2,1,0:T(8,128)(2,1)S(1)} %collective-permute-done.18.a1, bf16[4,2,48,384]{3,2,1,0:T(8,128)(2,1)S(1)} %collective-permute-done.19.a2, bf16[4,2,48,384]{3,2,1,0:T(8,128)(2,1)S(1)} %collective-permute-done.20.a3, ...), custom_call_target="tpu_custom_call" | custom-call | flops 1811939328 | bytes 12000000 | tf_op jit(solution)/shard_map/out_half/pallas_call | solution.py:179
  158.6 2.5 %collective-permute-start.24 = (bf16[192,3072]{1,0:T(8,128)(2,1)S(1)}, bf16[192,3072]{1,0:T(8,128)(2,1)S(1)}, u32[]{:S(2)}, u32[]{:S(2)}) collective-permute-start(bf16[192,3072]{1,0:T(8,128)(2,1)S(1)} %out_half.3), channel_id=1, source_target_pairs={{0,1},{1,0},{2,3},{3,2},{4,5},{5,4},{6,7},{7,6},{8,9},{9,8},{10,11... | collective-permute-start | bytes 3538952 | tf_op jit(solution)/shard_map/ppermute | solution.py:53
  161.1 1.2 fusion.8
  162.3 1.3 collective-permute-start.3
  163.6 1.3 collective-permute-start.4
  164.9 1.6 collective-permute-start.5
  166.6 4.0 %out_half.2 = f32[192,3072]{1,0:T(8,128)S(1)} custom-call(bf16[4,2,48,384]{3,2,1,0:T(8,128)(2,1)S(1)} %get-tuple-element.22.a0, bf16[4,2,48,384]{3,2,1,0:T(8,128)(2,1)S(1)} %collective-permute-done.18.a1, bf16[4,2,48,384]{3,2,1,0:T(8,128)(2,1)S(1)} %collective-permute-done.19.a2, bf16[4,2,48,384]{3,2,1,0:T(8,128)(2,1)S(1)} %collective-permute-done.20.a3, ...), custom_call_target="tpu_custom_call" | custom-call | flops 1811939328 | bytes 12000000 | tf_op jit(solution)/shard_map/out_half/pallas_call | solution.py:179
  170.6 1.6 row_prefix.1
  172.3 1.3 collective-permute-start.25
  173.6 1.4 collective-permute-start.26
  174.9 1.3 collective-permute-start.27
  176.3 27.1 %all-gather.6 = f16[768,768]{1,0:T(8,128)(2,1)S(1)} all-gather(f16[48,768]{1,0:T(8,128)(2,1)S(1)} %fusion.10), channel_id=2, replica_groups=mesh['tm'=16,'seq'=8] {'tm'}, dimensions={0}, use_global_device_ids=true | all-gather | bytes 1253376 | tf_op jit(solution)/shard_map/all_gather | solution.py:276
  203.7 2.9 %copy.33 = f32[4,4,48,768]{3,0,2,1:T(4,128)} copy(f32[4,4,48,768]{3,2,1,0:T(8,128)S(1)} %convert.19) | data formatting | bytes 4718592 | tf_op jit(solution)/shard_map/convert_element_type | solution.py:277
  206.6 3.8 %reshape.158 = f32[4,48,3072]{2,1,0:T(8,128)} reshape(f32[4,48,4,768]{3,2,1,0:T(4,128)} %bitcast.69) | data formatting | bytes 4718592 | tf_op jit(solution)/shard_map/convert_element_type | solution.py:277
  210.7 2.0 collective-permute-start.28
  212.7 0.8 collective-permute-start.29
  214.3 4.9 %collective-permute-done.28.p1 = bf16[48,3072]{1,0:T(8,128)(2,1)S(1)} collective-permute-done((bf16[48,3072]{1,0:T(8,128)(2,1)S(1)}, bf16[48,3072]{1,0:T(8,128)(2,1)S(1)}, u32[]{:S(2)}, u32[]{:S(2)}) %collective-permute-start.28) | collective-permute-done | bytes 294944 | tf_op jit(solution)/shard_map/ppermute | solution.py:58
  219.2 0.6 collective-permute-done.29.p2
  219.9 7.6 %collective-permute-done.30.p3 = bf16[48,3072]{1,0:T(8,128)(2,1)S(1)} collective-permute-done((bf16[48,3072]{1,0:T(8,128)(2,1)S(1)}, bf16[48,3072]{1,0:T(8,128)(2,1)S(1)}, u32[]{:S(2)}, u32[]{:S(2)}) %collective-permute-start.30) | collective-permute-done | bytes 294944 | tf_op jit(solution)/shard_map/ppermute | solution.py:58
  227.4 2.5 %final_sum.1 = f32[4,48,3072]{2,1,0:T(8,128)} custom-call(s32[4]{0:T(128)S(1)} %and_select_fusion.2.place_ref, f32[4,48,3072]{2,1,0:T(8,128)S(1)} %broadcast_select_fusion.lat_ref, bf16[48,3072]{1,0:T(8,128)(2,1)S(1)} %get-tuple-element.16.p0, bf16[48,3072]{1,0:T(8,128)(2,1)S(1)} %collective-permute-done.28.p1, ...), custom_call_target="tpu_custom_call" | custom-call | flops 589824 | bytes 6000000 | tf_op jit(solution)/shard_map/final_sum/pallas_call | solution.py:249
  (85 shorter events, 6.6 us)
Async XLA Ops:
  6.5 145.1 %all-gather.5.cloned.1.call-start = ((), (), s32[]{:S(2)}) async-start(), calls=%async_computation | async-start | bytes 7520256 | tf_op jit(solution)/shard_map/all_gather | solution.py:289
  7.5 6.5 %collective-permute-start.21 = (bf16[96,768]{1,0:T(8,128)(2,1)S(1)}, bf16[96,768]{1,0:T(8,128)(2,1)S(1)}, u32[]{:S(2)}, u32[]{:S(2)}) collective-permute-start(bf16[96,768]{1,0:T(8,128)(2,1)S(1)} %dynamic_slice.42), channel_id=1, source_target_pairs={{0,2},{1,3},{2,4},{3,5},{4,6},{5,7},{6,0},{7,1},{8,10},{9,11},{10,... | collective-permute-start | bytes 442376 | tf_op jit(solution)/shard_map/ppermute | solution.py:49
  9.6 8.9 %collective-permute-start.22 = (bf16[96,768]{1,0:T(8,128)(2,1)S(1)}, bf16[96,768]{1,0:T(8,128)(2,1)S(1)}, u32[]{:S(2)}, u32[]{:S(2)}) collective-permute-start(bf16[96,768]{1,0:T(8,128)(2,1)S(1)} %dynamic_slice.42), channel_id=1, source_target_pairs={{0,4},{1,5},{2,6},{3,7},{4,0},{5,1},{6,2},{7,3},{8,12},{9,13},{10,... | collective-permute-start | bytes 442376 | tf_op jit(solution)/shard_map/ppermute | solution.py:49
  12.0 6.4 %collective-permute-start.23 = (bf16[96,768]{1,0:T(8,128)(2,1)S(1)}, bf16[96,768]{1,0:T(8,128)(2,1)S(1)}, u32[]{:S(2)}, u32[]{:S(2)}) collective-permute-start(bf16[96,768]{1,0:T(8,128)(2,1)S(1)} %dynamic_slice.42), channel_id=1, source_target_pairs={{0,6},{1,7},{2,0},{3,1},{4,2},{5,3},{6,4},{7,5},{8,14},{9,15},{10,... | collective-permute-start | bytes 442376 | tf_op jit(solution)/shard_map/ppermute | solution.py:49
  18.4 5.9 %copy-start.5 = (f32[1,192,3072]{2,1,0:T(8,128)S(1)}, f32[1,192,3072]{2,1,0:T(8,128)}, u32[]{:S(2)}) copy-start(f32[1,192,3072]{2,1,0:T(8,128)} %param.7) | copy-start | bytes 7077892
  21.3 3.4 %copy-start.7 = (bf16[256,9216]{1,0:T(8,128)(2,1)S(1)}, bf16[256,9216]{1,0:T(8,128)(2,1)}, u32[]{:S(2)}) copy-start(bf16[256,9216]{1,0:T(8,128)(2,1)} %param.9) | copy-start | bytes 14155780
  25.2 4.3 %copy-start.9 = (s32[3,4,3]{2,1,0:T(4,128)S(1)}, s32[3,4,3]{2,1,0:T(4,128)}, u32[]{:S(2)}) copy-start(s32[3,4,3]{2,1,0:T(4,128)} %param.13) | copy-start | bytes 436
  25.7 26.1 %collective-permute-start.8 = (bf16[192,3072]{1,0:T(8,128)(2,1)S(1)}, bf16[192,3072]{1,0:T(8,128)(2,1)S(1)}, u32[]{:S(2)}, u32[]{:S(2)}) collective-permute-start(bf16[192,3072]{1,0:T(8,128)(2,1)S(1)} %add_convert_fusion.refs_0_), channel_id=1, source_target_pairs={{0,6},{1,7},{2,0},{3,1},{4,2},{5,3},{6,4},{7,5},{8,14},{9,15},{10,... | collective-permute-start | bytes 3538952 | tf_op jit(solution)/shard_map/ppermute | solution.py:49
  27.9 30.7 %collective-permute-start.6 = (bf16[192,3072]{1,0:T(8,128)(2,1)S(1)}, bf16[192,3072]{1,0:T(8,128)(2,1)S(1)}, u32[]{:S(2)}, u32[]{:S(2)}) collective-permute-start(bf16[192,3072]{1,0:T(8,128)(2,1)S(1)} %add_convert_fusion.refs_0_), channel_id=1, source_target_pairs={{0,2},{1,3},{2,4},{3,5},{4,6},{5,7},{6,0},{7,1},{8,10},{9,11},{10,... | collective-permute-start | bytes 3538952 | tf_op jit(solution)/shard_map/ppermute | solution.py:49
  27.9 35.6 %collective-permute-start.14 = (bf16[192,3072]{1,0:T(8,128)(2,1)S(1)}, bf16[192,3072]{1,0:T(8,128)(2,1)}, u32[]{:S(2)}, u32[]{:S(2)}) collective-permute-start(bf16[192,3072]{1,0:T(8,128)(2,1)S(1)} %add_convert_fusion.refs_0_), channel_id=1, source_target_pairs={{0,1},{1,0},{2,3},{3,2},{4,5},{5,4},{6,7},{7,6},{8,9},{9,8},{10,11... | collective-permute-start | bytes 3538952 | tf_op jit(solution)/shard_map/ppermute | solution.py:53
  51.8 34.4 %collective-permute-start.13 = (bf16[192,3072]{1,0:T(8,128)(2,1)S(1)}, bf16[192,3072]{1,0:T(8,128)(2,1)}, u32[]{:S(2)}, u32[]{:S(2)}) collective-permute-start(bf16[192,3072]{1,0:T(8,128)(2,1)S(1)} %collective-permute-done.8.refs_0_), channel_id=1, source_target_pairs={{0,1},{1,0},{2,3},{3,2},{4,5},{5,4},{6,7},{7,6},{8,9},{9,8},{10,11... | collective-permute-start | bytes 3538952 | tf_op jit(solution)/shard_map/ppermute | solution.py:53
  58.6 3.9 %copy-start.8 = (f16[192,3072]{1,0:T(8,128)(2,1)S(1)}, f16[192,3072]{1,0:T(8,128)(2,1)}, u32[]{:S(2)}) copy-start(f16[192,3072]{1,0:T(8,128)(2,1)} %get-tuple-element.18) | copy-start | bytes 3538948
  58.7 17.2 %collective-permute-start.7 = (bf16[96,3072]{1,0:T(8,128)(2,1)S(1)}, bf16[96,3072]{1,0:T(8,128)(2,1)S(1)}, u32[]{:S(2)}, u32[]{:S(2)}) collective-permute-start(bf16[96,3072]{1,0:T(8,128)(2,1)S(1)} %slice.87), channel_id=1, source_target_pairs={{0,2},{1,3},{2,4},{3,5},{4,6},{5,7},{6,0},{7,1},{8,10},{9,11},{10,... | collective-permute-start | bytes 1769480 | tf_op jit(solution)/shard_map/ppermute | solution.py:49
  59.9 16.4 %collective-permute-start.9 = (bf16[96,3072]{1,0:T(8,128)(2,1)S(1)}, bf16[96,3072]{1,0:T(8,128)(2,1)S(1)}, u32[]{:S(2)}, u32[]{:S(2)}) collective-permute-start(bf16[96,3072]{1,0:T(8,128)(2,1)S(1)} %slice.88), channel_id=1, source_target_pairs={{0,6},{1,7},{2,0},{3,1},{4,2},{5,3},{6,4},{7,5},{8,14},{9,15},{10,... | collective-permute-start | bytes 1769480 | tf_op jit(solution)/shard_map/ppermute | solution.py:49
  62.2 35.9 %collective-permute-start.12 = (bf16[192,3072]{1,0:T(8,128)(2,1)S(1)}, bf16[192,3072]{1,0:T(8,128)(2,1)S(1)}, u32[]{:S(2)}, u32[]{:S(2)}) collective-permute-start(bf16[192,3072]{1,0:T(8,128)(2,1)S(1)} %collective-permute-done.6.refs_0_), channel_id=1, source_target_pairs={{0,1},{1,0},{2,3},{3,2},{4,5},{5,4},{6,7},{7,6},{8,9},{9,8},{10,11... | collective-permute-start | bytes 3538952 | tf_op jit(solution)/shard_map/ppermute | solution.py:53
  62.5 14.3 %copy-start.4 = (f32[2,128]{1,0:T(2,128)S(1)}, f32[2,128]{1,0:T(2,128)}, u32[]{:S(2)}) copy-start(f32[2,128]{1,0:T(2,128)} %refs_4_.1) | copy-start | bytes 3076
  63.5 97.6 %collective-permute-start = (f16[48,3072]{1,0:T(8,128)(2,1)}, f16[48,3072]{1,0:T(8,128)(2,1)}, u32[]{:S(2)}, u32[]{:S(2)}) collective-permute-start(f16[48,3072]{1,0:T(8,128)(2,1)} %get-tuple-element.25), channel_id=1, source_target_pairs={{0,24},{1,25},{2,26},{3,27},{4,28},{5,29},{6,30},{7,31}} | collective-permute-start | bytes 884744 | tf_op jit(solution)/shard_map/ppermute | solution.py:268
  75.9 27.5 %collective-permute-start.10 = (bf16[96,3072]{1,0:T(8,128)(2,1)S(1)}, bf16[96,3072]{1,0:T(8,128)(2,1)S(1)}, u32[]{:S(2)}, u32[]{:S(2)}) collective-permute-start(bf16[96,3072]{1,0:T(8,128)(2,1)S(1)} %collective-permute-done.7.refs_0_), channel_id=1, source_target_pairs={{0,1},{1,0},{2,3},{3,2},{4,5},{5,4},{6,7},{7,6},{8,9},{9,8},{10,11... | collective-permute-start | bytes 1769480 | tf_op jit(solution)/shard_map/ppermute | solution.py:53
  76.4 27.0 %collective-permute-start.11 = (bf16[96,3072]{1,0:T(8,128)(2,1)S(1)}, bf16[96,3072]{1,0:T(8,128)(2,1)S(1)}, u32[]{:S(2)}, u32[]{:S(2)}) collective-permute-start(bf16[96,3072]{1,0:T(8,128)(2,1)S(1)} %collective-permute-done.9.refs_1_), channel_id=1, source_target_pairs={{0,1},{1,0},{2,3},{3,2},{4,5},{5,4},{6,7},{7,6},{8,9},{9,8},{10,11... | collective-permute-start | bytes 1769480 | tf_op jit(solution)/shard_map/ppermute | solution.py:53
  76.8 3.2 %copy-start = (bf16[3,3072,384]{2,1,0:T(8,128)(2,1)S(1)}, bf16[3,3072,384]{2,1,0:T(8,128)(2,1)}, u32[]{:S(2)}) copy-start(bf16[3,3072,384]{2,1,0:T(8,128)(2,1)} %refs_5_.1) | copy-start | bytes 21233668
  86.2 74.9 %collective-permute-start.1 = (f16[48,3072]{1,0:T(8,128)(2,1)}, f16[48,3072]{1,0:T(8,128)(2,1)}, u32[]{:S(2)}, u32[]{:S(2)}) collective-permute-start(f16[48,3072]{1,0:T(8,128)(2,1)} %get-tuple-element.24), channel_id=1, source_target_pairs={{0,16},{1,17},{2,18},{3,19},{4,20},{5,21},{6,22},{7,23}} | collective-permute-start | bytes 884744 | tf_op jit(solution)/shard_map/ppermute | solution.py:268
  113.1 18.4 %collective-permute-start.15 = (bf16[384,384]{1,0:T(8,128)(2,1)S(1)}, bf16[384,384]{1,0:T(8,128)(2,1)S(1)}, u32[]{:S(2)}, u32[]{:S(2)}) collective-permute-start(bf16[384,384]{1,0:T(8,128)(2,1)S(1)} %attend_tile.5), channel_id=1, source_target_pairs={{0,2},{1,3},{2,4},{3,5},{4,6},{5,7},{6,0},{7,1},{8,10},{9,11},{10,... | collective-permute-start | bytes 884744 | tf_op jit(solution)/shard_map/ppermute | solution.py:49
  118.5 8.4 %copy-start.10 = (f32[4]{0:T(128)S(1)}, f32[4]{0:T(128)}, u32[]{:S(2)}) copy-start(f32[4]{0:T(128)} %convert_element_type.71) | copy-start | bytes 52
  118.5 13.0 %collective-permute-start.16 = (bf16[384,384]{1,0:T(8,128)(2,1)S(1)}, bf16[384,384]{1,0:T(8,128)(2,1)S(1)}, u32[]{:S(2)}, u32[]{:S(2)}) collective-permute-start(bf16[384,384]{1,0:T(8,128)(2,1)S(1)} %attend_tile.6), channel_id=1, source_target_pairs={{0,4},{1,5},{2,6},{3,7},{4,0},{5,1},{6,2},{7,3},{8,12},{9,13},{10,... | collective-permute-start | bytes 884744 | tf_op jit(solution)/shard_map/ppermute | solution.py:49
  126.1 7.8 %collective-permute-start.17 = (bf16[384,384]{1,0:T(8,128)(2,1)S(1)}, bf16[384,384]{1,0:T(8,128)(2,1)S(1)}, u32[]{:S(2)}, u32[]{:S(2)}) collective-permute-start(bf16[384,384]{1,0:T(8,128)(2,1)S(1)} %attend_tile.7), channel_id=1, source_target_pairs={{0,6},{1,7},{2,0},{3,1},{4,2},{5,3},{6,4},{7,5},{8,14},{9,15},{10,... | collective-permute-start | bytes 884744 | tf_op jit(solution)/shard_map/ppermute | solution.py:49
  133.8 1.2 copy-start.11
  133.8 1.2 copy-start.12
  134.0 17.6 %copy-start.2 = (bf16[384,3072]{1,0:T(8,128)(2,1)S(1)}, bf16[384,3072]{1,0:T(8,128)(2,1)}, u32[]{:S(2)}) copy-start(bf16[384,3072]{1,0:T(8,128)(2,1)} %own_ref.3) | copy-start | bytes 7077892
  135.0 14.6 %collective-permute-start.18 = (bf16[4,2,48,384]{3,2,1,0:T(8,128)(2,1)S(1)}, bf16[4,2,48,384]{3,2,1,0:T(8,128)(2,1)S(1)}, u32[]{:S(2)}, u32[]{:S(2)}) collective-permute-start(bf16[4,2,48,384]{3,2,1,0:T(8,128)(2,1)S(1)} %get-tuple-element.21), channel_id=1, source_target_pairs={{0,8},{8,16},{16,24},{24,0},{32,40},{40,48},{48,56},{56,32},{64,72... | collective-permute-start | bytes 884744 | tf_op jit(solution)/shard_map/ppermute | solution.py:58
  135.1 16.6 %collective-permute-start.19 = (bf16[4,2,48,384]{3,2,1,0:T(8,128)(2,1)}, bf16[4,2,48,384]{3,2,1,0:T(8,128)(2,1)S(1)}, u32[]{:S(2)}, u32[]{:S(2)}) collective-permute-start(bf16[4,2,48,384]{3,2,1,0:T(8,128)(2,1)} %get-tuple-element.20), channel_id=1, source_target_pairs={{0,16},{8,24},{16,0},{24,8},{32,48},{40,56},{48,32},{56,40},{64,80... | collective-permute-start | bytes 884744 | tf_op jit(solution)/shard_map/ppermute | solution.py:58
  135.2 16.5 %collective-permute-start.20 = (bf16[4,2,48,384]{3,2,1,0:T(8,128)(2,1)}, bf16[4,2,48,384]{3,2,1,0:T(8,128)(2,1)S(1)}, u32[]{:S(2)}, u32[]{:S(2)}) collective-permute-start(bf16[4,2,48,384]{3,2,1,0:T(8,128)(2,1)} %get-tuple-element.19), channel_id=1, source_target_pairs={{0,24},{8,0},{16,8},{24,16},{32,56},{40,32},{48,40},{56,48},{64,88... | collective-permute-start | bytes 884744 | tf_op jit(solution)/shard_map/ppermute | solution.py:58
  149.6 11.5 %collective-permute-start.2 = (f16[48,3072]{1,0:T(8,128)(2,1)}, f16[48,3072]{1,0:T(8,128)(2,1)}, u32[]{:S(2)}, u32[]{:S(2)}) collective-permute-start(f16[48,3072]{1,0:T(8,128)(2,1)} %get-tuple-element.23), channel_id=1, source_target_pairs={{0,8},{1,9},{2,10},{3,11},{4,12},{5,13},{6,14},{7,15}} | collective-permute-start | bytes 884744 | tf_op jit(solution)/shard_map/ppermute | solution.py:268
  151.7 3.0 %copy-start.1 = (bf16[48,96,768]{2,1,0:T(8,128)(2,1)S(1)}, bf16[48,96,768]{2,1,0:T(8,128)(2,1)}, u32[]{:S(2)}) copy-start(bf16[48,96,768]{2,1,0:T(8,128)(2,1)} %all-gather.5.cloned.1.call-done) | copy-start | bytes 21233668
  158.6 12.0 %collective-permute-start.24 = (bf16[192,3072]{1,0:T(8,128)(2,1)S(1)}, bf16[192,3072]{1,0:T(8,128)(2,1)S(1)}, u32[]{:S(2)}, u32[]{:S(2)}) collective-permute-start(bf16[192,3072]{1,0:T(8,128)(2,1)S(1)} %out_half.3), channel_id=1, source_target_pairs={{0,1},{1,0},{2,3},{3,2},{4,5},{5,4},{6,7},{7,6},{8,9},{9,8},{10,11... | collective-permute-start | bytes 3538952 | tf_op jit(solution)/shard_map/ppermute | solution.py:53
  162.3 12.6 %collective-permute-start.3 = (f16[48,768]{1,0:T(8,128)(2,1)S(1)}, f16[48,768]{1,0:T(8,128)(2,1)S(1)}, u32[]{:S(2)}, u32[]{:S(2)}) collective-permute-start(f16[48,768]{1,0:T(8,128)(2,1)S(1)} %get-tuple-element.28), channel_id=1, source_target_pairs={{0,96},{8,104},{16,112},{24,120},{1,97},{9,105},{17,113},{25,121},... | collective-permute-start | bytes 221192 | tf_op jit(solution)/shard_map/ppermute | solution.py:272
  163.6 12.7 %collective-permute-start.4 = (f16[48,768]{1,0:T(8,128)(2,1)S(1)}, f16[48,768]{1,0:T(8,128)(2,1)S(1)}, u32[]{:S(2)}, u32[]{:S(2)}) collective-permute-start(f16[48,768]{1,0:T(8,128)(2,1)S(1)} %get-tuple-element.27), channel_id=1, source_target_pairs={{0,64},{8,72},{16,80},{24,88},{1,65},{9,73},{17,81},{25,89},{2,66}... | collective-permute-start | bytes 221192 | tf_op jit(solution)/shard_map/ppermute | solution.py:272
  164.9 5.7 %copy-start.3 = (f32[4,3072]{1,0:T(4,128)S(1)}, f32[4,3072]{1,0:T(4,128)}, u32[]{:S(2)}) copy-start(f32[4,3072]{1,0:T(4,128)} %convolution_multiply_fusion.gate_ref) | copy-start | bytes 147460
  164.9 11.4 %collective-permute-start.5 = (f16[48,768]{1,0:T(8,128)(2,1)S(1)}, f16[48,768]{1,0:T(8,128)(2,1)S(1)}, u32[]{:S(2)}, u32[]{:S(2)}) collective-permute-start(f16[48,768]{1,0:T(8,128)(2,1)S(1)} %get-tuple-element.26), channel_id=1, source_target_pairs={{0,32},{8,40},{16,48},{24,56},{1,33},{9,41},{17,49},{25,57},{2,34}... | collective-permute-start | bytes 221192 | tf_op jit(solution)/shard_map/ppermute | solution.py:272
  172.3 38.1 %collective-permute-start.25 = (bf16[48,3072]{1,0:T(8,128)(2,1)S(1)}, bf16[48,3072]{1,0:T(8,128)(2,1)S(1)}, u32[]{:S(2)}, u32[]{:S(2)}) collective-permute-start(bf16[48,3072]{1,0:T(8,128)(2,1)S(1)} %get-tuple-element.8), channel_id=1, source_target_pairs={{0,32},{8,40},{16,48},{24,56},{32,64},{40,72},{48,80},{56,88},{64,... | collective-permute-start | bytes 884744 | tf_op jit(solution)/shard_map/ppermute | solution.py:63
  173.6 36.8 %collective-permute-start.26 = (bf16[48,3072]{1,0:T(8,128)(2,1)S(1)}, bf16[48,3072]{1,0:T(8,128)(2,1)S(1)}, u32[]{:S(2)}, u32[]{:S(2)}) collective-permute-start(bf16[48,3072]{1,0:T(8,128)(2,1)S(1)} %get-tuple-element.8), channel_id=1, source_target_pairs={{0,64},{8,72},{16,80},{24,88},{32,96},{40,104},{48,112},{56,120},{... | collective-permute-start | bytes 884744 | tf_op jit(solution)/shard_map/ppermute | solution.py:63
  174.9 35.5 %collective-permute-start.27 = (bf16[48,3072]{1,0:T(8,128)(2,1)S(1)}, bf16[48,3072]{1,0:T(8,128)(2,1)S(1)}, u32[]{:S(2)}, u32[]{:S(2)}) collective-permute-start(bf16[48,3072]{1,0:T(8,128)(2,1)S(1)} %get-tuple-element.8), channel_id=1, source_target_pairs={{0,96},{8,104},{16,112},{24,120},{1,97},{9,105},{17,113},{25,121},... | collective-permute-start | bytes 884744 | tf_op jit(solution)/shard_map/ppermute | solution.py:63
  210.4 3.6 %copy-start.6 = (f32[1,192,3072]{2,1,0:T(8,128)S(1)}, f32[1,192,3072]{2,1,0:T(8,128)}, u32[]{:S(2)}) copy-start(f32[1,192,3072]{2,1,0:T(8,128)} %param.7) | copy-start | bytes 7077892
  210.7 8.5 %collective-permute-start.28 = (bf16[48,3072]{1,0:T(8,128)(2,1)S(1)}, bf16[48,3072]{1,0:T(8,128)(2,1)S(1)}, u32[]{:S(2)}, u32[]{:S(2)}) collective-permute-start(bf16[48,3072]{1,0:T(8,128)(2,1)S(1)} %get-tuple-element.15), channel_id=1, source_target_pairs={{0,24},{8,0},{16,8},{24,16},{32,56},{40,32},{48,40},{56,48},{64,88... | collective-permute-start | bytes 884744 | tf_op jit(solution)/shard_map/ppermute | solution.py:58
  212.7 7.2 %collective-permute-start.29 = (bf16[48,3072]{1,0:T(8,128)(2,1)S(1)}, bf16[48,3072]{1,0:T(8,128)(2,1)S(1)}, u32[]{:S(2)}, u32[]{:S(2)}) collective-permute-start(bf16[48,3072]{1,0:T(8,128)(2,1)S(1)} %get-tuple-element.14), channel_id=1, source_target_pairs={{0,16},{8,24},{16,0},{24,8},{32,48},{40,56},{48,32},{56,40},{64,80... | collective-permute-start | bytes 884744 | tf_op jit(solution)/shard_map/ppermute | solution.py:58
  213.5 13.9 %collective-permute-start.30 = (bf16[48,3072]{1,0:T(8,128)(2,1)S(1)}, bf16[48,3072]{1,0:T(8,128)(2,1)S(1)}, u32[]{:S(2)}, u32[]{:S(2)}) collective-permute-start(bf16[48,3072]{1,0:T(8,128)(2,1)S(1)} %get-tuple-element.13), channel_id=1, source_target_pairs={{0,8},{8,16},{16,24},{24,0},{32,40},{40,48},{48,56},{56,32},{64,72... | collective-permute-start | bytes 884744 | tf_op jit(solution)/shard_map/ppermute | solution.py:58
Sparse Core Ops, SparseCore 0:
  19.4 70.0 all-gather.4

commit v2 on v0

v2 whole, which is shorter than its diff:
```python
import functools
import math

import jax
import jax.numpy as jnp
from jax import lax
from jax.experimental import pallas as pl
from jax.experimental.pallas import tpu as pltpu
from jax.sharding import PartitionSpec as P

D = 3072
BLOCK = 384
HEAD = 128
LOCAL_HEADS = 3
WIDTH = LOCAL_HEADS * HEAD
NX = 4
NY = 4
NZ = 4
ROWS = 192
SUB = 48
COLS = D // NY
DEEP = WIDTH // NZ
eps_norm = 1e-06

BF = jnp.bfloat16
F32 = jnp.float32
VMEM = pl.BlockSpec(memory_space=pltpu.VMEM)
SMEM = pl.BlockSpec(memory_space=pltpu.SMEM)


def modulate_kernel(stamps_ref, freq_ref, w_hbm, lat_hbm, out_ref, gate_ref, w, lat, held, w_sems, lat_sems):
    step = lax.axis_index("tm")
    row, y = step // NY, step % NY
    lat_copies = [
        pltpu.make_async_copy(lat_hbm.at[0, part], lat.at[part], lat_sems.at[n])
        for n, part in enumerate(pl.ds(n * SUB, SUB) for n in range(4))
    ]
    w_copies = [
        pltpu.make_async_copy(w_hbm.at[:, part], w.at[:, part], w_sems.at[n])
        for n, part in enumerate(pl.ds(n * D, D) for n in range(3))
    ]
    for copy in lat_copies[:1] + w_copies[:2] + lat_copies[1:] + w_copies[2:]:
        copy.start()

    lane = lax.broadcasted_iota(jnp.int32, (8, HEAD), 0)
    stamps = jnp.zeros((8, HEAD), F32)
    for n in range(NY):
        stamps = jnp.where(lane == n, stamps_ref[row * NY + n].astype(F32), stamps)
    angles = stamps * freq_ref[...]
    emb = jnp.concatenate([jnp.cos(angles), jnp.sin(angles)], axis=1).astype(BF)

    def project(n):
        w_copies[n].wait()
        held[:, n * D : (n + 1) * D] = jnp.dot(
            emb, w[:, n * D : (n + 1) * D], preferred_element_type=F32
        )

    project(0)
    project(1)
    shift = held[pl.ds(y, 1), :D]
    scale = held[pl.ds(y, 1), D : 2 * D]
    for n in range(4):
        lat_copies[n].wait()
        part = slice(n * SUB, (n + 1) * SUB)
        current = lat[part, :]
        centred = current - jnp.mean(current, axis=-1, keepdims=True)
        var = jnp.mean(centred * centred, axis=-1, keepdims=True)
        normed = centred * lax.rsqrt(var + eps_norm)
        out_ref[part, :] = (normed * (1.0 + scale) + shift).astype(BF)
    project(2)
    for n in range(NY):
        delta = (stamps_ref[row * NY + n + 1] - stamps_ref[row * NY + n]).astype(F32) / 1000.0
        gate_ref[n : n + 1, :] = held[n : n + 1, 2 * D :] * delta


def modulate(latents, timesteps, mod_weight):
    half = mod_weight.shape[0] // 2
    freqs = jnp.exp(-jnp.log(10000.0) * jnp.arange(half, dtype=F32) / half)
    return pl.pallas_call(
        modulate_kernel,
        in_specs=[
            pl.BlockSpec(memory_space=pltpu.SMEM),
            VMEM,
            pl.BlockSpec(memory_space=pl.ANY),
            pl.BlockSpec(memory_space=pl.ANY),
        ],
        out_specs=[VMEM, VMEM],
        out_shape=[
            jax.ShapeDtypeStruct((ROWS, D), BF),
            jax.ShapeDtypeStruct((NY, D), F32),
        ],
        scratch_shapes=[
            pltpu.VMEM((2 * half, 3 * D), BF),
            pltpu.VMEM((ROWS, D), F32),
            pltpu.VMEM((8, 3 * D), F32),
            pltpu.SemaphoreType.DMA((3,)),
            pltpu.SemaphoreType.DMA((4,)),
        ],
        compiler_params=pltpu.CompilerParams(vmem_limit_bytes=58 << 20),
        cost_estimate=pl.CostEstimate(flops=1, bytes_accessed=1, transcendentals=0),
        name="modulate",
    )(timesteps, freqs[None], mod_weight, latents)


def shift_x(array, by):
    return lax.ppermute(array, "seq", [(i, (i + 2 * by) % 8) for i in range(8)])


def swap_core(array):
    return lax.ppermute(array, "seq", [(i, i ^ 1) for i in range(8)])


def shift_y(array, by):
    pairs = [(z * NY + y, z * NY + (y + by) % NY) for z in range(NZ) for y in range(NY)]
    return lax.ppermute(array, "tm", pairs)


def opposite_x(forward, backward):
    core = lax.axis_index("seq") % 2
    send = jnp.where(core == 0, forward, backward)
    return lax.ppermute(send, "seq", [(i, (i + 2 - 4 * (i % 2)) % 8) for i in range(8)])


def up_z(array, by):
    pairs = [(z * NY + y, (z + by) * NY + y) for z in range(NZ - by) for y in range(NY)]
    return lax.ppermute(array, "tm", pairs)


def qkv_kernel(place, first_ref, second_ref, gain_ref, w_ref, *refs):
    out_ref = refs[-1]
    rows = jnp.concatenate([first_ref[...], second_ref[...]], axis=0)
    blocks = [(kind, h) for kind in range(3) for h in range(LOCAL_HEADS)]
    for n in range(0, len(blocks), 2):
        pair = blocks[n : n + 2]
        weight = [w_ref[kind, :, h * HEAD : (h + 1) * HEAD] for kind, h in pair]
        weight = jnp.concatenate(weight, axis=1) if len(pair) > 1 else weight[0]
        proj = jnp.dot(rows, weight, preferred_element_type=F32)
        for m, (kind, h) in enumerate(pair):
            part = proj[:, m * HEAD : (m + 1) * HEAD]
            if kind < 2:
                inverse = lax.rsqrt(jnp.mean(part * part, axis=-1, keepdims=True) + eps_norm)
                part = part * inverse * gain_ref[kind : kind + 1, :]
            out_ref[place, kind, :, h * HEAD : (h + 1) * HEAD] = part.astype(BF)


def qkv_tile(first, second, place, gain, weight, held):
    earlier = [] if held is None else [held]
    return pl.pallas_call(
        functools.partial(qkv_kernel, place),
        in_specs=[VMEM] * (4 + len(earlier)),
        out_specs=VMEM,
        out_shape=jax.ShapeDtypeStruct((NX, 3, BLOCK, WIDTH), BF),
        input_output_aliases={4: 0} if earlier else {},
        compiler_params=pltpu.CompilerParams(vmem_limit_bytes=12 << 20),
        cost_estimate=pl.CostEstimate(flops=1, bytes_accessed=1, transcendentals=0),
        name="qkv_tile",
    )(first, second, gain, weight, *earlier)


def attend_kernel(place, list_ref, held_ref, out_ref):
    x = lax.axis_index("seq") // 2
    factor = 1.0 / math.sqrt(HEAD)
    ones = jnp.ones((BLOCK, HEAD), BF)
    for h in range(LOCAL_HEADS):
        cols = slice(h * HEAD, (h + 1) * HEAD)
        tiles = [(list_ref[h, (x + place) % NX, n] - x) % NX for n in range(3)]
        query = held_ref[place, 0, :, cols]
        scores = [
            lax.dot_general(
                query, held_ref[t, 1, :, cols], (((1,), (1,)), ((), ())), preferred_element_type=F32
            )
            for t in tiles
        ]
        top = functools.reduce(jnp.maximum, [jnp.max(s, axis=-1, keepdims=True) for s in scores])
        total = jnp.zeros((BLOCK, 2 * HEAD), F32)
        for s, t in zip(scores, tiles):
            probs = jnp.exp((s - top) * factor).astype(BF)
            values = jnp.concatenate([held_ref[t, 2, :, cols], ones], axis=1)
            total += jnp.dot(probs, values, preferred_element_type=F32)
        out_ref[:, cols] = (total[:, :HEAD] / total[:, HEAD:]).astype(BF)


def attend_tile(block_list, place, held):
    return pl.pallas_call(
        functools.partial(attend_kernel, place),
        in_specs=[SMEM, VMEM],
        out_specs=VMEM,
        out_shape=jax.ShapeDtypeStruct((BLOCK, WIDTH), BF),
        compiler_params=pltpu.CompilerParams(vmem_limit_bytes=12 << 20),
        cost_estimate=pl.CostEstimate(flops=1, bytes_accessed=1, transcendentals=0),
        name="attend_tile",
    )(block_list, held)


def out_kernel(half, p0, p1, p2, p3, w_ref, out_ref, rows):
    x = lax.axis_index("seq") // 2

    @pl.when(pl.program_id(0) == 0)
    def _():
        for d in range(NX):
            part = [p[d, half] for p in (p0, p1, p2, p3)]
            rows[:, d * WIDTH : (d + 1) * WIDTH] = jnp.concatenate(part, axis=0)

    weight = [w_ref[z, 0, (x - d) % NX] for d in range(NX) for z in range(NZ)]
    weight = jnp.concatenate(weight, axis=0)
    proj = jnp.dot(rows[...], weight, preferred_element_type=F32)
    out_ref[0] = proj.astype(out_ref.dtype)


def out_half(pieces, half, gathered, dtype):
    piece = pl.BlockSpec((NX, 2, SUB, WIDTH), lambda n: (0, 0, 0, 0))
    return pl.pallas_call(
        functools.partial(out_kernel, half),
        grid=(NY,),
        in_specs=[piece] * 4
        + [pl.BlockSpec((NZ, 1, NX, DEEP, COLS), lambda n: (0, n, 0, 0, 0))],
        out_specs=pl.BlockSpec((1, ROWS, COLS), lambda n: (n, 0, 0)),
        out_shape=jax.ShapeDtypeStruct((NY, ROWS, COLS), dtype),
        scratch_shapes=[pltpu.VMEM((ROWS, NX * WIDTH), BF)],
        compiler_params=pltpu.CompilerParams(vmem_limit_bytes=40 << 20),
        cost_estimate=pl.CostEstimate(flops=1, bytes_accessed=1, transcendentals=0),
        name="out_half",
    )(*pieces, gathered)


def row_kernel(own_ref, other_ref, gate_ref, part_ref, total_ref, held):
    y = lax.axis_index("tm") % NY
    for d in range(NY):
        term = own_ref[0, d] + other_ref[0, d].astype(F32)
        at = (y - d) % NY
        held[at] = gate_ref[pl.ds(at, 1), :] * term
    held[1] = held[0] + held[1]
    held[2] = held[1] + held[2]
    held[3] = held[2] + held[3]
    total_ref[0] = held[3].astype(BF)
    for d in range(NY):
        part_ref[d, 0] = held[(y - d) % NY]


def row_prefix(own, other, gates):
    block = pl.BlockSpec((1, NY, SUB, COLS), lambda n: (n, 0, 0, 0))
    return pl.pallas_call(
        row_kernel,
        grid=(NY,),
        in_specs=[block, block, pl.BlockSpec((NY, COLS), lambda n: (0, n))],
        out_specs=[
            pl.BlockSpec((NY, 1, SUB, COLS), lambda n: (0, n, 0, 0)),
            pl.BlockSpec((1, SUB, COLS), lambda n: (n, 0, 0)),
        ],
        out_shape=[
            jax.ShapeDtypeStruct((NY, NY, SUB, COLS), F32),
            jax.ShapeDtypeStruct((NY, SUB, COLS), BF),
        ],
        scratch_shapes=[pltpu.VMEM((NY, SUB, COLS), F32)],
        compiler_params=pltpu.CompilerParams(vmem_limit_bytes=32 << 20),
        cost_estimate=pl.CostEstimate(flops=1, bytes_accessed=1, transcendentals=0),
        name="row_prefix",
    )(own.reshape(NY, NY, SUB, COLS), other.reshape(NY, NY, SUB, COLS), gates)


def final_kernel(lat_ref, *refs):
    pieces, firsts, out_ref = refs[:4], refs[4:8], refs[8]
    step = lax.axis_index("tm")
    y = step % NY
    for d in range(NY):
        at = (y + d) % NY
        first = jnp.where(step == 0, lat_ref[at], firsts[d][...])
        out_ref[at] = first + pieces[d][0].astype(F32)


def final_sum(latents, pieces, firsts):
    piece = pl.BlockSpec((1, SUB, COLS), lambda n: (n, 0, 0))
    first = pl.BlockSpec((SUB, COLS), lambda n: (0, n))
    block = pl.BlockSpec((NY, SUB, COLS), lambda n: (0, 0, n))
    return pl.pallas_call(
        final_kernel,
        grid=(NY,),
        in_specs=[block] + [piece] * 4 + [first] * 4,
        out_specs=block,
        out_shape=jax.ShapeDtypeStruct((NY, SUB, D), F32),
        compiler_params=pltpu.CompilerParams(vmem_limit_bytes=32 << 20),
        cost_estimate=pl.CostEstimate(flops=1, bytes_accessed=1, transcendentals=0),
        name="final_sum",
    )(latents.reshape(NY, SUB, D), *pieces, *firsts)


def barrier(*arrays):
    return lax.optimization_barrier(arrays)


def per_device(latents, timesteps, mod_weight, qkv_weight, qk_gain, out_weight, block_list):
    step = lax.axis_index("tm")
    z, y = step // NY, step % NY

    piece = lax.dynamic_slice(out_weight, (z * DEEP, y * COLS), (DEEP, COLS))
    groups = [[i * 2 + c for i in range(NZ * NY * NX)] for c in range(2)]
    gathered = lax.all_gather(piece, ("tm", "seq"), axis_index_groups=groups)
    gathered = gathered.reshape(NZ, NY, NX, DEEP, COLS)

    modulated, gates = modulate(latents, timesteps, mod_weight)

    twin = swap_core(modulated)
    before = shift_x(modulated, 1)
    after = shift_x(modulated, -1)

    twin, current = barrier(twin, latents[0])
    half = current.astype(jnp.float16).reshape(NY, SUB, D)
    parts = [lax.ppermute(half[to], "tm", [(0, to)]) for to in range(1, NY)]
    held = qkv_tile(modulated, twin, 0, qk_gain, qkv_weight, None)

    before, after, held, parts, half = barrier(before, after, held, parts, half)
    far = opposite_x(before, after)
    quarter = half[0]
    for to in range(1, NY):
        quarter = jnp.where(y == to, parts[to - 1], quarter)
    parts = [
        lax.ppermute(quarter, "tm", [(n, to * NY + n) for n in range(NY)]) for to in range(1, NZ)
    ]
    held = qkv_tile(after, swap_core(after), 1, qk_gain, qkv_weight, held)
    held = qkv_tile(before, swap_core(before), 3, qk_gain, qkv_weight, held)
    far, held, parts, quarter = barrier(far, held, parts, quarter)
    for to in range(1, NZ):
        quarter = jnp.where(z == to, parts[to - 1], quarter)
    firsts = [shift_y(quarter, -d) if d else quarter for d in range(NY)]
    held = qkv_tile(far, swap_core(far), 2, qk_gain, qkv_weight, held)

    arrived = [None] * NX
    for d in (2, 1, 3, 0):
        attended = attend_tile(block_list, d, held)
        if d == 0:
            attended, firsts = barrier(attended, firsts)
        arrived[d] = shift_x(attended, d) if d else attended
    rows = jnp.stack(arrived).reshape(NX, 2, NY, SUB, WIDTH)

    pieces = []
    for d in range(NY):
        send = lax.dynamic_index_in_dim(rows, (y + d) % NY, 2, keepdims=False)
        pieces.append(shift_y(send, d) if d else send)

    other = swap_core(out_half(pieces, 1, gathered, BF))
    own = out_half(pieces, 0, gathered, F32)
    parts, total = row_prefix(own, other, gates)
    base = sum(up_z(total, by).astype(F32) for by in range(1, NZ))

    back = []
    for d in range(NY):
        send = (parts[d] + base).astype(BF)
        back.append(shift_y(send, -d) if d else send)
    firsts = [part.astype(F32) for part in firsts]
    return final_sum(latents, back, firsts).reshape(1, ROWS, D)


def solution(mesh):
    return jax.shard_map(
        per_device,
        mesh=mesh,
        in_specs=(
            P("tm", "seq", None),
            P(),
            P(),
            P(None, None, "seq"),
            P(),
            P("seq", None),
            P("seq", None, None),
        ),
        out_specs=P("tm", "seq", None),
        check_vma=False,
    )
```

time: 505 us -> 198 us (0.39)
  waiting for transfers between devices: 318 us -> 51.4 us
  other arithmetic: 85.8 us -> 11.9 us
  matrix products: 55.4 us -> 0 us
  starting transfers between devices: 0.09 us -> 51.5 us
  Pallas kernels: 0 us -> 47.8 us
  local copies, waits for them, and re-layouts: 30.1 us -> 21 us
    all_gather x2 -> x1, waiting for transfers between devices: 262 us -> 0.01 us  [per_device(): gathered = lax.all_gather(piece, ('tm', 'seq'), axis_index_groups=groups)]
    select_n x16 -> x3, other arithmetic: 67.3 us -> 5.46 us  [the longest x1 2.43 us: opposite_x(): send = jnp.where(core == 0, forward, backward)]
    reduce_scatter x1 -> x0, waiting for transfers between devices: 55.5 us -> none  [per_device(): lax.psum_scatter(jnp.dot(attended, out_weight, preferred_element_type=jnp...]
    ppermute x0 -> x29, starting transfers between devices: none -> 51.5 us  [the longest x9 12.4 us: shift_y(): return lax.ppermute(array, 'tm', pairs)]
    ppermute x0 -> x29, waiting for transfers between devices: none -> 51.4 us  [the longest x9 22.4 us: shift_y(): return lax.ppermute(array, 'tm', pairs)]
    pallas_call x0 -> x13, Pallas kernels: none -> 47.8 us  [the longest x4 17.7 us: qkv_tile(): pl.pallas_call(functools.partial(qkv_kernel, place), in_specs=[VMEM] * (4...]
    dot_general x6 -> x0, matrix products: 46.9 us -> none  [the longest x1 12.6 us: attend(): jnp.einsum('hqbk,hqkd->hqbd', probs, v_sel, preferred_element_type=jnp.fl...]
    unnamed x19 -> x34, local copies, waits for them, and re-layouts: 0.7 us -> 18.3 us
  transfers between devices with their start and end apart: 3 -> 30, of which waited for: 3 -> 14; matrix products, arithmetic and copies ran while one was open for 3% -> 6% of each run, Pallas kernels for 0% -> 21%
where the time goes in v2:
time: 198 us; the launch traced here: 197 us
  starting transfers between devices  51.5 us (26%)
  waiting for transfers between devices  51.4 us (26%)
  Pallas kernels  47.8 us (24%)
  local copies, waits for them, and re-layouts  21 us (11%)
  between operations  13.7 us (7%)
  other arithmetic  11.9 us (6%)
    ppermute x9, waiting for transfers between devices, shift_y(): return lax.ppermute(array, 'tm', pairs)  22.4 us
    unnamed x34, local copies, waits for them, and re-layouts  18.3 us
    pallas_call x4, Pallas kernels, qkv_tile(): pl.pallas_call(functools.partial(qkv_kernel, place), in_specs=[VMEM] * (4...  17.7 us
    pallas_call x4, Pallas kernels, attend_tile(): pl.pallas_call(functools.partial(attend_kernel, place), in_specs=[SMEM, V...  14.5 us
    ppermute x5, waiting for transfers between devices, shift_x(): return lax.ppermute(array, 'seq', [(i, (i + 2 * by) % 8) for i in range(8)])  12.9 us
    ppermute x9, starting transfers between devices, shift_y(): return lax.ppermute(array, 'tm', pairs)  12.4 us
    ppermute x3, waiting for transfers between devices, up_z(): return lax.ppermute(array, 'tm', pairs)  11.5 us
    ppermute x3, starting transfers between devices, per_device(): parts = [lax.ppermute(half[to], 'tm', [(0, to)]) for to in range(1, NY)]  8.98 us
  transfers between devices with their start and end apart: 30, of which 14 were waited for; matrix products, arithmetic and copies ran while one was open for 6% of the time, Pallas kernels for 21%

profile of v2, /device:TPU:1, one launch (start us, length us, event | category | flops | bytes accessed | tf_op | source)
XLA Modules:
  0.0 197.2 jit_solution(11256502800724582293)
XLA Ops:
  6.5 1.6 dynamic_slice.20
  8.6 5.6 %modulate.1 = (bf16[192,3072]{1,0:T(8,128)(2,1)}, f32[4,3072]{1,0:T(4,128)}) custom-call(s32[17]{0:T(128)} %stamps_ref.1, f32[1,128]{1,0:T(1,128)} %multiply_exponential_fusion.freq_ref, bf16[256,9216]{1,0:T(8,128)(2,1)} %w_hbm.1, f32[1,192,3072]{2,1,0:T(8,128)} %lat_hbm.1), custom_call_target="tpu_custom_call" | custom-call | flops 1 | bytes 1 | tf_op jit(solution)/shard_map/modulate/pallas_call | solution.py:79
  14.3 1.5 collective-permute-start.2
  15.8 1.3 collective-permute-start
  17.1 1.4 collective-permute-start.1
  18.5 1.0 copy-done.7
  19.7 1.0 copy-done.12
  20.7 1.0 fusion.6
  21.7 4.0 %collective-permute-start.3 = (f16[48,3072]{1,0:T(8,128)(2,1)}, f16[48,3072]{1,0:T(8,128)(2,1)}, u32[]{:S(2)}, u32[]{:S(2)}) collective-permute-start(f16[48,3072]{1,0:T(8,128)(2,1)} %get-tuple-element.63), channel_id=1, source_target_pairs={{0,8},{1,9},{2,10},{3,11},{4,12},{5,13},{6,14},{7,15}} | collective-permute-start | bytes 884744 | tf_op jit(solution)/shard_map/ppermute | solution.py:308
  25.7 3.0 %collective-permute-start.4 = (f16[48,3072]{1,0:T(8,128)(2,1)}, f16[48,3072]{1,0:T(8,128)(2,1)}, u32[]{:S(2)}, u32[]{:S(2)}) collective-permute-start(f16[48,3072]{1,0:T(8,128)(2,1)} %get-tuple-element.62), channel_id=1, source_target_pairs={{0,16},{1,17},{2,18},{3,19},{4,20},{5,21},{6,22},{7,23}} | collective-permute-start | bytes 884744 | tf_op jit(solution)/shard_map/ppermute | solution.py:308
  28.7 2.0 %collective-permute-start.5 = (f16[48,3072]{1,0:T(8,128)(2,1)}, f16[48,3072]{1,0:T(8,128)(2,1)}, u32[]{:S(2)}, u32[]{:S(2)}) collective-permute-start(f16[48,3072]{1,0:T(8,128)(2,1)} %get-tuple-element.61), channel_id=1, source_target_pairs={{0,24},{1,25},{2,26},{3,27},{4,28},{5,29},{6,30},{7,31}} | collective-permute-start | bytes 884744 | tf_op jit(solution)/shard_map/ppermute | solution.py:308
  30.7 3.0 %copy-done = bf16[3,3072,384]{2,1,0:T(8,128)(2,1)S(1)} copy-done((bf16[3,3072,384]{2,1,0:T(8,128)(2,1)S(1)}, bf16[3,3072,384]{2,1,0:T(8,128)(2,1)}, u32[]{:S(2)}) %copy-start) | copy-done | bytes 7077912
  33.7 1.3 copy-done.6
  35.0 1.3 copy-done.8
  36.2 3.2 %qkv_tile.4.refs_0_ = bf16[4,3,384,384]{3,2,1,0:T(8,128)(2,1)S(1)} custom-call(bf16[192,3072]{1,0:T(8,128)(2,1)S(1)} %copy-done.6, bf16[192,3072]{1,0:T(8,128)(2,1)S(1)} %copy-done.8, f32[2,128]{1,0:T(2,128)S(1)} %copy-done.11, bf16[3,3072,384]{2,1,0:T(8,128)(2,1)S(1)} %copy-done), custom_call_target="tpu_custom_call" | custom-call | flops 1 | bytes 1 | tf_op jit(solution)/shard_map/qkv_tile/pallas_call | solution.py:148
  39.5 7.0 %collective-permute-done.first_ref = bf16[192,3072]{1,0:T(8,128)(2,1)} collective-permute-done((bf16[192,3072]{1,0:T(8,128)(2,1)}, bf16[192,3072]{1,0:T(8,128)(2,1)}, u32[]{:S(2)}, u32[]{:S(2)}) %collective-permute-start) | collective-permute-done | bytes 1179680 | tf_op jit(solution)/shard_map/ppermute | solution.py:106
  46.4 2.2 %collective-permute-start.8 = (bf16[192,3072]{1,0:T(8,128)(2,1)}, bf16[192,3072]{1,0:T(8,128)(2,1)}, u32[]{:S(2)}, u32[]{:S(2)}) collective-permute-start(bf16[192,3072]{1,0:T(8,128)(2,1)} %collective-permute-done.1.first_ref), channel_id=1, source_target_pairs={{0,1},{1,0},{2,3},{3,2},{4,5},{5,4},{6,7},{7,6},{8,9},{9,8},{10,11... | collective-permute-start | bytes 3538952 | tf_op jit(solution)/shard_map/ppermute | solution.py:110
  48.7 2.4 %broadcast_select_fusion = bf16[192,3072]{1,0:T(8,128)(2,1)} fusion(bf16[192,3072]{1,0:T(8,128)(2,1)} %collective-permute-done.first_ref, bf16[192,3072]{1,0:T(8,128)(2,1)} %collective-permute-done.1.first_ref, pred[]{:T(512)S(6)} %eq.28), kind=kLoop, calls=%fused_computation.1 | loop fusion | flops 589824 | bytes 3538945 | tf_op jit(solution)/shard_map/jit(_where)/select_n | solution.py:120
  51.2 3.4 %collective-permute-start.6 = (bf16[192,3072]{1,0:T(8,128)(2,1)}, bf16[192,3072]{1,0:T(8,128)(2,1)}, u32[]{:S(2)}, u32[]{:S(2)}) collective-permute-start(bf16[192,3072]{1,0:T(8,128)(2,1)} %broadcast_select_fusion), channel_id=1, source_target_pairs={{0,2},{1,7},{2,4},{3,1},{4,6},{5,3},{6,0},{7,5},{8,10},{9,15},{10,... | collective-permute-start | bytes 3538952 | tf_op jit(solution)/shard_map/ppermute | solution.py:121
  54.6 1.1 fusion.5
  55.8 5.7 %collective-permute-start.10 = (f16[48,3072]{1,0:T(8,128)(2,1)S(1)}, f16[48,3072]{1,0:T(8,128)(2,1)S(1)}, u32[]{:S(2)}, u32[]{:S(2)}) collective-permute-start(f16[48,3072]{1,0:T(8,128)(2,1)S(1)} %fusion.5), channel_id=1, source_target_pairs={{0,64},{8,72},{16,80},{24,88},{1,65},{9,73},{17,81},{25,89},{2,66}... | collective-permute-start | bytes 884744 | tf_op jit(solution)/shard_map/ppermute | solution.py:317
  61.4 1.3 collective-permute-start.11
  62.8 1.3 collective-permute-start.9
  64.1 3.1 %copy-done.1 = bf16[3,3072,384]{2,1,0:T(8,128)(2,1)S(1)} copy-done((bf16[3,3072,384]{2,1,0:T(8,128)(2,1)S(1)}, bf16[3,3072,384]{2,1,0:T(8,128)(2,1)}, u32[]{:S(2)}) %copy-start.1) | copy-done | bytes 7077912
  67.2 4.8 %qkv_tile.5.refs_0_ = bf16[4,3,384,384]{3,2,1,0:T(8,128)(2,1)S(1)} custom-call(bf16[192,3072]{1,0:T(8,128)(2,1)} %collective-permute-done.1.first_ref, bf16[192,3072]{1,0:T(8,128)(2,1)} %collective-permute-done.8.second_ref, f32[2,128]{1,0:T(2,128)S(1)} %copy-done.11, bf16[3,3072,384]{2,1,0:T(8,128)(2,1)S(1)} %copy-done.1, ...), custom_call_target="tpu_custom_call", output_to_operand_aliasing={{}: (4, {})} | custom-call | flops 1 | bytes 1 | tf_op jit(solution)/shard_map/qkv_tile/pallas_call | solution.py:148
  72.0 4.9 %qkv_tile.6.refs_0_ = bf16[4,3,384,384]{3,2,1,0:T(8,128)(2,1)S(1)} custom-call(bf16[192,3072]{1,0:T(8,128)(2,1)} %collective-permute-done.first_ref, bf16[192,3072]{1,0:T(8,128)(2,1)} %collective-permute-done.7.second_ref, f32[2,128]{1,0:T(2,128)S(1)} %copy-done.11, bf16[3,3072,384]{2,1,0:T(8,128)(2,1)S(1)} %copy-done.1, ...), custom_call_target="tpu_custom_call", output_to_operand_aliasing={{}: (4, {})} | custom-call | flops 1 | bytes 1 | tf_op jit(solution)/shard_map/qkv_tile/pallas_call | solution.py:148
  77.0 4.6 %collective-permute-done.9 = f16[48,3072]{1,0:T(8,128)(2,1)S(1)} collective-permute-done((f16[48,3072]{1,0:T(8,128)(2,1)S(1)}, f16[48,3072]{1,0:T(8,128)(2,1)S(1)}, u32[]{:S(2)}, u32[]{:S(2)}) %collective-permute-start.9) | collective-permute-done | bytes 294944 | tf_op jit(solution)/shard_map/ppermute | solution.py:317
  82.2 1.9 select_select_fusion
  84.1 3.5 %collective-permute-start.13 = (f16[48,3072]{1,0:T(8,128)(2,1)}, f16[48,3072]{1,0:T(8,128)(2,1)}, u32[]{:S(2)}, u32[]{:S(2)}) collective-permute-start(f16[48,3072]{1,0:T(8,128)(2,1)} %select_select_fusion), channel_id=1, source_target_pairs={{0,24},{8,0},{16,8},{24,16},{32,56},{40,32},{48,40},{56,48},{64,88... | collective-permute-start | bytes 884744 | tf_op jit(solution)/shard_map/ppermute | solution.py:115
  88.4 3.2 %copy-done.2 = bf16[3,3072,384]{2,1,0:T(8,128)(2,1)S(1)} copy-done((bf16[3,3072,384]{2,1,0:T(8,128)(2,1)S(1)}, bf16[3,3072,384]{2,1,0:T(8,128)(2,1)}, u32[]{:S(2)}) %copy-start.2) | copy-done | bytes 7077912
  91.5 4.8 %qkv_tile.7.held_ref = bf16[4,3,384,384]{3,2,1,0:T(8,128)(2,1)S(1)} custom-call(bf16[192,3072]{1,0:T(8,128)(2,1)} %collective-permute-done.6.first_ref, bf16[192,3072]{1,0:T(8,128)(2,1)} %collective-permute-done.12.second_ref, f32[2,128]{1,0:T(2,128)S(1)} %copy-done.11, bf16[3,3072,384]{2,1,0:T(8,128)(2,1)S(1)} %copy-done.2, ...), custom_call_target="tpu_custom_call", output_to_operand_aliasing={{}: (4, {})} | custom-call | flops 1 | bytes 1 | tf_op jit(solution)/shard_map/qkv_tile/pallas_call | solution.py:148
  96.4 3.8 %attend_tile.5 = bf16[384,384]{1,0:T(8,128)(2,1)} custom-call(s32[3,4,3]{2,1,0:T(4,128)S(1)} %copy-done.9, bf16[4,3,384,384]{3,2,1,0:T(8,128)(2,1)S(1)} %qkv_tile.7.held_ref), custom_call_target="tpu_custom_call" | custom-call | flops 1 | bytes 1 | tf_op jit(solution)/shard_map/attend_tile/pallas_call | solution.py:184
  100.2 3.8 %attend_tile.6 = bf16[384,384]{1,0:T(8,128)(2,1)} custom-call(s32[3,4,3]{2,1,0:T(4,128)S(1)} %copy-done.9, bf16[4,3,384,384]{3,2,1,0:T(8,128)(2,1)S(1)} %qkv_tile.7.held_ref), custom_call_target="tpu_custom_call" | custom-call | flops 1 | bytes 1 | tf_op jit(solution)/shard_map/attend_tile/pallas_call | solution.py:184
  104.0 1.0 collective-permute-start.17
  105.1 3.8 %attend_tile.7 = bf16[384,384]{1,0:T(8,128)(2,1)} custom-call(s32[3,4,3]{2,1,0:T(4,128)S(1)} %copy-done.9, bf16[4,3,384,384]{3,2,1,0:T(8,128)(2,1)S(1)} %qkv_tile.7.held_ref), custom_call_target="tpu_custom_call" | custom-call | flops 1 | bytes 1 | tf_op jit(solution)/shard_map/attend_tile/pallas_call | solution.py:184
  108.9 1.8 collective-permute-start.18
  110.7 3.1 %attend_tile.4 = bf16[384,384]{1,0:T(8,128)(2,1)S(1)} custom-call(s32[3,4,3]{2,1,0:T(4,128)S(1)} %copy-done.9, bf16[4,3,384,384]{3,2,1,0:T(8,128)(2,1)S(1)} %qkv_tile.7.held_ref), custom_call_target="tpu_custom_call" | custom-call | flops 1 | bytes 1 | tf_op jit(solution)/shard_map/attend_tile/pallas_call | solution.py:184
  114.0 3.9 %collective-permute-done.17 = bf16[384,384]{1,0:T(8,128)(2,1)} collective-permute-done((bf16[384,384]{1,0:T(8,128)(2,1)}, bf16[384,384]{1,0:T(8,128)(2,1)}, u32[]{:S(2)}, u32[]{:S(2)}) %collective-permute-start.17) | collective-permute-done | bytes 294944 | tf_op jit(solution)/shard_map/ppermute | solution.py:106
  117.9 1.8 collective-permute-done.18
  119.8 1.3 pad_maximum_fusion
  121.2 1.8 collective-permute-start.19
  123.0 1.5 collective-permute-start.20
  124.5 1.3 collective-permute-start.21
  125.8 3.1 %collective-permute-done.19.p1 = bf16[4,2,48,384]{3,2,1,0:T(8,128)(2,1)S(1)} collective-permute-done((bf16[4,2,48,384]{3,2,1,0:T(8,128)(2,1)S(1)}, bf16[4,2,48,384]{3,2,1,0:T(8,128)(2,1)S(1)}, u32[]{:S(2)}, u32[]{:S(2)}) %collective-permute-start.19) | collective-permute-done | bytes 294944 | tf_op jit(solution)/shard_map/ppermute | solution.py:115
  128.9 7.0 %collective-permute-done.20.p2 = bf16[4,2,48,384]{3,2,1,0:T(8,128)(2,1)S(1)} collective-permute-done((bf16[4,2,48,384]{3,2,1,0:T(8,128)(2,1)S(1)}, bf16[4,2,48,384]{3,2,1,0:T(8,128)(2,1)S(1)}, u32[]{:S(2)}, u32[]{:S(2)}) %collective-permute-start.20) | collective-permute-done | bytes 294944 | tf_op jit(solution)/shard_map/ppermute | solution.py:115
  136.8 3.7 %copy-done.3 = bf16[6144,768]{1,0:T(8,128)(2,1)S(1)} copy-done((bf16[6144,768]{1,0:T(8,128)(2,1)S(1)}, bf16[6144,768]{1,0:T(8,128)(2,1)}, u32[]{:S(2)}) %copy-start.3) | copy-done | bytes 9437208
  140.5 3.3 %out_half.3 = bf16[4,192,768]{2,1,0:T(8,128)(2,1)S(1)} custom-call(bf16[4,2,48,384]{3,2,1,0:T(8,128)(2,1)S(1)} %get-tuple-element.60.p0, bf16[4,2,48,384]{3,2,1,0:T(8,128)(2,1)S(1)} %collective-permute-done.19.p1, bf16[4,2,48,384]{3,2,1,0:T(8,128)(2,1)S(1)} %collective-permute-done.20.p2, bf16[4,2,48,384]{3,2,1,0:T(8,128)(2,1)S(1)} %collective-permute-done.21.p3, ...), custom_call_target="tpu_custom_call" | custom-call | flops 1 | bytes 1 | tf_op jit(solution)/shard_map/out_half/pallas_call | solution.py:212
  143.8 2.2 %collective-permute-start.22 = (bf16[4,192,768]{2,1,0:T(8,128)(2,1)S(1)}, bf16[4,192,768]{2,1,0:T(8,128)(2,1)S(1)}, u32[]{:S(2)}, u32[]{:S(2)}) collective-permute-start(bf16[4,192,768]{2,1,0:T(8,128)(2,1)S(1)} %out_half.3), channel_id=1, source_target_pairs={{0,1},{1,0},{2,3},{3,2},{4,5},{5,4},{6,7},{7,6},{8,9},{9,8},{10,11... | collective-permute-start | bytes 3538952 | tf_op jit(solution)/shard_map/ppermute | solution.py:110
  146.0 3.3 %out_half.2 = f32[4,192,768]{2,1,0:T(8,128)S(1)} custom-call(bf16[4,2,48,384]{3,2,1,0:T(8,128)(2,1)S(1)} %get-tuple-element.60.p0, bf16[4,2,48,384]{3,2,1,0:T(8,128)(2,1)S(1)} %collective-permute-done.19.p1, bf16[4,2,48,384]{3,2,1,0:T(8,128)(2,1)S(1)} %collective-permute-done.20.p2, bf16[4,2,48,384]{3,2,1,0:T(8,128)(2,1)S(1)} %collective-permute-done.21.p3, ...), custom_call_target="tpu_custom_call" | custom-call | flops 1 | bytes 1 | tf_op jit(solution)/shard_map/out_half/pallas_call | solution.py:212
  150.2 4.3 %collective-permute-start.23 = (bf16[4,48,768]{2,1,0:T(8,128)(2,1)S(1)}, bf16[4,48,768]{2,1,0:T(8,128)(2,1)S(1)}, u32[]{:S(2)}, u32[]{:S(2)}) collective-permute-start(bf16[4,48,768]{2,1,0:T(8,128)(2,1)S(1)} %get-tuple-element.48), channel_id=1, source_target_pairs={{0,32},{8,40},{16,48},{24,56},{32,64},{40,72},{48,80},{56,88},{64,... | collective-permute-start | bytes 884744 | tf_op jit(solution)/shard_map/ppermute | solution.py:126
  154.5 1.3 collective-permute-start.24
  155.8 1.3 collective-permute-start.25
  157.1 3.7 %collective-permute-done.23 = bf16[4,48,768]{2,1,0:T(8,128)(2,1)S(1)} collective-permute-done((bf16[4,48,768]{2,1,0:T(8,128)(2,1)S(1)}, bf16[4,48,768]{2,1,0:T(8,128)(2,1)S(1)}, u32[]{:S(2)}, u32[]{:S(2)}) %collective-permute-start.23) | collective-permute-done | bytes 294944 | tf_op jit(solution)/shard_map/ppermute | solution.py:126
  160.9 6.3 %collective-permute-done.24 = bf16[4,48,768]{2,1,0:T(8,128)(2,1)S(1)} collective-permute-done((bf16[4,48,768]{2,1,0:T(8,128)(2,1)S(1)}, bf16[4,48,768]{2,1,0:T(8,128)(2,1)S(1)}, u32[]{:S(2)}, u32[]{:S(2)}) %collective-permute-start.24) | collective-permute-done | bytes 294944 | tf_op jit(solution)/shard_map/ppermute | solution.py:126
  167.2 1.4 collective-permute-done.25
  168.9 2.4 %collective-permute-start.26 = (bf16[4,48,768]{2,1,0:T(8,128)(2,1)S(1)}, bf16[4,48,768]{2,1,0:T(8,128)(2,1)S(1)}, u32[]{:S(2)}, u32[]{:S(2)}) collective-permute-start(bf16[4,48,768]{2,1,0:T(8,128)(2,1)S(1)} %get-tuple-element.55), channel_id=1, source_target_pairs={{0,24},{8,0},{16,8},{24,16},{32,56},{40,32},{48,40},{56,48},{64,88... | collective-permute-start | bytes 884744 | tf_op jit(solution)/shard_map/ppermute | solution.py:115
  172.4 1.0 convert_element_type.44.refs_4_
  173.5 1.2 convert_element_type.45.refs_5_
  174.6 1.0 convert_element_type.46.refs_6_
  175.6 1.0 convert_element_type.47.refs_7_
  176.6 1.1 collective-permute-done.26.refs_1_
  177.8 2.8 %collective-permute-done.27.refs_2_ = bf16[4,48,768]{2,1,0:T(8,128)(2,1)S(1)} collective-permute-done((bf16[4,48,768]{2,1,0:T(8,128)(2,1)S(1)}, bf16[4,48,768]{2,1,0:T(8,128)(2,1)S(1)}, u32[]{:S(2)}, u32[]{:S(2)}) %collective-permute-start.27) | collective-permute-done | bytes 294944 | tf_op jit(solution)/shard_map/ppermute | solution.py:115
  180.6 7.4 %collective-permute-done.28.refs_3_ = bf16[4,48,768]{2,1,0:T(8,128)(2,1)S(1)} collective-permute-done((bf16[4,48,768]{2,1,0:T(8,128)(2,1)S(1)}, bf16[4,48,768]{2,1,0:T(8,128)(2,1)S(1)}, u32[]{:S(2)}, u32[]{:S(2)}) %collective-permute-start.28) | collective-permute-done | bytes 294944 | tf_op jit(solution)/shard_map/ppermute | solution.py:115
  188.0 2.4 %final_sum.1 = f32[4,48,3072]{2,1,0:T(8,128)} custom-call(f32[4,48,3072]{2,1,0:T(8,128)S(1)} %bitcast.52, bf16[4,48,768]{2,1,0:T(8,128)(2,1)S(1)} %get-tuple-element.56.refs_0_, bf16[4,48,768]{2,1,0:T(8,128)(2,1)S(1)} %collective-permute-done.26.refs_1_, bf16[4,48,768]{2,1,0:T(8,128)(2,1)S(1)} %collective-permute-done.27.refs_2_, ...), custom_call_target="tpu_custom_call" | custom-call | flops 1 | bytes 1 | tf_op jit(solution)/shard_map/final_sum/pallas_call | solution.py:275
  (58 shorter events, 6.0 us)
Async XLA Ops:
  6.5 130.3 %all-gather.3.cloned.1.call-start = ((), (), s32[]{:S(2)}) async-start(), calls=%async_computation | async-start | bytes 9584640 | tf_op jit(solution)/shard_map/all_gather | solution.py:297
  8.6 10.9 %copy-start.4 = (f32[1,192,3072]{2,1,0:T(8,128)S(1)}, f32[1,192,3072]{2,1,0:T(8,128)}, u32[]{:S(2)}) copy-start(f32[1,192,3072]{2,1,0:T(8,128)} %lat_hbm.1) | copy-start | bytes 7077892
  14.3 4.2 %collective-permute-start.2 = (bf16[192,3072]{1,0:T(8,128)(2,1)}, bf16[192,3072]{1,0:T(8,128)(2,1)S(1)}, u32[]{:S(2)}, u32[]{:S(2)}) collective-permute-start(bf16[192,3072]{1,0:T(8,128)(2,1)} %get-tuple-element.29.first_ref), channel_id=1, source_target_pairs={{0,1},{1,0},{2,3},{3,2},{4,5},{5,4},{6,7},{7,6},{8,9},{9,8},{10,11... | collective-permute-start | bytes 3538952 | tf_op jit(solution)/shard_map/ppermute | solution.py:110
  15.8 30.6 %collective-permute-start = (bf16[192,3072]{1,0:T(8,128)(2,1)}, bf16[192,3072]{1,0:T(8,128)(2,1)}, u32[]{:S(2)}, u32[]{:S(2)}) collective-permute-start(bf16[192,3072]{1,0:T(8,128)(2,1)} %get-tuple-element.29.first_ref), channel_id=1, source_target_pairs={{0,2},{1,3},{2,4},{3,5},{4,6},{5,7},{6,0},{7,1},{8,10},{9,11},{10,... | collective-permute-start | bytes 3538952 | tf_op jit(solution)/shard_map/ppermute | solution.py:106
  17.1 29.3 %collective-permute-start.1 = (bf16[192,3072]{1,0:T(8,128)(2,1)}, bf16[192,3072]{1,0:T(8,128)(2,1)}, u32[]{:S(2)}, u32[]{:S(2)}) collective-permute-start(bf16[192,3072]{1,0:T(8,128)(2,1)} %get-tuple-element.29.first_ref), channel_id=1, source_target_pairs={{0,6},{1,7},{2,0},{3,1},{4,2},{5,3},{6,4},{7,5},{8,14},{9,15},{10,... | collective-permute-start | bytes 3538952 | tf_op jit(solution)/shard_map/ppermute | solution.py:106
  18.5 1.0 copy-start.7
  19.7 1.0 copy-start.12
  20.7 10.0 %copy-start.11 = (f32[2,128]{1,0:T(2,128)S(1)}, f32[2,128]{1,0:T(2,128)}, u32[]{:S(2)}) copy-start(f32[2,128]{1,0:T(2,128)} %gain_ref.7) | copy-start | bytes 3076
  21.7 24.7 %collective-permute-start.3 = (f16[48,3072]{1,0:T(8,128)(2,1)}, f16[48,3072]{1,0:T(8,128)(2,1)}, u32[]{:S(2)}, u32[]{:S(2)}) collective-permute-start(f16[48,3072]{1,0:T(8,128)(2,1)} %get-tuple-element.63), channel_id=1, source_target_pairs={{0,8},{1,9},{2,10},{3,11},{4,12},{5,13},{6,14},{7,15}} | collective-permute-start | bytes 884744 | tf_op jit(solution)/shard_map/ppermute | solution.py:308
  25.7 20.7 %collective-permute-start.4 = (f16[48,3072]{1,0:T(8,128)(2,1)}, f16[48,3072]{1,0:T(8,128)(2,1)}, u32[]{:S(2)}, u32[]{:S(2)}) collective-permute-start(f16[48,3072]{1,0:T(8,128)(2,1)} %get-tuple-element.62), channel_id=1, source_target_pairs={{0,16},{1,17},{2,18},{3,19},{4,20},{5,21},{6,22},{7,23}} | collective-permute-start | bytes 884744 | tf_op jit(solution)/shard_map/ppermute | solution.py:308
  28.7 17.8 %collective-permute-start.5 = (f16[48,3072]{1,0:T(8,128)(2,1)}, f16[48,3072]{1,0:T(8,128)(2,1)}, u32[]{:S(2)}, u32[]{:S(2)}) collective-permute-start(f16[48,3072]{1,0:T(8,128)(2,1)} %get-tuple-element.61), channel_id=1, source_target_pairs={{0,24},{1,25},{2,26},{3,27},{4,28},{5,29},{6,30},{7,31}} | collective-permute-start | bytes 884744 | tf_op jit(solution)/shard_map/ppermute | solution.py:308
  30.7 3.0 %copy-start = (bf16[3,3072,384]{2,1,0:T(8,128)(2,1)S(1)}, bf16[3,3072,384]{2,1,0:T(8,128)(2,1)}, u32[]{:S(2)}) copy-start(bf16[3,3072,384]{2,1,0:T(8,128)(2,1)} %w_ref.7) | copy-start | bytes 21233668
  33.7 1.3 copy-start.6
  35.0 1.3 copy-start.8
  46.4 16.3 %collective-permute-start.8 = (bf16[192,3072]{1,0:T(8,128)(2,1)}, bf16[192,3072]{1,0:T(8,128)(2,1)}, u32[]{:S(2)}, u32[]{:S(2)}) collective-permute-start(bf16[192,3072]{1,0:T(8,128)(2,1)} %collective-permute-done.1.first_ref), channel_id=1, source_target_pairs={{0,1},{1,0},{2,3},{3,2},{4,5},{5,4},{6,7},{7,6},{8,9},{9,8},{10,11... | collective-permute-start | bytes 3538952 | tf_op jit(solution)/shard_map/ppermute | solution.py:110
  48.6 23.4 %collective-permute-start.7 = (bf16[192,3072]{1,0:T(8,128)(2,1)}, bf16[192,3072]{1,0:T(8,128)(2,1)}, u32[]{:S(2)}, u32[]{:S(2)}) collective-permute-start(bf16[192,3072]{1,0:T(8,128)(2,1)} %collective-permute-done.first_ref), channel_id=1, source_target_pairs={{0,1},{1,0},{2,3},{3,2},{4,5},{5,4},{6,7},{7,6},{8,9},{9,8},{10,11... | collective-permute-start | bytes 3538952 | tf_op jit(solution)/shard_map/ppermute | solution.py:110
  51.2 30.4 %collective-permute-start.6 = (bf16[192,3072]{1,0:T(8,128)(2,1)}, bf16[192,3072]{1,0:T(8,128)(2,1)}, u32[]{:S(2)}, u32[]{:S(2)}) collective-permute-start(bf16[192,3072]{1,0:T(8,128)(2,1)} %broadcast_select_fusion), channel_id=1, source_target_pairs={{0,2},{1,7},{2,4},{3,1},{4,6},{5,3},{6,0},{7,5},{8,10},{9,15},{10,... | collective-permute-start | bytes 3538952 | tf_op jit(solution)/shard_map/ppermute | solution.py:121
  55.7 16.3 %copy-start.13 = (f16[48,3072]{1,0:T(8,128)(2,1)}, f16[48,3072]{1,0:T(8,128)(2,1)S(1)}, u32[]{:S(2)}) copy-start(f16[48,3072]{1,0:T(8,128)(2,1)S(1)} %fusion.5) | copy-start | bytes 884740
  55.8 21.2 %collective-permute-start.10 = (f16[48,3072]{1,0:T(8,128)(2,1)S(1)}, f16[48,3072]{1,0:T(8,128)(2,1)S(1)}, u32[]{:S(2)}, u32[]{:S(2)}) collective-permute-start(f16[48,3072]{1,0:T(8,128)(2,1)S(1)} %fusion.5), channel_id=1, source_target_pairs={{0,64},{8,72},{16,80},{24,88},{1,65},{9,73},{17,81},{25,89},{2,66}... | collective-permute-start | bytes 884744 | tf_op jit(solution)/shard_map/ppermute | solution.py:317
  61.4 15.5 %collective-permute-start.11 = (f16[48,3072]{1,0:T(8,128)(2,1)S(1)}, f16[48,3072]{1,0:T(8,128)(2,1)S(1)}, u32[]{:S(2)}, u32[]{:S(2)}) collective-permute-start(f16[48,3072]{1,0:T(8,128)(2,1)S(1)} %fusion.5), channel_id=1, source_target_pairs={{0,96},{8,104},{16,112},{24,120},{1,97},{9,105},{17,113},{25,121},... | collective-permute-start | bytes 884744 | tf_op jit(solution)/shard_map/ppermute | solution.py:317
  62.8 18.8 %collective-permute-start.9 = (f16[48,3072]{1,0:T(8,128)(2,1)S(1)}, f16[48,3072]{1,0:T(8,128)(2,1)S(1)}, u32[]{:S(2)}, u32[]{:S(2)}) collective-permute-start(f16[48,3072]{1,0:T(8,128)(2,1)S(1)} %fusion.5), channel_id=1, source_target_pairs={{0,32},{8,40},{16,48},{24,56},{1,33},{9,41},{17,49},{25,57},{2,34}... | collective-permute-start | bytes 884744 | tf_op jit(solution)/shard_map/ppermute | solution.py:317
  64.1 3.1 %copy-start.1 = (bf16[3,3072,384]{2,1,0:T(8,128)(2,1)S(1)}, bf16[3,3072,384]{2,1,0:T(8,128)(2,1)}, u32[]{:S(2)}) copy-start(bf16[3,3072,384]{2,1,0:T(8,128)(2,1)} %w_ref.7) | copy-start | bytes 21233668
  76.9 4.6 %copy-start.14 = (f16[48,3072]{1,0:T(8,128)(2,1)}, f16[48,3072]{1,0:T(8,128)(2,1)S(1)}, u32[]{:S(2)}) copy-start(f16[48,3072]{1,0:T(8,128)(2,1)S(1)} %collective-permute-done.10) | copy-start | bytes 884740
  76.9 4.6 %copy-start.15 = (f16[48,3072]{1,0:T(8,128)(2,1)}, f16[48,3072]{1,0:T(8,128)(2,1)S(1)}, u32[]{:S(2)}) copy-start(f16[48,3072]{1,0:T(8,128)(2,1)S(1)} %collective-permute-done.11) | copy-start | bytes 884740
  81.5 0.7 copy-start.16
  82.2 6.1 %collective-permute-start.12 = (bf16[192,3072]{1,0:T(8,128)(2,1)}, bf16[192,3072]{1,0:T(8,128)(2,1)}, u32[]{:S(2)}, u32[]{:S(2)}) collective-permute-start(bf16[192,3072]{1,0:T(8,128)(2,1)} %collective-permute-done.6.first_ref), channel_id=1, source_target_pairs={{0,1},{1,0},{2,3},{3,2},{4,5},{5,4},{6,7},{7,6},{8,9},{9,8},{10,11... | collective-permute-start | bytes 3538952 | tf_op jit(solution)/shard_map/ppermute | solution.py:110
  82.2 14.1 %copy-start.9 = (s32[3,4,3]{2,1,0:T(4,128)S(1)}, s32[3,4,3]{2,1,0:T(4,128)}, u32[]{:S(2)}) copy-start(s32[3,4,3]{2,1,0:T(4,128)} %list_ref.7) | copy-start | bytes 436
  84.1 24.7 %collective-permute-start.13 = (f16[48,3072]{1,0:T(8,128)(2,1)}, f16[48,3072]{1,0:T(8,128)(2,1)}, u32[]{:S(2)}, u32[]{:S(2)}) collective-permute-start(f16[48,3072]{1,0:T(8,128)(2,1)} %select_select_fusion), channel_id=1, source_target_pairs={{0,24},{8,0},{16,8},{24,16},{32,56},{40,32},{48,40},{56,48},{64,88... | collective-permute-start | bytes 884744 | tf_op jit(solution)/shard_map/ppermute | solution.py:115
  87.6 26.2 %collective-permute-start.14 = (f16[48,3072]{1,0:T(8,128)(2,1)}, f16[48,3072]{1,0:T(8,128)(2,1)}, u32[]{:S(2)}, u32[]{:S(2)}) collective-permute-start(f16[48,3072]{1,0:T(8,128)(2,1)} %select_select_fusion), channel_id=1, source_target_pairs={{0,16},{8,24},{16,0},{24,8},{32,48},{40,56},{48,32},{56,40},{64,80... | collective-permute-start | bytes 884744 | tf_op jit(solution)/shard_map/ppermute | solution.py:115
  87.6 26.2 %collective-permute-start.15 = (f16[48,3072]{1,0:T(8,128)(2,1)}, f16[48,3072]{1,0:T(8,128)(2,1)}, u32[]{:S(2)}, u32[]{:S(2)}) collective-permute-start(f16[48,3072]{1,0:T(8,128)(2,1)} %select_select_fusion), channel_id=1, source_target_pairs={{0,8},{8,16},{16,24},{24,0},{32,40},{40,48},{48,56},{56,32},{64,72... | collective-permute-start | bytes 884744 | tf_op jit(solution)/shard_map/ppermute | solution.py:115
  88.4 3.2 %copy-start.2 = (bf16[3,3072,384]{2,1,0:T(8,128)(2,1)S(1)}, bf16[3,3072,384]{2,1,0:T(8,128)(2,1)}, u32[]{:S(2)}) copy-start(bf16[3,3072,384]{2,1,0:T(8,128)(2,1)} %w_ref.7) | copy-start | bytes 21233668
  104.0 10.0 %collective-permute-start.16 = (bf16[384,384]{1,0:T(8,128)(2,1)}, bf16[384,384]{1,0:T(8,128)(2,1)}, u32[]{:S(2)}, u32[]{:S(2)}) collective-permute-start(bf16[384,384]{1,0:T(8,128)(2,1)} %attend_tile.5), channel_id=1, source_target_pairs={{0,2},{1,3},{2,4},{3,5},{4,6},{5,7},{6,0},{7,1},{8,10},{9,11},{10,... | collective-permute-start | bytes 884744 | tf_op jit(solution)/shard_map/ppermute | solution.py:106
  104.0 13.9 %collective-permute-start.17 = (bf16[384,384]{1,0:T(8,128)(2,1)}, bf16[384,384]{1,0:T(8,128)(2,1)}, u32[]{:S(2)}, u32[]{:S(2)}) collective-permute-start(bf16[384,384]{1,0:T(8,128)(2,1)} %attend_tile.6), channel_id=1, source_target_pairs={{0,4},{1,5},{2,6},{3,7},{4,0},{5,1},{6,2},{7,3},{8,12},{9,13},{10,... | collective-permute-start | bytes 884744 | tf_op jit(solution)/shard_map/ppermute | solution.py:106
  108.9 10.9 %collective-permute-start.18 = (bf16[384,384]{1,0:T(8,128)(2,1)}, bf16[384,384]{1,0:T(8,128)(2,1)}, u32[]{:S(2)}, u32[]{:S(2)}) collective-permute-start(bf16[384,384]{1,0:T(8,128)(2,1)} %attend_tile.7), channel_id=1, source_target_pairs={{0,6},{1,7},{2,0},{3,1},{4,2},{5,3},{6,4},{7,5},{8,14},{9,15},{10,... | collective-permute-start | bytes 884744 | tf_op jit(solution)/shard_map/ppermute | solution.py:106
  121.2 7.7 %collective-permute-start.19 = (bf16[4,2,48,384]{3,2,1,0:T(8,128)(2,1)S(1)}, bf16[4,2,48,384]{3,2,1,0:T(8,128)(2,1)S(1)}, u32[]{:S(2)}, u32[]{:S(2)}) collective-permute-start(bf16[4,2,48,384]{3,2,1,0:T(8,128)(2,1)S(1)} %get-tuple-element.59), channel_id=1, source_target_pairs={{0,8},{8,16},{16,24},{24,0},{32,40},{40,48},{48,56},{56,32},{64,72... | collective-permute-start | bytes 884744 | tf_op jit(solution)/shard_map/ppermute | solution.py:115
  123.0 12.9 %collective-permute-start.20 = (bf16[4,2,48,384]{3,2,1,0:T(8,128)(2,1)S(1)}, bf16[4,2,48,384]{3,2,1,0:T(8,128)(2,1)S(1)}, u32[]{:S(2)}, u32[]{:S(2)}) collective-permute-start(bf16[4,2,48,384]{3,2,1,0:T(8,128)(2,1)S(1)} %get-tuple-element.58), channel_id=1, source_target_pairs={{0,16},{8,24},{16,0},{24,8},{32,48},{40,56},{48,32},{56,40},{64,80... | collective-permute-start | bytes 884744 | tf_op jit(solution)/shard_map/ppermute | solution.py:115
  124.5 12.3 %collective-permute-start.21 = (bf16[4,2,48,384]{3,2,1,0:T(8,128)(2,1)S(1)}, bf16[4,2,48,384]{3,2,1,0:T(8,128)(2,1)S(1)}, u32[]{:S(2)}, u32[]{:S(2)}) collective-permute-start(bf16[4,2,48,384]{3,2,1,0:T(8,128)(2,1)S(1)} %get-tuple-element.57), channel_id=1, source_target_pairs={{0,24},{8,0},{16,8},{24,16},{32,56},{40,32},{48,40},{56,48},{64,88... | collective-permute-start | bytes 884744 | tf_op jit(solution)/shard_map/ppermute | solution.py:115
  136.8 3.7 %copy-start.3 = (bf16[6144,768]{1,0:T(8,128)(2,1)S(1)}, bf16[6144,768]{1,0:T(8,128)(2,1)}, u32[]{:S(2)}) copy-start(bf16[6144,768]{1,0:T(8,128)(2,1)} %all-gather.3.cloned.1.call-done) | copy-start | bytes 28311556
  143.8 5.5 %copy-start.10 = (f32[4,3072]{1,0:T(4,128)S(1)}, f32[4,3072]{1,0:T(4,128)}, u32[]{:S(2)}) copy-start(f32[4,3072]{1,0:T(4,128)} %get-tuple-element.46.gate_ref) | copy-start | bytes 147460
  143.8 5.5 %collective-permute-start.22 = (bf16[4,192,768]{2,1,0:T(8,128)(2,1)S(1)}, bf16[4,192,768]{2,1,0:T(8,128)(2,1)S(1)}, u32[]{:S(2)}, u32[]{:S(2)}) collective-permute-start(bf16[4,192,768]{2,1,0:T(8,128)(2,1)S(1)} %out_half.3), channel_id=1, source_target_pairs={{0,1},{1,0},{2,3},{3,2},{4,5},{5,4},{6,7},{7,6},{8,9},{9,8},{10,11... | collective-permute-start | bytes 3538952 | tf_op jit(solution)/shard_map/ppermute | solution.py:110
  150.2 10.7 %collective-permute-start.23 = (bf16[4,48,768]{2,1,0:T(8,128)(2,1)S(1)}, bf16[4,48,768]{2,1,0:T(8,128)(2,1)S(1)}, u32[]{:S(2)}, u32[]{:S(2)}) collective-permute-start(bf16[4,48,768]{2,1,0:T(8,128)(2,1)S(1)} %get-tuple-element.48), channel_id=1, source_target_pairs={{0,32},{8,40},{16,48},{24,56},{32,64},{40,72},{48,80},{56,88},{64,... | collective-permute-start | bytes 884744 | tf_op jit(solution)/shard_map/ppermute | solution.py:126
  154.5 12.7 %collective-permute-start.24 = (bf16[4,48,768]{2,1,0:T(8,128)(2,1)S(1)}, bf16[4,48,768]{2,1,0:T(8,128)(2,1)S(1)}, u32[]{:S(2)}, u32[]{:S(2)}) collective-permute-start(bf16[4,48,768]{2,1,0:T(8,128)(2,1)S(1)} %get-tuple-element.48), channel_id=1, source_target_pairs={{0,64},{8,72},{16,80},{24,88},{32,96},{40,104},{48,112},{56,120},{... | collective-permute-start | bytes 884744 | tf_op jit(solution)/shard_map/ppermute | solution.py:126
  155.8 12.8 %collective-permute-start.25 = (bf16[4,48,768]{2,1,0:T(8,128)(2,1)S(1)}, bf16[4,48,768]{2,1,0:T(8,128)(2,1)S(1)}, u32[]{:S(2)}, u32[]{:S(2)}) collective-permute-start(bf16[4,48,768]{2,1,0:T(8,128)(2,1)S(1)} %get-tuple-element.48), channel_id=1, source_target_pairs={{0,96},{8,104},{16,112},{24,120},{1,97},{9,105},{17,113},{25,121},... | collective-permute-start | bytes 884744 | tf_op jit(solution)/shard_map/ppermute | solution.py:126
  168.9 8.9 %collective-permute-start.26 = (bf16[4,48,768]{2,1,0:T(8,128)(2,1)S(1)}, bf16[4,48,768]{2,1,0:T(8,128)(2,1)S(1)}, u32[]{:S(2)}, u32[]{:S(2)}) collective-permute-start(bf16[4,48,768]{2,1,0:T(8,128)(2,1)S(1)} %get-tuple-element.55), channel_id=1, source_target_pairs={{0,24},{8,0},{16,8},{24,16},{32,56},{40,32},{48,40},{56,48},{64,88... | collective-permute-start | bytes 884744 | tf_op jit(solution)/shard_map/ppermute | solution.py:115
  171.2 9.3 %collective-permute-start.27 = (bf16[4,48,768]{2,1,0:T(8,128)(2,1)S(1)}, bf16[4,48,768]{2,1,0:T(8,128)(2,1)S(1)}, u32[]{:S(2)}, u32[]{:S(2)}) collective-permute-start(bf16[4,48,768]{2,1,0:T(8,128)(2,1)S(1)} %get-tuple-element.54), channel_id=1, source_target_pairs={{0,16},{8,24},{16,0},{24,8},{32,48},{40,56},{48,32},{56,40},{64,80... | collective-permute-start | bytes 884744 | tf_op jit(solution)/shard_map/ppermute | solution.py:115
  172.1 15.9 %collective-permute-start.28 = (bf16[4,48,768]{2,1,0:T(8,128)(2,1)S(1)}, bf16[4,48,768]{2,1,0:T(8,128)(2,1)S(1)}, u32[]{:S(2)}, u32[]{:S(2)}) collective-permute-start(bf16[4,48,768]{2,1,0:T(8,128)(2,1)S(1)} %get-tuple-element.53), channel_id=1, source_target_pairs={{0,8},{8,16},{16,24},{24,0},{32,40},{40,48},{48,56},{56,32},{64,72... | collective-permute-start | bytes 884744 | tf_op jit(solution)/shard_map/ppermute | solution.py:115
  173.4 14.6 %copy-start.5 = (f32[1,192,3072]{2,1,0:T(8,128)S(1)}, f32[1,192,3072]{2,1,0:T(8,128)}, u32[]{:S(2)}) copy-start(f32[1,192,3072]{2,1,0:T(8,128)} %lat_hbm.1) | copy-start | bytes 7077892
Sparse Core Ops, SparseCore 0:
  10.1 94.6 all-gather.2

commit v3 on v2

v3 whole, which is shorter than its diff:
```python
import functools
import math

import jax
import jax.numpy as jnp
from jax import lax
from jax.experimental import pallas as pl
from jax.experimental.pallas import tpu as pltpu
from jax.sharding import PartitionSpec as P

D = 3072
BLOCK = 384
HEAD = 128
LOCAL_HEADS = 3
WIDTH = LOCAL_HEADS * HEAD
NX = 4
NY = 4
NZ = 4
ROWS = 192
SUB = 48
COLS = D // NY
DEEP = WIDTH // NZ
eps_norm = 1e-06

BF = jnp.bfloat16
F32 = jnp.float32
VMEM = pl.BlockSpec(memory_space=pltpu.VMEM)
SMEM = pl.BlockSpec(memory_space=pltpu.SMEM)


def modulate_kernel(stamps_ref, freq_ref, w_hbm, lat_hbm, out_ref, gate_ref, w, lat, held, w_sems, lat_sems):
    step = lax.axis_index("tm")
    row, y = step // NY, step % NY
    lat_copies = [
        pltpu.make_async_copy(lat_hbm.at[0, part], lat.at[part], lat_sems.at[n])
        for n, part in enumerate(pl.ds(n * SUB, SUB) for n in range(4))
    ]
    w_copies = [
        pltpu.make_async_copy(w_hbm.at[:, part], w.at[:, part], w_sems.at[n])
        for n, part in enumerate(pl.ds(n * D, D) for n in range(3))
    ]
    for copy in lat_copies + w_copies:
        copy.start()

    lane = lax.broadcasted_iota(jnp.int32, (8, HEAD), 0)
    stamps = jnp.zeros((8, HEAD), F32)
    for n in range(NY):
        stamps = jnp.where(lane == n, stamps_ref[row * NY + n].astype(F32), stamps)
    angles = stamps * freq_ref[...]
    emb = jnp.concatenate([jnp.cos(angles), jnp.sin(angles)], axis=1).astype(BF)

    for n in range(4):
        lat_copies[n].wait()
        part = slice(n * SUB, (n + 1) * SUB)
        current = lat[part, :]
        centred = current - jnp.mean(current, axis=-1, keepdims=True)
        var = jnp.mean(centred * centred, axis=-1, keepdims=True)
        lat[part, :] = centred * lax.rsqrt(var + eps_norm)

    def project(n):
        w_copies[n].wait()
        held[:, n * D : (n + 1) * D] = jnp.dot(
            emb, w[:, n * D : (n + 1) * D], preferred_element_type=F32
        )

    project(0)
    project(1)
    shift = held[pl.ds(y, 1), :D]
    scale = held[pl.ds(y, 1), D : 2 * D]
    for n in range(4):
        part = slice(n * SUB, (n + 1) * SUB)
        out_ref[part, :] = (lat[part, :] * (1.0 + scale) + shift).astype(BF)
    project(2)
    for n in range(NY):
        delta = (stamps_ref[row * NY + n + 1] - stamps_ref[row * NY + n]).astype(F32) / 1000.0
        gate_ref[n : n + 1, :] = held[n : n + 1, 2 * D :] * delta


def modulate(latents, timesteps, mod_weight):
    half = mod_weight.shape[0] // 2
    freqs = jnp.exp(-jnp.log(10000.0) * jnp.arange(half, dtype=F32) / half)
    return pl.pallas_call(
        modulate_kernel,
        in_specs=[
            pl.BlockSpec(memory_space=pltpu.SMEM),
            VMEM,
            pl.BlockSpec(memory_space=pl.ANY),
            pl.BlockSpec(memory_space=pl.ANY),
        ],
        out_specs=[VMEM, VMEM],
        out_shape=[
            jax.ShapeDtypeStruct((ROWS, D), BF),
            jax.ShapeDtypeStruct((NY, D), F32),
        ],
        scratch_shapes=[
            pltpu.VMEM((2 * half, 3 * D), BF),
            pltpu.VMEM((ROWS, D), F32),
            pltpu.VMEM((8, 3 * D), F32),
            pltpu.SemaphoreType.DMA((3,)),
            pltpu.SemaphoreType.DMA((4,)),
        ],
        compiler_params=pltpu.CompilerParams(vmem_limit_bytes=58 << 20),
        cost_estimate=pl.CostEstimate(
            flops=10 * ROWS * D, bytes_accessed=9_000_000, transcendentals=ROWS
        ),
        name="modulate",
    )(timesteps, freqs[None], mod_weight, latents)


def shift_x(array, by):
    return lax.ppermute(array, "seq", [(i, (i + 2 * by) % 8) for i in range(8)])


def swap_core(array):
    return lax.ppermute(array, "seq", [(i, i ^ 1) for i in range(8)])


def shift_y(array, by):
    pairs = [(z * NY + y, z * NY + (y + by) % NY) for z in range(NZ) for y in range(NY)]
    return lax.ppermute(array, "tm", pairs)


def opposite_x(forward, backward):
    core = lax.axis_index("seq") % 2
    send = jnp.where(core == 0, forward, backward)
    return lax.ppermute(send, "seq", [(i, (i + 2 - 4 * (i % 2)) % 8) for i in range(8)])


def up_z(array, by):
    pairs = [(z * NY + y, (z + by) * NY + y) for z in range(NZ - by) for y in range(NY)]
    return lax.ppermute(array, "tm", pairs)


def qkv_kernel(places, *refs):
    parts, (gain_ref, w_ref), out_ref = refs[: 2 * len(places)], refs[2 * len(places) :][:2], refs[-1]
    rows = jnp.concatenate([part[...] for part in parts], axis=0)
    blocks = [(kind, h) for kind in range(3) for h in range(LOCAL_HEADS)]
    for n in range(0, len(blocks), 2):
        pair = blocks[n : n + 2]
        weight = [w_ref[kind, :, h * HEAD : (h + 1) * HEAD] for kind, h in pair]
        weight = jnp.concatenate(weight, axis=1) if len(pair) > 1 else weight[0]
        proj = jnp.dot(rows, weight, preferred_element_type=F32)
        for m, (kind, h) in enumerate(pair):
            part = proj[:, m * HEAD : (m + 1) * HEAD]
            if kind < 2:
                inverse = lax.rsqrt(jnp.mean(part * part, axis=-1, keepdims=True) + eps_norm)
                part = part * inverse * gain_ref[kind : kind + 1, :]
            part = part.astype(BF)
            for t, place in enumerate(places):
                out_ref[place, kind, :, h * HEAD : (h + 1) * HEAD] = part[t * BLOCK : (t + 1) * BLOCK]


def qkv_tiles(parts, places, gain, weight, held):
    earlier = [] if held is None else [held]
    return pl.pallas_call(
        functools.partial(qkv_kernel, places),
        in_specs=[VMEM] * (len(parts) + 2 + len(earlier)),
        out_specs=VMEM,
        out_shape=jax.ShapeDtypeStruct((NX, 3, BLOCK, WIDTH), BF),
        input_output_aliases={len(parts) + 2: 0} if earlier else {},
        compiler_params=pltpu.CompilerParams(vmem_limit_bytes=16 << 20),
        cost_estimate=pl.CostEstimate(
            flops=2 * len(places) * BLOCK * D * 3 * WIDTH, bytes_accessed=10_000_000, transcendentals=0
        ),
        name="qkv_tiles",
    )(*parts, gain, weight, *earlier)


def attend_kernel(place, list_ref, held_ref, out_ref):
    x = lax.axis_index("seq") // 2
    factor = 1.0 / math.sqrt(HEAD)
    ones = jnp.ones((BLOCK, HEAD), BF)
    for h in range(LOCAL_HEADS):
        cols = slice(h * HEAD, (h + 1) * HEAD)
        tiles = [(list_ref[h, (x + place) % NX, n] - x) % NX for n in range(3)]
        query = held_ref[place, 0, :, cols]
        scores = [
            lax.dot_general(
                query, held_ref[t, 1, :, cols], (((1,), (1,)), ((), ())), preferred_element_type=F32
            )
            for t in tiles
        ]
        top = functools.reduce(jnp.maximum, [jnp.max(s, axis=-1, keepdims=True) for s in scores])
        total = jnp.zeros((BLOCK, 2 * HEAD), F32)
        for s, t in zip(scores, tiles):
            probs = jnp.exp((s - top) * factor).astype(BF)
            values = jnp.concatenate([held_ref[t, 2, :, cols], ones], axis=1)
            total += jnp.dot(probs, values, preferred_element_type=F32)
        out_ref[:, cols] = (total[:, :HEAD] / total[:, HEAD:]).astype(BF)


def attend_tile(block_list, place, held):
    return pl.pallas_call(
        functools.partial(attend_kernel, place),
        in_specs=[SMEM, VMEM],
        out_specs=VMEM,
        out_shape=jax.ShapeDtypeStruct((BLOCK, WIDTH), BF),
        compiler_params=pltpu.CompilerParams(vmem_limit_bytes=12 << 20),
        cost_estimate=pl.CostEstimate(
            flops=4 * 3 * BLOCK * 3 * BLOCK * HEAD, bytes_accessed=4_000_000, transcendentals=0
        ),
        name="attend_tile",
    )(block_list, held)


def pack_kernel(a0, a1, a2, a3, *outs):
    y = lax.axis_index("tm") % NY
    for d, out_ref in enumerate(outs):
        sub = (y + d) % NY
        for n, a in enumerate((a0, a1, a2, a3)):
            for half in range(2):
                at = pl.multiple_of(half * ROWS + sub * SUB, 16)
                out_ref[n, half] = a[pl.ds(at, SUB), :]


def pack(arrived):
    return pl.pallas_call(
        pack_kernel,
        in_specs=[VMEM] * NX,
        out_specs=[VMEM] * NY,
        out_shape=[jax.ShapeDtypeStruct((NX, 2, SUB, WIDTH), BF)] * NY,
        compiler_params=pltpu.CompilerParams(vmem_limit_bytes=12 << 20),
        cost_estimate=pl.CostEstimate(flops=1, bytes_accessed=40_000_000, transcendentals=0),
        name="pack",
    )(*arrived)


def out_kernel(p0, p1, p2, p3, own_ref, w_ref, gate_ref, mine_ref, other_ref, rows):
    y = lax.axis_index("tm") % NY
    for half in range(2):
        for d in range(NX):
            part = [p[d, half] for p in (p0, p1, p2, p3)]
            at = slice(half * ROWS, (half + 1) * ROWS)
            rows[at, d * WIDTH : (d + 1) * WIDTH] = jnp.concatenate(part, axis=0)
    for n in range(NY):
        cols = slice(n * COLS, (n + 1) * COLS)
        block = [own_ref[:, cols]]
        block += [w_ref[z, n, d] for d in range(NX - 1) for z in range(NZ)]
        block = jnp.concatenate(block, axis=0)
        proj = jnp.dot(rows[...], block, preferred_element_type=F32)
        for d in range(NY):
            gate = gate_ref[pl.ds((y - d) % NY, 1), cols]
            mine_ref[n, d] = (proj[d * SUB : (d + 1) * SUB] * gate).astype(BF)
            other_ref[n, d] = (proj[ROWS + d * SUB : ROWS + (d + 1) * SUB] * gate).astype(BF)


def out_project(pieces, own, gathered, gates):
    return pl.pallas_call(
        out_kernel,
        in_specs=[VMEM] * 7,
        out_specs=[VMEM] * 2,
        out_shape=[jax.ShapeDtypeStruct((NY, NY, SUB, COLS), BF)] * 2,
        scratch_shapes=[pltpu.VMEM((2 * ROWS, NX * WIDTH), BF)],
        compiler_params=pltpu.CompilerParams(vmem_limit_bytes=12 << 20),
        cost_estimate=pl.CostEstimate(
            flops=4 * ROWS * NX * WIDTH * D, bytes_accessed=12_000_000, transcendentals=0
        ),
        name="out_project",
    )(*pieces, own, gathered, gates)


def row_kernel(part, own_ref, other_ref, part_ref, total_ref, held):
    y = lax.axis_index("tm") % NY
    for n in range(2):
        for d in range(NY):
            at = 2 * part + n
            held[(y - d) % NY] = own_ref[at, d].astype(F32) + other_ref[at, d].astype(F32)
        held[1] = held[0] + held[1]
        held[2] = held[1] + held[2]
        held[3] = held[2] + held[3]
        total_ref[n] = held[3].astype(BF)
        for d in range(NY):
            part_ref[d, n] = held[(y - d) % NY]


def row_prefix(part, own, other):
    return pl.pallas_call(
        functools.partial(row_kernel, part),
        in_specs=[VMEM] * 2,
        out_specs=[VMEM] * 2,
        out_shape=[
            jax.ShapeDtypeStruct((NY, 2, SUB, COLS), F32),
            jax.ShapeDtypeStruct((2, SUB, COLS), BF),
        ],
        scratch_shapes=[pltpu.VMEM((NY, SUB, COLS), F32)],
        compiler_params=pltpu.CompilerParams(vmem_limit_bytes=12 << 20),
        cost_estimate=pl.CostEstimate(flops=1, bytes_accessed=2_000_000, transcendentals=0),
        name="row_prefix",
    )(own, other)


def final_kernel(lat_ref, *refs):
    pieces, firsts, out_ref = refs[:4], refs[4:8], refs[-1]
    step = lax.axis_index("tm")
    y = step % NY
    for d in range(NY):
        at = (y + d) % NY
        first = jnp.where(step == 0, lat_ref[at], firsts[d][...])
        out_ref[at] = first + pieces[d][0].astype(F32)


def final_sum(part, latents, pieces, firsts, earlier):
    piece = pl.BlockSpec((1, SUB, COLS), lambda n: (n, 0, 0))
    first = pl.BlockSpec((SUB, COLS), lambda n: (0, 2 * part + n))
    block = pl.BlockSpec((NY, SUB, COLS), lambda n: (0, 0, 2 * part + n))
    more = [] if earlier is None else [earlier]
    return pl.pallas_call(
        final_kernel,
        grid=(2,),
        in_specs=[block] + [piece] * 4 + [first] * 4 + [pl.BlockSpec(memory_space=pl.ANY)] * len(more),
        out_specs=block,
        out_shape=jax.ShapeDtypeStruct((NY, SUB, D), F32),
        input_output_aliases={9: 0} if more else {},
        compiler_params=pltpu.CompilerParams(vmem_limit_bytes=12 << 20),
        cost_estimate=pl.CostEstimate(flops=1, bytes_accessed=1, transcendentals=0),
        name="final_sum",
    )(latents.reshape(NY, SUB, D), *pieces, *firsts, *more)


def barrier(*arrays):
    return lax.optimization_barrier(arrays)


def per_device(latents, timesteps, mod_weight, qkv_weight, qk_gain, out_weight, block_list):
    step = lax.axis_index("tm")
    z, y = step // NY, step % NY

    piece = lax.dynamic_slice(out_weight, (z * DEEP, y * COLS), (DEEP, COLS))
    pieces = [shift_x(piece, d) for d in range(1, NX)]
    modulated, gates = modulate(latents, timesteps, mod_weight)
    modulated, pieces = barrier(modulated, pieces)
    gathered = lax.all_gather(jnp.stack(pieces), "tm").reshape(NZ, NY, NX - 1, DEEP, COLS)

    twin = swap_core(modulated)
    before = shift_x(modulated, 1)
    after = shift_x(modulated, -1)

    twin, current, weight = barrier(twin, latents[0], qkv_weight)
    half = current.astype(jnp.float16).reshape(NY, SUB, D)
    parts = [lax.ppermute(half[to], "tm", [(0, to)]) for to in range(1, NY)]
    held = qkv_tiles([modulated, twin], (0,), qk_gain, weight, None)

    before, after, held, parts, half = barrier(before, after, held, parts, half)
    far = opposite_x(before, after)
    quarter = half[0]
    for to in range(1, NY):
        quarter = jnp.where(y == to, parts[to - 1], quarter)
    near = [after, swap_core(after), before, swap_core(before)]
    held = qkv_tiles(near, (1, 3), qk_gain, weight, held)
    far, held, quarter = barrier(far, held, quarter)
    held = qkv_tiles([far, swap_core(far)], (2,), qk_gain, weight, held)

    arrived = [None] * NX
    for d in (2, 1, 3, 0):
        if d == 0:
            held, arrived[2] = barrier(held, arrived[2])
        attended = attend_tile(block_list, d, held)
        arrived[d] = shift_x(attended, d) if d else attended

    arrived, gathered, quarter, own_weight = barrier(arrived, gathered, quarter, out_weight)
    pieces = pack(arrived)
    pieces = [shift_y(send, d) if d else send for d, send in enumerate(pieces)]
    got = lax.ppermute(quarter, "tm", [(n, 2 * NY + n) for n in range(NY)])
    quarter = jnp.where(z == 2, got, quarter)
    pieces, quarter = barrier(pieces, quarter)
    got = lax.ppermute(
        quarter, "tm", [(at * NY + n, (at + 1) * NY + n) for n in range(NY) for at in (0, 2)]
    )
    own, other = out_project(pieces, own_weight, gathered, gates)

    own, other, got, quarter = barrier(own, other, got, quarter)
    other = swap_core(other)
    quarter = jnp.where(z % 2 == 1, got, quarter)
    firsts = [shift_y(quarter, -d) if d else quarter for d in range(NY)]

    result = None
    for part in range(2):
        parts, total = row_prefix(part, own, other)
        base = sum(up_z(total, by).astype(F32) for by in range(1, NZ))
        back = []
        for d in range(NY):
            send = (parts[d] + base).astype(BF)
            back.append(shift_y(send, -d) if d else send)
        if part == 0:
            firsts = [first.astype(F32) for first in firsts]
        result = final_sum(part, latents, back, firsts, result)
    return result.reshape(1, ROWS, D)


def solution(mesh):
    return jax.shard_map(
        per_device,
        mesh=mesh,
        in_specs=(
            P("tm", "seq", None),
            P(),
            P(),
            P(None, None, "seq"),
            P(),
            P("seq", None),
            P("seq", None, None),
        ),
        out_specs=P("tm", "seq", None),
        check_vma=False,
    )
```

time: 198 us -> 188 us (0.949)
  starting transfers between devices: 51.5 us -> 65.2 us
  local copies, waits for them, and re-layouts: 21 us -> 14.3 us
  other arithmetic: 11.9 us -> 5.27 us
  waiting for transfers between devices: 51.4 us -> 44.8 us
  Pallas kernels: 47.8 us -> 43.6 us
    ppermute x3 -> x6, waiting for transfers between devices: 11.5 us -> 3.62 us  [up_z(): return lax.ppermute(array, 'tm', pairs)]
    ppermute x5 -> x8, starting transfers between devices: 5.53 us -> 11.6 us  [shift_x(): return lax.ppermute(array, 'seq', [(i, (i + 2 * by) % 8) for i in range(8)])]
    unnamed x34 -> x32, local copies, waits for them, and re-layouts: 18.3 us -> 12.4 us
    ppermute x5, waiting for transfers between devices: 0.01 us -> 5.3 us  [swap_core(): return lax.ppermute(array, 'seq', [(i, i ^ 1) for i in range(8)])]
    ppermute x3 -> x6, starting transfers between devices: 6.92 us -> 12 us  [up_z(): return lax.ppermute(array, 'tm', pairs)]
    ppermute x3 -> x2, waiting for transfers between devices: 4.57 us -> 0.01 us  [the longest x1 0.01 us: per_device(): got = lax.ppermute(quarter, 'tm', [(n, 2 * NY + n) for n in range(NY)])]
    convert_element_type x4, other arithmetic: 4.16 us -> 0.22 us  [per_device(): firsts = [first.astype(F32) for first in firsts]]
    ppermute x1, waiting for transfers between devices: 0.01 us -> 3.35 us  [opposite_x(): lax.ppermute(send, 'seq', [(i, (i + 2 - 4 * (i % 2)) % 8) for i in range(...]
  transfers between devices with their start and end apart: 30 -> 38, of which waited for: 14 -> 15; matrix products, arithmetic and copies ran while one was open for 6% -> 3% of each run, Pallas kernels for 21% -> 22%
where the time goes in v3:
time: 188 us; the launch traced here: 187 us
  starting transfers between devices  65.2 us (35%)
  waiting for transfers between devices  44.8 us (24%)
  Pallas kernels  43.6 us (23%)
  local copies, waits for them, and re-layouts  14.3 us (8%)
  between operations  13.8 us (7%)
  other arithmetic  5.27 us (3%)
    ppermute x12, waiting for transfers between devices, shift_y(): return lax.ppermute(array, 'tm', pairs)  22.1 us
    ppermute x12, starting transfers between devices, shift_y(): return lax.ppermute(array, 'tm', pairs)  15.3 us
    pallas_call x3, Pallas kernels, qkv_tiles(): pl.pallas_call(functools.partial(qkv_kernel, places), in_specs=[VMEM] * (...  14.5 us
    pallas_call x4, Pallas kernels, attend_tile(): pl.pallas_call(functools.partial(attend_kernel, place), in_specs=[SMEM, V...  12.6 us
    unnamed x32, local copies, waits for them, and re-layouts  12.4 us
    ppermute x6, starting transfers between devices, up_z(): return lax.ppermute(array, 'tm', pairs)  12 us
    ppermute x8, starting transfers between devices, shift_x(): return lax.ppermute(array, 'seq', [(i, (i + 2 * by) % 8) for i in range(8)])  11.6 us
    ppermute x8, waiting for transfers between devices, shift_x(): return lax.ppermute(array, 'seq', [(i, (i + 2 * by) % 8) for i in range(8)])  10.4 us
  transfers between devices with their start and end apart: 38, of which 15 were waited for; matrix products, arithmetic and copies ran while one was open for 3% of the time, Pallas kernels for 22%

profile of v3, /device:TPU:1, one launch (start us, length us, event | category | flops | bytes accessed | tf_op | source)
XLA Modules:
  0.0 187.0 jit_solution(7648120886009694718)
XLA Ops:
  6.5 0.9 dynamic_slice.3
  7.5 2.1 %collective-permute-start = (bf16[96,768]{1,0:T(8,128)(2,1)S(1)}, bf16[96,768]{1,0:T(8,128)(2,1)S(1)}, u32[]{:S(2)}, u32[]{:S(2)}) collective-permute-start(bf16[96,768]{1,0:T(8,128)(2,1)S(1)} %dynamic_slice.3), channel_id=1, source_target_pairs={{0,2},{1,3},{2,4},{3,5},{4,6},{5,7},{6,0},{7,1},{8,10},{9,11},{10,... | collective-permute-start | bytes 442376 | tf_op jit(solution)/shard_map/ppermute | solution.py:111
  9.6 2.5 %collective-permute-start.1 = (bf16[96,768]{1,0:T(8,128)(2,1)S(1)}, bf16[96,768]{1,0:T(8,128)(2,1)S(1)}, u32[]{:S(2)}, u32[]{:S(2)}) collective-permute-start(bf16[96,768]{1,0:T(8,128)(2,1)S(1)} %dynamic_slice.3), channel_id=1, source_target_pairs={{0,4},{1,5},{2,6},{3,7},{4,0},{5,1},{6,2},{7,3},{8,12},{9,13},{10,... | collective-permute-start | bytes 442376 | tf_op jit(solution)/shard_map/ppermute | solution.py:111
  12.0 1.2 collective-permute-start.2
  13.7 5.7 %modulate.1 = (bf16[192,3072]{1,0:T(8,128)(2,1)}, f32[4,3072]{1,0:T(4,128)}) custom-call(s32[17]{0:T(128)} %stamps_ref.1, f32[1,128]{1,0:T(1,128)} %multiply_exponential_fusion.freq_ref, bf16[256,9216]{1,0:T(8,128)(2,1)} %w_hbm.1, f32[1,192,3072]{2,1,0:T(8,128)} %lat_hbm.1), custom_call_target="tpu_custom_call" | custom-call | flops 5898240 | bytes 9000000 | tf_op jit(solution)/shard_map/modulate/pallas_call | solution.py:82
  19.5 0.8 pad_maximum_fusion
  20.9 1.5 collective-permute-start.5
  22.7 2.4 %collective-permute-start.4 = (bf16[192,3072]{1,0:T(8,128)(2,1)S(1)}, bf16[192,3072]{1,0:T(8,128)(2,1)}, u32[]{:S(2)}, u32[]{:S(2)}) collective-permute-start(bf16[192,3072]{1,0:T(8,128)(2,1)S(1)} %copy-done.2), channel_id=1, source_target_pairs={{0,6},{1,7},{2,0},{3,1},{4,2},{5,3},{6,4},{7,5},{8,14},{9,15},{10,... | collective-permute-start | bytes 3538952 | tf_op jit(solution)/shard_map/ppermute | solution.py:111
  25.1 1.0 copy-done.3
  26.3 1.0 copy-done.10
  27.3 1.0 fusion.11
  28.3 3.9 %collective-permute-start.6 = (f16[48,3072]{1,0:T(8,128)(2,1)}, f16[48,3072]{1,0:T(8,128)(2,1)}, u32[]{:S(2)}, u32[]{:S(2)}) collective-permute-start(f16[48,3072]{1,0:T(8,128)(2,1)} %get-tuple-element.111), channel_id=1, source_target_pairs={{0,8},{1,9},{2,10},{3,11},{4,12},{5,13},{6,14},{7,15}} | collective-permute-start | bytes 884744 | tf_op jit(solution)/shard_map/ppermute | solution.py:340
  32.2 3.0 %collective-permute-start.7 = (f16[48,3072]{1,0:T(8,128)(2,1)}, f16[48,3072]{1,0:T(8,128)(2,1)}, u32[]{:S(2)}, u32[]{:S(2)}) collective-permute-start(f16[48,3072]{1,0:T(8,128)(2,1)} %get-tuple-element.110), channel_id=1, source_target_pairs={{0,16},{1,17},{2,18},{3,19},{4,20},{5,21},{6,22},{7,23}} | collective-permute-start | bytes 884744 | tf_op jit(solution)/shard_map/ppermute | solution.py:340
  35.2 2.0 %collective-permute-start.8 = (f16[48,3072]{1,0:T(8,128)(2,1)}, f16[48,3072]{1,0:T(8,128)(2,1)}, u32[]{:S(2)}, u32[]{:S(2)}) collective-permute-start(f16[48,3072]{1,0:T(8,128)(2,1)} %get-tuple-element.109), channel_id=1, source_target_pairs={{0,24},{1,25},{2,26},{3,27},{4,28},{5,29},{6,30},{7,31}} | collective-permute-start | bytes 884744 | tf_op jit(solution)/shard_map/ppermute | solution.py:340
  37.2 3.1 %copy-done.1 = bf16[3,3072,384]{2,1,0:T(8,128)(2,1)S(1)} copy-done((bf16[3,3072,384]{2,1,0:T(8,128)(2,1)S(1)}, bf16[3,3072,384]{2,1,0:T(8,128)(2,1)}, u32[]{:S(2)}) %copy-start.1) | copy-done | bytes 7077912
  40.4 1.3 copy-done.4
  41.6 3.3 %qkv_tiles.3.refs_6_ = bf16[4,3,384,384]{3,2,1,0:T(8,128)(2,1)S(1)} custom-call(bf16[192,3072]{1,0:T(8,128)(2,1)S(1)} %copy-done.2, bf16[192,3072]{1,0:T(8,128)(2,1)S(1)} %copy-done.4, f32[2,128]{1,0:T(2,128)S(1)} %copy-done.7, bf16[3,3072,384]{2,1,0:T(8,128)(2,1)S(1)} %copy-done.1), custom_call_target="tpu_custom_call" | custom-call | flops 2717908992 | bytes 10000000 | tf_op jit(solution)/shard_map/qkv_tiles/pallas_call | solution.py:155
  44.9 6.4 %collective-permute-done.3.refs_2_ = bf16[192,3072]{1,0:T(8,128)(2,1)} collective-permute-done((bf16[192,3072]{1,0:T(8,128)(2,1)S(1)}, bf16[192,3072]{1,0:T(8,128)(2,1)}, u32[]{:S(2)}, u32[]{:S(2)}) %collective-permute-start.3) | collective-permute-done | bytes 1179680 | tf_op jit(solution)/shard_map/ppermute | solution.py:111
  51.3 1.1 collective-permute-start.10
  52.5 1.4 broadcast_select_fusion
  53.9 2.7 %collective-permute-start.9 = (bf16[192,3072]{1,0:T(8,128)(2,1)S(1)}, bf16[192,3072]{1,0:T(8,128)(2,1)S(1)}, u32[]{:S(2)}, u32[]{:S(2)}) collective-permute-start(bf16[192,3072]{1,0:T(8,128)(2,1)S(1)} %broadcast_select_fusion), channel_id=1, source_target_pairs={{0,2},{1,7},{2,4},{3,1},{4,6},{5,3},{6,0},{7,5},{8,10},{9,15},{10,... | collective-permute-start | bytes 3538952 | tf_op jit(solution)/shard_map/ppermute | solution.py:126
  56.6 1.8 fusion.9
  58.5 7.9 %qkv_tiles.4.refs_4_ = bf16[4,3,384,384]{3,2,1,0:T(8,128)(2,1)S(1)} custom-call(bf16[192,3072]{1,0:T(8,128)(2,1)} %collective-permute-done.4.refs_0_, bf16[192,3072]{1,0:T(8,128)(2,1)S(1)} %collective-permute-done.10.refs_1_, bf16[192,3072]{1,0:T(8,128)(2,1)} %collective-permute-done.3.refs_2_, ...), custom_call_target="tpu_custom_call", output_to_operand_aliasing={{}: (6, {})} | custom-call | flops 5435817984 | bytes 10000000 | tf_op jit(solution)/shard_map/qkv_tiles/pallas_call | solution.py:155
  66.4 3.3 %collective-permute-done.9.refs_0_ = bf16[192,3072]{1,0:T(8,128)(2,1)S(1)} collective-permute-done((bf16[192,3072]{1,0:T(8,128)(2,1)S(1)}, bf16[192,3072]{1,0:T(8,128)(2,1)S(1)}, u32[]{:S(2)}, u32[]{:S(2)}) %collective-permute-start.9) | collective-permute-done | bytes 1179680 | tf_op jit(solution)/shard_map/ppermute | solution.py:126
  69.8 2.3 %collective-permute-start.12 = (bf16[192,3072]{1,0:T(8,128)(2,1)S(1)}, bf16[192,3072]{1,0:T(8,128)(2,1)S(1)}, u32[]{:S(2)}, u32[]{:S(2)}) collective-permute-start(bf16[192,3072]{1,0:T(8,128)(2,1)S(1)} %collective-permute-done.9.refs_0_), channel_id=1, source_target_pairs={{0,1},{1,0},{2,3},{3,2},{4,5},{5,4},{6,7},{7,6},{8,9},{9,8},{10,11... | collective-permute-start | bytes 3538952 | tf_op jit(solution)/shard_map/ppermute | solution.py:115
  72.0 2.5 %collective-permute-done.12.refs_1_ = bf16[192,3072]{1,0:T(8,128)(2,1)S(1)} collective-permute-done((bf16[192,3072]{1,0:T(8,128)(2,1)S(1)}, bf16[192,3072]{1,0:T(8,128)(2,1)S(1)}, u32[]{:S(2)}, u32[]{:S(2)}) %collective-permute-start.12) | collective-permute-done | bytes 1179680 | tf_op jit(solution)/shard_map/ppermute | solution.py:115
  74.5 3.3 %qkv_tiles.5.held_ref = bf16[4,3,384,384]{3,2,1,0:T(8,128)(2,1)S(1)} custom-call(bf16[192,3072]{1,0:T(8,128)(2,1)S(1)} %collective-permute-done.9.refs_0_, bf16[192,3072]{1,0:T(8,128)(2,1)S(1)} %collective-permute-done.12.refs_1_, f32[2,128]{1,0:T(2,128)S(1)} %copy-done.7, bf16[3,3072,384]{2,1,0:T(8,128)(2,1)S(1)} %copy-done.1, ...), custom_call_target="tpu_custom_call", output_to_operand_aliasing={{}: (4, {})} | custom-call | flops 2717908992 | bytes 10000000 | tf_op jit(solution)/shard_map/qkv_tiles/pallas_call | solution.py:155
  77.8 3.2 %attend_tile.4 = bf16[384,384]{1,0:T(8,128)(2,1)S(1)} custom-call(s32[3,4,3]{2,1,0:T(4,128)S(1)} %copy-done.5, bf16[4,3,384,384]{3,2,1,0:T(8,128)(2,1)S(1)} %qkv_tiles.5.held_ref), custom_call_target="tpu_custom_call" | custom-call | flops 679477248 | bytes 4000000 | tf_op jit(solution)/shard_map/attend_tile/pallas_call | solution.py:193
  81.4 3.2 %attend_tile.6 = bf16[384,384]{1,0:T(8,128)(2,1)S(1)} custom-call(s32[3,4,3]{2,1,0:T(4,128)S(1)} %copy-done.5, bf16[4,3,384,384]{3,2,1,0:T(8,128)(2,1)S(1)} %qkv_tiles.5.held_ref), custom_call_target="tpu_custom_call" | custom-call | flops 679477248 | bytes 4000000 | tf_op jit(solution)/shard_map/attend_tile/pallas_call | solution.py:193
  84.6 3.2 %attend_tile.7 = bf16[384,384]{1,0:T(8,128)(2,1)S(1)} custom-call(s32[3,4,3]{2,1,0:T(4,128)S(1)} %copy-done.5, bf16[4,3,384,384]{3,2,1,0:T(8,128)(2,1)S(1)} %qkv_tiles.5.held_ref), custom_call_target="tpu_custom_call" | custom-call | flops 679477248 | bytes 4000000 | tf_op jit(solution)/shard_map/attend_tile/pallas_call | solution.py:193
  87.8 2.1 %collective-permute-start.14 = (bf16[384,384]{1,0:T(8,128)(2,1)S(1)}, bf16[384,384]{1,0:T(8,128)(2,1)S(1)}, u32[]{:S(2)}, u32[]{:S(2)}) collective-permute-start(bf16[384,384]{1,0:T(8,128)(2,1)S(1)} %attend_tile.6), channel_id=1, source_target_pairs={{0,2},{1,3},{2,4},{3,5},{4,6},{5,7},{6,0},{7,1},{8,10},{9,11},{10,... | collective-permute-start | bytes 884744 | tf_op jit(solution)/shard_map/ppermute | solution.py:111
  91.0 3.2 %attend_tile.5.a0 = bf16[384,384]{1,0:T(8,128)(2,1)S(1)} custom-call(s32[3,4,3]{2,1,0:T(4,128)S(1)} %copy-done.5, bf16[4,3,384,384]{3,2,1,0:T(8,128)(2,1)S(1)} %qkv_tiles.5.held_ref), custom_call_target="tpu_custom_call" | custom-call | flops 679477248 | bytes 4000000 | tf_op jit(solution)/shard_map/attend_tile/pallas_call | solution.py:193
  94.1 2.9 %collective-permute-done.14.a1 = bf16[384,384]{1,0:T(8,128)(2,1)S(1)} collective-permute-done((bf16[384,384]{1,0:T(8,128)(2,1)S(1)}, bf16[384,384]{1,0:T(8,128)(2,1)S(1)}, u32[]{:S(2)}, u32[]{:S(2)}) %collective-permute-start.14) | collective-permute-done | bytes 294944 | tf_op jit(solution)/shard_map/ppermute | solution.py:111
  97.7 6.2 %collective-permute-start.19 = (f16[48,3072]{1,0:T(8,128)(2,1)}, f16[48,3072]{1,0:T(8,128)(2,1)}, u32[]{:S(2)}, u32[]{:S(2)}) collective-permute-start(f16[48,3072]{1,0:T(8,128)(2,1)} %fusion.9), channel_id=1, source_target_pairs={{0,64},{8,72},{16,80},{24,88},{1,65},{9,73},{17,81},{25,89},{2,66}... | collective-permute-start | bytes 884744 | tf_op jit(solution)/shard_map/ppermute | solution.py:363
  104.1 0.7 collective-permute-start.16
  104.8 3.2 %collective-permute-start.17 = (bf16[4,2,48,384]{3,2,1,0:T(8,128)(2,1)S(1)}, bf16[4,2,48,384]{3,2,1,0:T(8,128)(2,1)S(1)}, u32[]{:S(2)}, u32[]{:S(2)}) collective-permute-start(bf16[4,2,48,384]{3,2,1,0:T(8,128)(2,1)S(1)} %get-tuple-element.78), channel_id=1, source_target_pairs={{0,16},{8,24},{16,0},{24,8},{32,48},{40,56},{48,32},{56,40},{64,80... | collective-permute-start | bytes 884744 | tf_op jit(solution)/shard_map/ppermute | solution.py:120
  108.6 3.5 %collective-permute-done.16.p1 = bf16[4,2,48,384]{3,2,1,0:T(8,128)(2,1)S(1)} collective-permute-done((bf16[4,2,48,384]{3,2,1,0:T(8,128)(2,1)S(1)}, bf16[4,2,48,384]{3,2,1,0:T(8,128)(2,1)S(1)}, u32[]{:S(2)}, u32[]{:S(2)}) %collective-permute-start.16) | collective-permute-done | bytes 294944 | tf_op jit(solution)/shard_map/ppermute | solution.py:120
  112.1 7.4 %collective-permute-done.17.p2 = bf16[4,2,48,384]{3,2,1,0:T(8,128)(2,1)S(1)} collective-permute-done((bf16[4,2,48,384]{3,2,1,0:T(8,128)(2,1)S(1)}, bf16[4,2,48,384]{3,2,1,0:T(8,128)(2,1)S(1)}, u32[]{:S(2)}, u32[]{:S(2)}) %collective-permute-start.17) | collective-permute-done | bytes 294944 | tf_op jit(solution)/shard_map/ppermute | solution.py:120
  120.1 1.3 collective-permute-start.20
  121.4 1.7 copy-done.6
  123.1 3.0 %copy-done.8 = bf16[48,96,768]{2,1,0:T(8,128)(2,1)S(1)} copy-done((bf16[48,96,768]{2,1,0:T(8,128)(2,1)S(1)}, bf16[48,96,768]{2,1,0:T(8,128)(2,1)}, u32[]{:S(2)}) %copy-start.8) | copy-done | bytes 7077912
  126.1 4.9 %out_project.1 = (bf16[4,4,48,768]{3,2,1,0:T(8,128)(2,1)S(1)}, bf16[4,4,48,768]{3,2,1,0:T(8,128)(2,1)}) custom-call(bf16[4,2,48,384]{3,2,1,0:T(8,128)(2,1)S(1)} %get-tuple-element.81.p0, bf16[4,2,48,384]{3,2,1,0:T(8,128)(2,1)S(1)} %collective-permute-done.16.p1, bf16[4,2,48,384]{3,2,1,0:T(8,128)(2,1)S(1)} %collective-permute-done.17.p2, ...), custom_call_target="tpu_custom_call" | custom-call | flops 3623878656 | bytes 12000000 | tf_op jit(solution)/shard_map/out_project/pallas_call | solution.py:248
  130.9 0.7 copy-done.14
  131.6 2.2 %collective-permute-start.21 = (bf16[4,4,48,768]{3,2,1,0:T(8,128)(2,1)}, bf16[4,4,48,768]{3,2,1,0:T(8,128)(2,1)}, u32[]{:S(2)}, u32[]{:S(2)}) collective-permute-start(bf16[4,4,48,768]{3,2,1,0:T(8,128)(2,1)} %get-tuple-element.92), channel_id=1, source_target_pairs={{0,1},{1,0},{2,3},{3,2},{4,5},{5,4},{6,7},{7,6},{8,9},{9,8},{10,11... | collective-permute-start | bytes 3538952 | tf_op jit(solution)/shard_map/ppermute | solution.py:115
  133.9 2.8 %collective-permute-done.21.other_ref = bf16[4,4,48,768]{3,2,1,0:T(8,128)(2,1)} collective-permute-done((bf16[4,4,48,768]{3,2,1,0:T(8,128)(2,1)}, bf16[4,4,48,768]{3,2,1,0:T(8,128)(2,1)}, u32[]{:S(2)}, u32[]{:S(2)}) %collective-permute-start.21) | collective-permute-done | bytes 1179680 | tf_op jit(solution)/shard_map/ppermute | solution.py:115
  136.7 1.6 row_prefix.3
  138.3 1.4 collective-permute-start.31
  139.7 3.5 %collective-permute-start.32 = (bf16[2,48,768]{2,1,0:T(8,128)(2,1)S(1)}, bf16[2,48,768]{2,1,0:T(8,128)(2,1)S(1)}, u32[]{:S(2)}, u32[]{:S(2)}) collective-permute-start(bf16[2,48,768]{2,1,0:T(8,128)(2,1)S(1)} %get-tuple-element.98), channel_id=1, source_target_pairs={{0,64},{8,72},{16,80},{24,88},{32,96},{40,104},{48,112},{56,120},{... | collective-permute-start | bytes 442376 | tf_op jit(solution)/shard_map/ppermute | solution.py:131
  143.2 1.3 collective-permute-start.33
  144.6 1.6 row_prefix.2
  146.1 1.3 collective-permute-start.22
  147.5 1.9 %collective-permute-start.28 = (f16[48,3072]{1,0:T(8,128)(2,1)S(1)}, f16[48,3072]{1,0:T(8,128)(2,1)S(1)}, u32[]{:S(2)}, u32[]{:S(2)}) collective-permute-start(f16[48,3072]{1,0:T(8,128)(2,1)S(1)} %get-tuple-element.100), channel_id=1, source_target_pairs={{0,24},{8,0},{16,8},{24,16},{32,56},{40,32},{48,40},{56,48},{64,88... | collective-permute-start | bytes 884744 | tf_op jit(solution)/shard_map/ppermute | solution.py:120
  149.5 0.9 collective-permute-start.29
  150.8 1.9 collective-permute-start.23
  152.7 2.6 %collective-permute-start.24 = (bf16[2,48,768]{2,1,0:T(8,128)(2,1)S(1)}, bf16[2,48,768]{2,1,0:T(8,128)(2,1)S(1)}, u32[]{:S(2)}, u32[]{:S(2)}) collective-permute-start(bf16[2,48,768]{2,1,0:T(8,128)(2,1)S(1)} %get-tuple-element.94), channel_id=1, source_target_pairs={{0,96},{8,104},{16,112},{24,120},{1,97},{9,105},{17,113},{25,121},... | collective-permute-start | bytes 442376 | tf_op jit(solution)/shard_map/ppermute | solution.py:131
  155.4 1.9 %collective-permute-start.34 = (bf16[2,48,768]{2,1,0:T(8,128)(2,1)S(1)}, bf16[2,48,768]{2,1,0:T(8,128)(2,1)S(1)}, u32[]{:S(2)}, u32[]{:S(2)}) collective-permute-start(bf16[2,48,768]{2,1,0:T(8,128)(2,1)S(1)} %get-tuple-element.103), channel_id=1, source_target_pairs={{0,24},{8,0},{16,8},{24,16},{32,56},{40,32},{48,40},{56,48},{64,88... | collective-permute-start | bytes 442376 | tf_op jit(solution)/shard_map/ppermute | solution.py:120
  157.3 3.6 %collective-permute-done.24 = bf16[2,48,768]{2,1,0:T(8,128)(2,1)S(1)} collective-permute-done((bf16[2,48,768]{2,1,0:T(8,128)(2,1)S(1)}, bf16[2,48,768]{2,1,0:T(8,128)(2,1)S(1)}, u32[]{:S(2)}, u32[]{:S(2)}) %collective-permute-start.24) | collective-permute-done | bytes 147488 | tf_op jit(solution)/shard_map/ppermute | solution.py:131
  160.9 2.3 %collective-permute-start.35 = (bf16[2,48,768]{2,1,0:T(8,128)(2,1)S(1)}, bf16[2,48,768]{2,1,0:T(8,128)(2,1)S(1)}, u32[]{:S(2)}, u32[]{:S(2)}) collective-permute-start(bf16[2,48,768]{2,1,0:T(8,128)(2,1)S(1)} %get-tuple-element.102), channel_id=1, source_target_pairs={{0,16},{8,24},{16,0},{24,8},{32,48},{40,56},{48,32},{56,40},{64,80... | collective-permute-start | bytes 442376 | tf_op jit(solution)/shard_map/ppermute | solution.py:120
  163.6 2.5 %collective-permute-start.25 = (bf16[2,48,768]{2,1,0:T(8,128)(2,1)S(1)}, bf16[2,48,768]{2,1,0:T(8,128)(2,1)S(1)}, u32[]{:S(2)}, u32[]{:S(2)}) collective-permute-start(bf16[2,48,768]{2,1,0:T(8,128)(2,1)S(1)} %get-tuple-element.107), channel_id=1, source_target_pairs={{0,24},{8,0},{16,8},{24,16},{32,56},{40,32},{48,40},{56,48},{64,88... | collective-permute-start | bytes 442376 | tf_op jit(solution)/shard_map/ppermute | solution.py:120
  166.1 1.2 collective-permute-done.30
  168.4 5.2 %collective-permute-done.36.refs_3_ = bf16[2,48,768]{2,1,0:T(8,128)(2,1)S(1)} collective-permute-done((bf16[2,48,768]{2,1,0:T(8,128)(2,1)S(1)}, bf16[2,48,768]{2,1,0:T(8,128)(2,1)S(1)}, u32[]{:S(2)}, u32[]{:S(2)}) %collective-permute-start.36) | collective-permute-done | bytes 147488 | tf_op jit(solution)/shard_map/ppermute | solution.py:120
  173.5 1.4 final_sum.2.refs_8_
  174.9 4.0 %collective-permute-done.27.refs_3_ = bf16[2,48,768]{2,1,0:T(8,128)(2,1)S(1)} collective-permute-done((bf16[2,48,768]{2,1,0:T(8,128)(2,1)S(1)}, bf16[2,48,768]{2,1,0:T(8,128)(2,1)S(1)}, u32[]{:S(2)}, u32[]{:S(2)}) %collective-permute-start.27) | collective-permute-done | bytes 147488 | tf_op jit(solution)/shard_map/ppermute | solution.py:120
  178.8 1.4 final_sum.3
  (73 shorter events, 7.2 us)
Async XLA Ops:
  6.5 91.2 %all-gather.3.cloned.1.call-start = ((), (), s32[]{:S(2)}) async-start(), calls=%async_computation | async-start | bytes 7520256 | tf_op jit(solution)/shard_map/all_gather | solution.py:332
  7.5 12.0 %collective-permute-start = (bf16[96,768]{1,0:T(8,128)(2,1)S(1)}, bf16[96,768]{1,0:T(8,128)(2,1)S(1)}, u32[]{:S(2)}, u32[]{:S(2)}) collective-permute-start(bf16[96,768]{1,0:T(8,128)(2,1)S(1)} %dynamic_slice.3), channel_id=1, source_target_pairs={{0,2},{1,3},{2,4},{3,5},{4,6},{5,7},{6,0},{7,1},{8,10},{9,11},{10,... | collective-permute-start | bytes 442376 | tf_op jit(solution)/shard_map/ppermute | solution.py:111
  9.6 9.9 %collective-permute-start.1 = (bf16[96,768]{1,0:T(8,128)(2,1)S(1)}, bf16[96,768]{1,0:T(8,128)(2,1)S(1)}, u32[]{:S(2)}, u32[]{:S(2)}) collective-permute-start(bf16[96,768]{1,0:T(8,128)(2,1)S(1)} %dynamic_slice.3), channel_id=1, source_target_pairs={{0,4},{1,5},{2,6},{3,7},{4,0},{5,1},{6,2},{7,3},{8,12},{9,13},{10,... | collective-permute-start | bytes 442376 | tf_op jit(solution)/shard_map/ppermute | solution.py:111
  12.0 7.5 %collective-permute-start.2 = (bf16[96,768]{1,0:T(8,128)(2,1)S(1)}, bf16[96,768]{1,0:T(8,128)(2,1)S(1)}, u32[]{:S(2)}, u32[]{:S(2)}) collective-permute-start(bf16[96,768]{1,0:T(8,128)(2,1)S(1)} %dynamic_slice.3), channel_id=1, source_target_pairs={{0,6},{1,7},{2,0},{3,1},{4,2},{5,3},{6,4},{7,5},{8,14},{9,15},{10,... | collective-permute-start | bytes 442376 | tf_op jit(solution)/shard_map/ppermute | solution.py:111
  13.7 12.4 %copy-start = (f32[1,192,3072]{2,1,0:T(8,128)S(1)}, f32[1,192,3072]{2,1,0:T(8,128)}, u32[]{:S(2)}) copy-start(f32[1,192,3072]{2,1,0:T(8,128)} %lat_hbm.1) | copy-start | bytes 7077892
  19.4 1.4 copy-start.2
  20.9 4.2 %collective-permute-start.5 = (bf16[192,3072]{1,0:T(8,128)(2,1)S(1)}, bf16[192,3072]{1,0:T(8,128)(2,1)S(1)}, u32[]{:S(2)}, u32[]{:S(2)}) collective-permute-start(bf16[192,3072]{1,0:T(8,128)(2,1)S(1)} %copy-done.2), channel_id=1, source_target_pairs={{0,1},{1,0},{2,3},{3,2},{4,5},{5,4},{6,7},{7,6},{8,9},{9,8},{10,11... | collective-permute-start | bytes 3538952 | tf_op jit(solution)/shard_map/ppermute | solution.py:115
  22.4 28.9 %collective-permute-start.3 = (bf16[192,3072]{1,0:T(8,128)(2,1)S(1)}, bf16[192,3072]{1,0:T(8,128)(2,1)}, u32[]{:S(2)}, u32[]{:S(2)}) collective-permute-start(bf16[192,3072]{1,0:T(8,128)(2,1)S(1)} %copy-done.2), channel_id=1, source_target_pairs={{0,2},{1,3},{2,4},{3,5},{4,6},{5,7},{6,0},{7,1},{8,10},{9,11},{10,... | collective-permute-start | bytes 3538952 | tf_op jit(solution)/shard_map/ppermute | solution.py:111
  22.7 28.6 %collective-permute-start.4 = (bf16[192,3072]{1,0:T(8,128)(2,1)S(1)}, bf16[192,3072]{1,0:T(8,128)(2,1)}, u32[]{:S(2)}, u32[]{:S(2)}) collective-permute-start(bf16[192,3072]{1,0:T(8,128)(2,1)S(1)} %copy-done.2), channel_id=1, source_target_pairs={{0,6},{1,7},{2,0},{3,1},{4,2},{5,3},{6,4},{7,5},{8,14},{9,15},{10,... | collective-permute-start | bytes 3538952 | tf_op jit(solution)/shard_map/ppermute | solution.py:111
  25.1 1.0 copy-start.3
  26.3 1.0 copy-start.10
  27.3 9.9 %copy-start.7 = (f32[2,128]{1,0:T(2,128)S(1)}, f32[2,128]{1,0:T(2,128)}, u32[]{:S(2)}) copy-start(f32[2,128]{1,0:T(2,128)} %refs_2_.3) | copy-start | bytes 3076
  28.3 23.0 %collective-permute-start.6 = (f16[48,3072]{1,0:T(8,128)(2,1)}, f16[48,3072]{1,0:T(8,128)(2,1)}, u32[]{:S(2)}, u32[]{:S(2)}) collective-permute-start(f16[48,3072]{1,0:T(8,128)(2,1)} %get-tuple-element.111), channel_id=1, source_target_pairs={{0,8},{1,9},{2,10},{3,11},{4,12},{5,13},{6,14},{7,15}} | collective-permute-start | bytes 884744 | tf_op jit(solution)/shard_map/ppermute | solution.py:340
  32.2 19.1 %collective-permute-start.7 = (f16[48,3072]{1,0:T(8,128)(2,1)}, f16[48,3072]{1,0:T(8,128)(2,1)}, u32[]{:S(2)}, u32[]{:S(2)}) collective-permute-start(f16[48,3072]{1,0:T(8,128)(2,1)} %get-tuple-element.110), channel_id=1, source_target_pairs={{0,16},{1,17},{2,18},{3,19},{4,20},{5,21},{6,22},{7,23}} | collective-permute-start | bytes 884744 | tf_op jit(solution)/shard_map/ppermute | solution.py:340
  35.2 16.1 %collective-permute-start.8 = (f16[48,3072]{1,0:T(8,128)(2,1)}, f16[48,3072]{1,0:T(8,128)(2,1)}, u32[]{:S(2)}, u32[]{:S(2)}) collective-permute-start(f16[48,3072]{1,0:T(8,128)(2,1)} %get-tuple-element.109), channel_id=1, source_target_pairs={{0,24},{1,25},{2,26},{3,27},{4,28},{5,29},{6,30},{7,31}} | collective-permute-start | bytes 884744 | tf_op jit(solution)/shard_map/ppermute | solution.py:340
  37.2 3.1 %copy-start.1 = (bf16[3,3072,384]{2,1,0:T(8,128)(2,1)S(1)}, bf16[3,3072,384]{2,1,0:T(8,128)(2,1)}, u32[]{:S(2)}) copy-start(bf16[3,3072,384]{2,1,0:T(8,128)(2,1)} %refs_3_.1) | copy-start | bytes 21233668
  40.3 1.3 copy-start.4
  51.3 7.1 %collective-permute-start.10 = (bf16[192,3072]{1,0:T(8,128)(2,1)}, bf16[192,3072]{1,0:T(8,128)(2,1)S(1)}, u32[]{:S(2)}, u32[]{:S(2)}) collective-permute-start(bf16[192,3072]{1,0:T(8,128)(2,1)} %collective-permute-done.4.refs_0_), channel_id=1, source_target_pairs={{0,1},{1,0},{2,3},{3,2},{4,5},{5,4},{6,7},{7,6},{8,9},{9,8},{10,11... | collective-permute-start | bytes 3538952 | tf_op jit(solution)/shard_map/ppermute | solution.py:115
  52.5 6.0 %collective-permute-start.11 = (bf16[192,3072]{1,0:T(8,128)(2,1)}, bf16[192,3072]{1,0:T(8,128)(2,1)S(1)}, u32[]{:S(2)}, u32[]{:S(2)}) collective-permute-start(bf16[192,3072]{1,0:T(8,128)(2,1)} %collective-permute-done.3.refs_2_), channel_id=1, source_target_pairs={{0,1},{1,0},{2,3},{3,2},{4,5},{5,4},{6,7},{7,6},{8,9},{9,8},{10,11... | collective-permute-start | bytes 3538952 | tf_op jit(solution)/shard_map/ppermute | solution.py:115
  53.9 15.9 %collective-permute-start.9 = (bf16[192,3072]{1,0:T(8,128)(2,1)S(1)}, bf16[192,3072]{1,0:T(8,128)(2,1)S(1)}, u32[]{:S(2)}, u32[]{:S(2)}) collective-permute-start(bf16[192,3072]{1,0:T(8,128)(2,1)S(1)} %broadcast_select_fusion), channel_id=1, source_target_pairs={{0,2},{1,7},{2,4},{3,1},{4,6},{5,3},{6,0},{7,5},{8,10},{9,15},{10,... | collective-permute-start | bytes 3538952 | tf_op jit(solution)/shard_map/ppermute | solution.py:126
  66.4 11.4 %copy-start.5 = (s32[3,4,3]{2,1,0:T(4,128)S(1)}, s32[3,4,3]{2,1,0:T(4,128)}, u32[]{:S(2)}) copy-start(s32[3,4,3]{2,1,0:T(4,128)} %list_ref.7) | copy-start | bytes 436
  69.8 4.7 %collective-permute-start.12 = (bf16[192,3072]{1,0:T(8,128)(2,1)S(1)}, bf16[192,3072]{1,0:T(8,128)(2,1)S(1)}, u32[]{:S(2)}, u32[]{:S(2)}) collective-permute-start(bf16[192,3072]{1,0:T(8,128)(2,1)S(1)} %collective-permute-done.9.refs_0_), channel_id=1, source_target_pairs={{0,1},{1,0},{2,3},{3,2},{4,5},{5,4},{6,7},{7,6},{8,9},{9,8},{10,11... | collective-permute-start | bytes 3538952 | tf_op jit(solution)/shard_map/ppermute | solution.py:115
  81.0 10.0 %collective-permute-start.13 = (bf16[384,384]{1,0:T(8,128)(2,1)S(1)}, bf16[384,384]{1,0:T(8,128)(2,1)S(1)}, u32[]{:S(2)}, u32[]{:S(2)}) collective-permute-start(bf16[384,384]{1,0:T(8,128)(2,1)S(1)} %attend_tile.4), channel_id=1, source_target_pairs={{0,4},{1,5},{2,6},{3,7},{4,0},{5,1},{6,2},{7,3},{8,12},{9,13},{10,... | collective-permute-start | bytes 884744 | tf_op jit(solution)/shard_map/ppermute | solution.py:111
  87.8 9.2 %collective-permute-start.14 = (bf16[384,384]{1,0:T(8,128)(2,1)S(1)}, bf16[384,384]{1,0:T(8,128)(2,1)S(1)}, u32[]{:S(2)}, u32[]{:S(2)}) collective-permute-start(bf16[384,384]{1,0:T(8,128)(2,1)S(1)} %attend_tile.6), channel_id=1, source_target_pairs={{0,2},{1,3},{2,4},{3,5},{4,6},{5,7},{6,0},{7,1},{8,10},{9,11},{10,... | collective-permute-start | bytes 884744 | tf_op jit(solution)/shard_map/ppermute | solution.py:111
  89.9 7.8 %collective-permute-start.15 = (bf16[384,384]{1,0:T(8,128)(2,1)S(1)}, bf16[384,384]{1,0:T(8,128)(2,1)S(1)}, u32[]{:S(2)}, u32[]{:S(2)}) collective-permute-start(bf16[384,384]{1,0:T(8,128)(2,1)S(1)} %attend_tile.7), channel_id=1, source_target_pairs={{0,6},{1,7},{2,0},{3,1},{4,2},{5,3},{6,4},{7,5},{8,14},{9,15},{10,... | collective-permute-start | bytes 884744 | tf_op jit(solution)/shard_map/ppermute | solution.py:111
  97.7 10.8 %collective-permute-start.19 = (f16[48,3072]{1,0:T(8,128)(2,1)}, f16[48,3072]{1,0:T(8,128)(2,1)}, u32[]{:S(2)}, u32[]{:S(2)}) collective-permute-start(f16[48,3072]{1,0:T(8,128)(2,1)} %fusion.9), channel_id=1, source_target_pairs={{0,64},{8,72},{16,80},{24,88},{1,65},{9,73},{17,81},{25,89},{2,66}... | collective-permute-start | bytes 884744 | tf_op jit(solution)/shard_map/ppermute | solution.py:363
  103.9 4.5 %copy-start.11 = (f16[48,3072]{1,0:T(8,128)(2,1)S(1)}, f16[48,3072]{1,0:T(8,128)(2,1)}, u32[]{:S(2)}) copy-start(f16[48,3072]{1,0:T(8,128)(2,1)} %fusion.9) | copy-start | bytes 884740
  103.9 17.4 %copy-start.9 = (f32[4,3072]{1,0:T(4,128)S(1)}, f32[4,3072]{1,0:T(4,128)}, u32[]{:S(2)}) copy-start(f32[4,3072]{1,0:T(4,128)} %get-tuple-element.87.gate_ref) | copy-start | bytes 147460
  104.1 8.0 %collective-permute-start.16 = (bf16[4,2,48,384]{3,2,1,0:T(8,128)(2,1)S(1)}, bf16[4,2,48,384]{3,2,1,0:T(8,128)(2,1)S(1)}, u32[]{:S(2)}, u32[]{:S(2)}) collective-permute-start(bf16[4,2,48,384]{3,2,1,0:T(8,128)(2,1)S(1)} %get-tuple-element.77), channel_id=1, source_target_pairs={{0,8},{8,16},{16,24},{24,0},{32,40},{40,48},{48,56},{56,32},{64,72... | collective-permute-start | bytes 884744 | tf_op jit(solution)/shard_map/ppermute | solution.py:120
  104.8 14.7 %collective-permute-start.17 = (bf16[4,2,48,384]{3,2,1,0:T(8,128)(2,1)S(1)}, bf16[4,2,48,384]{3,2,1,0:T(8,128)(2,1)S(1)}, u32[]{:S(2)}, u32[]{:S(2)}) collective-permute-start(bf16[4,2,48,384]{3,2,1,0:T(8,128)(2,1)S(1)} %get-tuple-element.78), channel_id=1, source_target_pairs={{0,16},{8,24},{16,0},{24,8},{32,48},{40,56},{48,32},{56,40},{64,80... | collective-permute-start | bytes 884744 | tf_op jit(solution)/shard_map/ppermute | solution.py:120
  108.0 12.0 %collective-permute-start.18 = (bf16[4,2,48,384]{3,2,1,0:T(8,128)(2,1)S(1)}, bf16[4,2,48,384]{3,2,1,0:T(8,128)(2,1)S(1)}, u32[]{:S(2)}, u32[]{:S(2)}) collective-permute-start(bf16[4,2,48,384]{3,2,1,0:T(8,128)(2,1)S(1)} %get-tuple-element.79), channel_id=1, source_target_pairs={{0,24},{8,0},{16,8},{24,16},{32,56},{40,32},{48,40},{56,48},{64,88... | collective-permute-start | bytes 884744 | tf_op jit(solution)/shard_map/ppermute | solution.py:120
  108.6 22.3 %copy-start.12 = (f16[48,3072]{1,0:T(8,128)(2,1)}, f16[48,3072]{1,0:T(8,128)(2,1)S(1)}, u32[]{:S(2)}) copy-start(f16[48,3072]{1,0:T(8,128)(2,1)S(1)} %broadcast_select_fusion.2) | copy-start | bytes 884740
  120.1 10.9 %collective-permute-start.20 = (f16[48,3072]{1,0:T(8,128)(2,1)S(1)}, f16[48,3072]{1,0:T(8,128)(2,1)S(1)}, u32[]{:S(2)}, u32[]{:S(2)}) collective-permute-start(f16[48,3072]{1,0:T(8,128)(2,1)S(1)} %broadcast_select_fusion.2), channel_id=1, source_target_pairs={{0,32},{64,96},{8,40},{72,104},{16,48},{80,112},{24,56},{88,120},{... | collective-permute-start | bytes 884744 | tf_op jit(solution)/shard_map/ppermute | solution.py:366
  121.4 1.7 copy-start.6
  123.1 3.0 %copy-start.8 = (bf16[48,96,768]{2,1,0:T(8,128)(2,1)S(1)}, bf16[48,96,768]{2,1,0:T(8,128)(2,1)}, u32[]{:S(2)}) copy-start(bf16[48,96,768]{2,1,0:T(8,128)(2,1)} %all-gather.3.cloned.1.call-done) | copy-start | bytes 21233668
  130.9 0.7 copy-start.14
  131.6 5.1 %collective-permute-start.21 = (bf16[4,4,48,768]{3,2,1,0:T(8,128)(2,1)}, bf16[4,4,48,768]{3,2,1,0:T(8,128)(2,1)}, u32[]{:S(2)}, u32[]{:S(2)}) collective-permute-start(bf16[4,4,48,768]{3,2,1,0:T(8,128)(2,1)} %get-tuple-element.92), channel_id=1, source_target_pairs={{0,1},{1,0},{2,3},{3,2},{4,5},{5,4},{6,7},{7,6},{8,9},{9,8},{10,11... | collective-permute-start | bytes 3538952 | tf_op jit(solution)/shard_map/ppermute | solution.py:115
  138.3 9.2 %copy-start.13 = (f16[48,3072]{1,0:T(8,128)(2,1)S(1)}, f16[48,3072]{1,0:T(8,128)(2,1)}, u32[]{:S(2)}) copy-start(f16[48,3072]{1,0:T(8,128)(2,1)} %copy-done.12) | copy-start | bytes 884740
  138.3 9.2 %copy-start.15 = (f16[48,3072]{1,0:T(8,128)(2,1)S(1)}, f16[48,3072]{1,0:T(8,128)(2,1)}, u32[]{:S(2)}) copy-start(f16[48,3072]{1,0:T(8,128)(2,1)} %copy-done.14) | copy-start | bytes 884740
  138.3 11.2 %collective-permute-start.31 = (bf16[2,48,768]{2,1,0:T(8,128)(2,1)S(1)}, bf16[2,48,768]{2,1,0:T(8,128)(2,1)S(1)}, u32[]{:S(2)}, u32[]{:S(2)}) collective-permute-start(bf16[2,48,768]{2,1,0:T(8,128)(2,1)S(1)} %get-tuple-element.98), channel_id=1, source_target_pairs={{0,32},{8,40},{16,48},{24,56},{32,64},{40,72},{48,80},{56,88},{64,... | collective-permute-start | bytes 442376 | tf_op jit(solution)/shard_map/ppermute | solution.py:131
  139.7 10.6 %collective-permute-start.32 = (bf16[2,48,768]{2,1,0:T(8,128)(2,1)S(1)}, bf16[2,48,768]{2,1,0:T(8,128)(2,1)S(1)}, u32[]{:S(2)}, u32[]{:S(2)}) collective-permute-start(bf16[2,48,768]{2,1,0:T(8,128)(2,1)S(1)} %get-tuple-element.98), channel_id=1, source_target_pairs={{0,64},{8,72},{16,80},{24,88},{32,96},{40,104},{48,112},{56,120},{... | collective-permute-start | bytes 442376 | tf_op jit(solution)/shard_map/ppermute | solution.py:131
  143.2 7.5 %collective-permute-start.33 = (bf16[2,48,768]{2,1,0:T(8,128)(2,1)S(1)}, bf16[2,48,768]{2,1,0:T(8,128)(2,1)S(1)}, u32[]{:S(2)}, u32[]{:S(2)}) collective-permute-start(bf16[2,48,768]{2,1,0:T(8,128)(2,1)S(1)} %get-tuple-element.98), channel_id=1, source_target_pairs={{0,96},{8,104},{16,112},{24,120},{1,97},{9,105},{17,113},{25,121},... | collective-permute-start | bytes 442376 | tf_op jit(solution)/shard_map/ppermute | solution.py:131
  146.1 6.5 %collective-permute-start.22 = (bf16[2,48,768]{2,1,0:T(8,128)(2,1)S(1)}, bf16[2,48,768]{2,1,0:T(8,128)(2,1)S(1)}, u32[]{:S(2)}, u32[]{:S(2)}) collective-permute-start(bf16[2,48,768]{2,1,0:T(8,128)(2,1)S(1)} %get-tuple-element.94), channel_id=1, source_target_pairs={{0,32},{8,40},{16,48},{24,56},{32,64},{40,72},{48,80},{56,88},{64,... | collective-permute-start | bytes 442376 | tf_op jit(solution)/shard_map/ppermute | solution.py:131
  147.5 15.8 %collective-permute-start.28 = (f16[48,3072]{1,0:T(8,128)(2,1)S(1)}, f16[48,3072]{1,0:T(8,128)(2,1)S(1)}, u32[]{:S(2)}, u32[]{:S(2)}) collective-permute-start(f16[48,3072]{1,0:T(8,128)(2,1)S(1)} %get-tuple-element.100), channel_id=1, source_target_pairs={{0,24},{8,0},{16,8},{24,16},{32,56},{40,32},{48,40},{56,48},{64,88... | collective-permute-start | bytes 884744 | tf_op jit(solution)/shard_map/ppermute | solution.py:120
  149.5 14.1 %collective-permute-start.29 = (f16[48,3072]{1,0:T(8,128)(2,1)S(1)}, f16[48,3072]{1,0:T(8,128)(2,1)S(1)}, u32[]{:S(2)}, u32[]{:S(2)}) collective-permute-start(f16[48,3072]{1,0:T(8,128)(2,1)S(1)} %get-tuple-element.100), channel_id=1, source_target_pairs={{0,16},{8,24},{16,0},{24,8},{32,48},{40,56},{48,32},{56,40},{64,80... | collective-permute-start | bytes 884744 | tf_op jit(solution)/shard_map/ppermute | solution.py:120
  150.4 16.9 %collective-permute-start.30 = (f16[48,3072]{1,0:T(8,128)(2,1)S(1)}, f16[48,3072]{1,0:T(8,128)(2,1)S(1)}, u32[]{:S(2)}, u32[]{:S(2)}) collective-permute-start(f16[48,3072]{1,0:T(8,128)(2,1)S(1)} %get-tuple-element.100), channel_id=1, source_target_pairs={{0,8},{8,16},{16,24},{24,0},{32,40},{40,48},{48,56},{56,32},{64,72... | collective-permute-start | bytes 884744 | tf_op jit(solution)/shard_map/ppermute | solution.py:120
  150.8 4.6 %collective-permute-start.23 = (bf16[2,48,768]{2,1,0:T(8,128)(2,1)S(1)}, bf16[2,48,768]{2,1,0:T(8,128)(2,1)S(1)}, u32[]{:S(2)}, u32[]{:S(2)}) collective-permute-start(bf16[2,48,768]{2,1,0:T(8,128)(2,1)S(1)} %get-tuple-element.94), channel_id=1, source_target_pairs={{0,64},{8,72},{16,80},{24,88},{32,96},{40,104},{48,112},{56,120},{... | collective-permute-start | bytes 442376 | tf_op jit(solution)/shard_map/ppermute | solution.py:131
  152.7 8.3 %collective-permute-start.24 = (bf16[2,48,768]{2,1,0:T(8,128)(2,1)S(1)}, bf16[2,48,768]{2,1,0:T(8,128)(2,1)S(1)}, u32[]{:S(2)}, u32[]{:S(2)}) collective-permute-start(bf16[2,48,768]{2,1,0:T(8,128)(2,1)S(1)} %get-tuple-element.94), channel_id=1, source_target_pairs={{0,96},{8,104},{16,112},{24,120},{1,97},{9,105},{17,113},{25,121},... | collective-permute-start | bytes 442376 | tf_op jit(solution)/shard_map/ppermute | solution.py:131
  155.4 11.9 %collective-permute-start.34 = (bf16[2,48,768]{2,1,0:T(8,128)(2,1)S(1)}, bf16[2,48,768]{2,1,0:T(8,128)(2,1)S(1)}, u32[]{:S(2)}, u32[]{:S(2)}) collective-permute-start(bf16[2,48,768]{2,1,0:T(8,128)(2,1)S(1)} %get-tuple-element.103), channel_id=1, source_target_pairs={{0,24},{8,0},{16,8},{24,16},{32,56},{40,32},{48,40},{56,48},{64,88... | collective-permute-start | bytes 442376 | tf_op jit(solution)/shard_map/ppermute | solution.py:120
  160.9 7.4 %collective-permute-start.35 = (bf16[2,48,768]{2,1,0:T(8,128)(2,1)S(1)}, bf16[2,48,768]{2,1,0:T(8,128)(2,1)S(1)}, u32[]{:S(2)}, u32[]{:S(2)}) collective-permute-start(bf16[2,48,768]{2,1,0:T(8,128)(2,1)S(1)} %get-tuple-element.102), channel_id=1, source_target_pairs={{0,16},{8,24},{16,0},{24,8},{32,48},{40,56},{48,32},{56,40},{64,80... | collective-permute-start | bytes 442376 | tf_op jit(solution)/shard_map/ppermute | solution.py:120
  163.3 10.2 %collective-permute-start.36 = (bf16[2,48,768]{2,1,0:T(8,128)(2,1)S(1)}, bf16[2,48,768]{2,1,0:T(8,128)(2,1)S(1)}, u32[]{:S(2)}, u32[]{:S(2)}) collective-permute-start(bf16[2,48,768]{2,1,0:T(8,128)(2,1)S(1)} %get-tuple-element.101), channel_id=1, source_target_pairs={{0,8},{8,16},{16,24},{24,0},{32,40},{40,48},{48,56},{56,32},{64,72... | collective-permute-start | bytes 442376 | tf_op jit(solution)/shard_map/ppermute | solution.py:120
  163.6 11.3 %collective-permute-start.25 = (bf16[2,48,768]{2,1,0:T(8,128)(2,1)S(1)}, bf16[2,48,768]{2,1,0:T(8,128)(2,1)S(1)}, u32[]{:S(2)}, u32[]{:S(2)}) collective-permute-start(bf16[2,48,768]{2,1,0:T(8,128)(2,1)S(1)} %get-tuple-element.107), channel_id=1, source_target_pairs={{0,24},{8,0},{16,8},{24,16},{32,56},{40,32},{48,40},{56,48},{64,88... | collective-permute-start | bytes 442376 | tf_op jit(solution)/shard_map/ppermute | solution.py:120
  167.3 7.6 %collective-permute-start.26 = (bf16[2,48,768]{2,1,0:T(8,128)(2,1)S(1)}, bf16[2,48,768]{2,1,0:T(8,128)(2,1)S(1)}, u32[]{:S(2)}, u32[]{:S(2)}) collective-permute-start(bf16[2,48,768]{2,1,0:T(8,128)(2,1)S(1)} %get-tuple-element.106), channel_id=1, source_target_pairs={{0,16},{8,24},{16,0},{24,8},{32,48},{40,56},{48,32},{56,40},{64,80... | collective-permute-start | bytes 442376 | tf_op jit(solution)/shard_map/ppermute | solution.py:120
  167.3 11.5 %collective-permute-start.27 = (bf16[2,48,768]{2,1,0:T(8,128)(2,1)S(1)}, bf16[2,48,768]{2,1,0:T(8,128)(2,1)S(1)}, u32[]{:S(2)}, u32[]{:S(2)}) collective-permute-start(bf16[2,48,768]{2,1,0:T(8,128)(2,1)S(1)} %get-tuple-element.105), channel_id=1, source_target_pairs={{0,8},{8,16},{16,24},{24,0},{32,40},{40,48},{48,56},{56,32},{64,72... | collective-permute-start | bytes 442376 | tf_op jit(solution)/shard_map/ppermute | solution.py:120
Sparse Core Ops, SparseCore 0:
  20.5 67.4 all-gather.2
